TPU v7x, 32 devices: a whole 2x2x4 slice. The times are simulated.
32 devices in a mesh: pipe: 4 (over z), dp: 8 (over y, x, core).
Axes of the slice: x: 2, y: 2, z: 4, core: 2. Of those that a mesh axis runs over, the one named last changes fastest.
Arguments:
- tokens: bfloat16 [4096, 768], P('dp'), may hold values from -6 to 6
- gain_one: float32 [8, 768], P('pipe'), may hold values from 0.25 to 1.75
- qkv_weight: bfloat16 [8, 768, 2304], P('pipe'), may hold values from -0.21875 to 0.21875
- out_weight: bfloat16 [8, 768, 768], P('pipe'), may hold values from -1.25 to 1.25
- gain_two: float32 [8, 768], P('pipe'), may hold values from 0.25 to 1.75
- up_weight: bfloat16 [8, 768, 3072], P('pipe'), may hold values from -0.21875 to 0.21875
- down_weight: bfloat16 [8, 3072, 768], P('pipe'), may hold values from -0.109375 to 0.109375
- cotangent: bfloat16 [4096, 768], P('dp'), may hold values from -6 to 6
- flags: int32 [4096], P('dp'), may hold values from 0 to 1, as said below
- groups: int32 [32], P('dp'), may hold values from 0 to 1, as said below
Outputs:
- final_acts: bfloat16 [4096, 768], P('dp', 'pipe')
- input_grad: float32 [4096, 768], P('dp', 'pipe')
- grad_gain_one: float32 [8, 768], P('pipe', 'dp')
- grad_qkv: float32 [8, 768, 2304], P('pipe', 'dp')
- grad_out: float32 [8, 768, 768], P('pipe', 'dp')
- grad_gain_two: float32 [8, 768], P('pipe', 'dp')
- grad_up: float32 [8, 768, 3072], P('pipe', 'dp')
- grad_down: float32 [8, 3072, 768], P('pipe', 'dp')
Inputs may be any that keep to these rules, and one draw needn't show every extreme that they name: `groups`: 0: the micro-batch is one image of 128 slots; 1: it holds four images of 32 slots each. `flags`: the valid slots of each image form a prefix of it covering at least half of its slots.
All inputs are finite; a program needn't handle non-finite values.
Results may differ from a plain program's by a relative error of at most 0.024.
Values may be sent and summed in bfloat16 or wider, within the bound.
A program may use at most 320 MiB of HBM per device.

v0:
```python
import jax
import jax.numpy as jnp
from jax import lax
from jax.sharding import PartitionSpec as P

D = 768
HEADS = 16
HEAD_DIM = 48
FF = 3072
SEQ = 128
MB = 4


EPS = 1e-06


def shifted(array, axis, by):
    devices = lax.axis_size(axis)
    pairs = [(i, i + by) for i in range(devices) if 0 <= i + by < devices]
    return lax.ppermute(array, axis, pairs)


def norm(x, g):
    centre = x - jnp.mean(x, axis=-1, keepdims=True)
    spread = jnp.mean(centre * centre, axis=-1, keepdims=True)
    return centre * lax.rsqrt(spread + EPS) * g


def gelu_exact(v):
    return jax.nn.gelu(v, approximate=False)


def make_mask(flags, groups, slot):
    valid = lax.dynamic_slice_in_dim(flags, slot * SEQ, SEQ)
    group = lax.dynamic_index_in_dim(groups, slot, keepdims=False)
    position = jnp.arange(SEQ)
    image = jnp.where(group == 1, position // (SEQ // 4), 0)
    return (image[:, None] == image[None, :]) & (valid[None, :] == 1)


def split_heads(qkvb):
    query = qkvb[:, :D].reshape(SEQ, HEADS, HEAD_DIM)
    keys = qkvb[:, D : 2 * D].reshape(SEQ, HEADS, HEAD_DIM)
    values = qkvb[:, 2 * D :].reshape(SEQ, HEADS, HEAD_DIM)
    return (query, keys, values)


def raw_scores(query, keys, mask):
    scores = jnp.einsum(
        "qhd,khd->hqk", query, keys, preferred_element_type=jnp.float32
    ) * HEAD_DIM ** (-0.5)
    return jnp.where(mask[None], scores, -1e30)


def pick(weights, index):
    return tuple((w[index] for w in weights))


def layer_zeros(lead):
    return (
        jnp.zeros(lead + (SEQ, D), jnp.float32),
        jnp.zeros(lead + (SEQ, D), jnp.bfloat16),
        jnp.zeros(lead + (SEQ, 3 * D), jnp.bfloat16),
        jnp.zeros(lead + (HEADS, SEQ, 1), jnp.float32),
        jnp.zeros(lead + (SEQ, D), jnp.bfloat16),
        jnp.zeros(lead + (SEQ, D), jnp.float32),
        jnp.zeros(lead + (SEQ, D), jnp.bfloat16),
        jnp.zeros(lead + (SEQ, FF), jnp.float32),
        jnp.zeros(lead + (SEQ, FF), jnp.bfloat16),
    )


def section_zeros(entry):
    return (jnp.zeros((SEQ, D), jnp.bfloat16), (layer_zeros(()), layer_zeros(())))


def one_layer_zeros():
    return (
        jnp.zeros((D,), jnp.float32),
        jnp.zeros((D, 3 * D), jnp.float32),
        jnp.zeros((D, D), jnp.float32),
        jnp.zeros((D,), jnp.float32),
        jnp.zeros((D, FF), jnp.float32),
        jnp.zeros((FF, D), jnp.float32),
    )


def grad_zeros(grad_arg):
    return (jnp.zeros((SEQ, D), jnp.float32), one_layer_zeros(), one_layer_zeros())


def layer_forward(x, weights, mask):
    g1, wqkv, wo, g2, w1, w2 = weights
    u = norm(x, g1).astype(jnp.bfloat16)
    qkvb = jnp.dot(u, wqkv, preferred_element_type=jnp.float32).astype(jnp.bfloat16)
    query, keys, values = split_heads(qkvb)
    scores = raw_scores(query, keys, mask)
    peak = jnp.max(scores, axis=-1, keepdims=True)
    expo = jnp.exp(scores - peak)
    total = jnp.sum(expo, axis=-1, keepdims=True)
    probs = (expo / total).astype(jnp.bfloat16)
    logsum = peak + jnp.log(total)
    mixed = jnp.einsum("hqk,khd->qhd", probs, values, preferred_element_type=jnp.float32)
    mixed = mixed.reshape(SEQ, D).astype(jnp.bfloat16)
    h = x + jnp.dot(mixed, wo, preferred_element_type=jnp.float32)
    u_two = norm(h, g2).astype(jnp.bfloat16)
    inner = jnp.dot(u_two, w1, preferred_element_type=jnp.float32)
    active = gelu_exact(inner).astype(jnp.bfloat16)
    result = h + jnp.dot(active, w2, preferred_element_type=jnp.float32)
    return (result, (x, u, qkvb, logsum, mixed, h, u_two, inner, active))


def layer_backward(saved, grad_out, weights, mask):
    g1, wqkv, wo, g2, w1, w2 = weights
    x, u, qkvb, logsum, mixed, h, u_two, inner, active = saved
    grad_low = grad_out.astype(jnp.bfloat16)
    g_down = jnp.einsum("sf,sd->fd", active, grad_low, preferred_element_type=jnp.float32)
    grad_act = jnp.einsum("sd,fd->sf", grad_low, w2, preferred_element_type=jnp.float32)
    _, gelu_back = jax.vjp(gelu_exact, inner)
    grad_inner = gelu_back(grad_act)[0].astype(jnp.bfloat16)
    g_up = jnp.einsum("sd,sf->df", u_two, grad_inner, preferred_element_type=jnp.float32)
    grad_u_two = jnp.einsum("sf,df->sd", grad_inner, w1, preferred_element_type=jnp.float32)
    _, norm_back_two = jax.vjp(norm, h, g2)
    grad_h_norm, g_gain_two = norm_back_two(grad_u_two)
    grad_h = grad_out + grad_h_norm
    grad_attn = grad_h.astype(jnp.bfloat16)
    g_out = jnp.einsum("se,sd->ed", mixed, grad_attn, preferred_element_type=jnp.float32)
    grad_mixed = jnp.einsum("sd,ed->se", grad_attn, wo, preferred_element_type=jnp.float32)
    grad_mixed = grad_mixed.astype(jnp.bfloat16).reshape(SEQ, HEADS, HEAD_DIM)
    query, keys, values = split_heads(qkvb)
    scores = raw_scores(query, keys, mask)
    probs_full = jnp.exp(scores - logsum)
    probs = probs_full.astype(jnp.bfloat16)
    grad_probs = jnp.einsum("qhd,khd->hqk", grad_mixed, values, preferred_element_type=jnp.float32)
    grad_values = jnp.einsum("hqk,qhd->khd", probs, grad_mixed, preferred_element_type=jnp.float32)
    inner_sum = jnp.sum(probs_full * grad_probs, axis=-1, keepdims=True)
    grad_scores = (probs_full * (grad_probs - inner_sum)).astype(jnp.bfloat16)
    grad_query = jnp.einsum(
        "hqk,khd->qhd", grad_scores, keys, preferred_element_type=jnp.float32
    ) * HEAD_DIM ** (-0.5)
    grad_keys = jnp.einsum(
        "hqk,qhd->khd", grad_scores, query, preferred_element_type=jnp.float32
    ) * HEAD_DIM ** (-0.5)
    grad_qkv = jnp.concatenate(
        [grad_query.reshape(SEQ, D), grad_keys.reshape(SEQ, D), grad_values.reshape(SEQ, D)], axis=1
    ).astype(jnp.bfloat16)
    g_qkv = jnp.einsum("sd,se->de", u, grad_qkv, preferred_element_type=jnp.float32)
    grad_u = jnp.einsum("se,de->sd", grad_qkv, wqkv, preferred_element_type=jnp.float32)
    _, norm_back_one = jax.vjp(norm, x, g1)
    grad_x_norm, g_gain_one = norm_back_one(grad_u)
    return (grad_h + grad_x_norm, (g_gain_one, g_qkv, g_out, g_gain_two, g_up, g_down))


def section_forward(entry, weights, mask):
    x = entry.astype(jnp.float32)
    x, saved_first = layer_forward(x, pick(weights, 0), mask)
    x, saved_second = layer_forward(x, pick(weights, 1), mask)
    return (x.astype(jnp.bfloat16), (saved_first, saved_second))


def place(buffer, slot, value, flag):
    current = lax.dynamic_index_in_dim(buffer, slot, 0, keepdims=False)
    return lax.dynamic_update_index_in_dim(buffer, jnp.where(flag, value, current), slot, 0)


def body(
    tokens,
    gain_one,
    qkv_weight,
    out_weight,
    gain_two,
    up_weight,
    down_weight,
    cotangent,
    flags,
    groups,
):
    weights = (gain_one, qkv_weight, out_weight, gain_two, up_weight, down_weight)
    sections = lax.axis_size("pipe")
    section = lax.axis_index("pipe")
    replicas = lax.axis_size("dp")
    ticks = MB + sections - 1
    first_input = tokens.reshape(MB, SEQ, D)
    grads_in = cotangent.reshape(MB, SEQ, D)
    kept_start = None

    def forward_tick(tick, carry):
        received, inputs, finals, kept = carry
        micro = tick - section
        active = (micro >= 0) & (micro < MB)
        slot = jnp.clip(micro, 0, MB - 1)
        mask = make_mask(flags, groups, slot)
        entry = jnp.where(section == 0, first_input[slot], received)
        result, saved = lax.cond(
            active, lambda arg: section_forward(arg, weights, mask), section_zeros, entry
        )
        inputs = place(inputs, slot, entry, active)
        finals = place(finals, slot, result, active)
        received = shifted(result, "pipe", 1)
        return (received, inputs, finals, kept)

    start = (
        jnp.zeros((SEQ, D), jnp.bfloat16),
        jnp.zeros((MB, SEQ, D), jnp.bfloat16),
        jnp.zeros((MB, SEQ, D), jnp.bfloat16),
        kept_start,
    )
    _, inputs, finals, kept = lax.fori_loop(0, ticks, forward_tick, start)
    sent_start = tuple(
        (jnp.zeros((w.shape[1] // replicas,) + w.shape[2:], jnp.float32) for w in weights)
    )

    def backward_tick(tick, carry):
        received, acc_first, acc_second, sent, igrads = carry
        turn = tick - (sections - 1 - section)
        micro = MB - 1 - turn
        active = (turn >= 0) & (turn < MB)
        slot = jnp.clip(micro, 0, MB - 1)
        mask = make_mask(flags, groups, slot)
        grad_out = jnp.where(
            section == sections - 1,
            grads_in[slot].astype(jnp.float32),
            received.astype(jnp.float32),
        )

        def work(grad_arg):
            saved = section_forward(inputs[slot], weights, mask)[1]
            grad_mid, grads_second = layer_backward(saved[1], grad_arg, pick(weights, 1), mask)
            grad_low, grads_first = layer_backward(saved[0], grad_mid, pick(weights, 0), mask)
            return (grad_low, grads_first, grads_second)

        grad_in, grads_first, grads_second = lax.cond(active, work, grad_zeros, grad_out)
        acc_first = tuple((total + term for total, term in zip(acc_first, grads_first)))
        acc_second = tuple((total + term for total, term in zip(acc_second, grads_second)))
        igrads = place(igrads, slot, grad_in, active)
        received = shifted(grad_in.astype(jnp.bfloat16), "pipe", -1)
        return (received, acc_first, acc_second, sent, igrads)

    back_start = (
        jnp.zeros((SEQ, D), jnp.bfloat16),
        one_layer_zeros(),
        one_layer_zeros(),
        sent_start,
        jnp.zeros((MB, SEQ, D), jnp.float32),
    )
    _, acc_first, acc_second, sent, igrads = lax.fori_loop(0, ticks, backward_tick, back_start)
    stacked = tuple((jnp.stack([first, second]) for first, second in zip(acc_first, acc_second)))
    sums = (
        lax.psum_scatter(
            stacked[0].astype(jnp.bfloat16), "dp", scatter_dimension=1, tiled=True
        ).astype(jnp.float32),
        lax.psum_scatter(
            stacked[1].astype(jnp.bfloat16), "dp", scatter_dimension=1, tiled=True
        ).astype(jnp.float32),
        lax.psum_scatter(
            stacked[2].astype(jnp.bfloat16), "dp", scatter_dimension=1, tiled=True
        ).astype(jnp.float32),
        lax.psum_scatter(
            stacked[3].astype(jnp.bfloat16), "dp", scatter_dimension=1, tiled=True
        ).astype(jnp.float32),
        lax.psum_scatter(
            stacked[4].astype(jnp.bfloat16), "dp", scatter_dimension=1, tiled=True
        ).astype(jnp.float32),
        lax.psum_scatter(
            stacked[5].astype(jnp.bfloat16), "dp", scatter_dimension=1, tiled=True
        ).astype(jnp.float32),
    )
    final_term = jnp.where(
        section == sections - 1, finals.reshape(MB * SEQ, D).astype(jnp.float32), 0.0
    )
    input_term = jnp.where(section == 0, igrads.reshape(MB * SEQ, D), 0.0)
    final_part, input_part = (
        lax.psum_scatter(
            final_term.astype(jnp.bfloat16), "pipe", scatter_dimension=1, tiled=True
        ).astype(jnp.float32),
        lax.psum_scatter(
            input_term.astype(jnp.bfloat16), "pipe", scatter_dimension=1, tiled=True
        ).astype(jnp.float32),
    )
    return (
        final_part.astype(jnp.bfloat16),
        input_part,
        sums[0],
        sums[1],
        sums[2],
        sums[3],
        sums[4],
        sums[5],
    )


def solution(mesh):
    return jax.shard_map(
        body,
        mesh=mesh,
        in_specs=(
            P("dp", None),
            P("pipe", None),
            P("pipe", None, None),
            P("pipe", None, None),
            P("pipe", None),
            P("pipe", None, None),
            P("pipe", None, None),
            P("dp", None),
            P("dp"),
            P("dp"),
        ),
        out_specs=(
            P("dp", "pipe"),
            P("dp", "pipe"),
            P("pipe", "dp"),
            P("pipe", "dp", None),
            P("pipe", "dp", None),
            P("pipe", "dp"),
            P("pipe", "dp", None),
            P("pipe", "dp", None),
        ),
        check_vma=False,
    )
```

profile of v0, /device:TPU:0, one launch (start us, length us, event | category | flops | bytes accessed | tf_op | source)
XLA Modules:
  0.0 1849.0 jit_solution(14845201158132526198)
XLA Ops:
  9.3 281.1 %while.61 = (s32[]{:T(128)}, bf16[128,768]{1,0:T(8,128)(2,1)S(1)}, bf16[4,128,768]{2,1,0:T(8,128)(2,1)}, bf16[4,128,768]{2,1,0:T(8,128)(2,1)}, s32[]{:T(128)}, /...) while((s32[]{:T(128)}, bf16[128,768]{1,0:T(8,128)(2,1)S(1)}, ...), condition=%wide.region_15.16_spmd, body=%wide.region_0.15_spmd.sunk | while | flops 3835862272 | bytes 59632388 | solution.py:208
  11.9 35.3 %conditional.5 = (bf16[128,768]{1,0:T(8,128)(2,1)S(1)}) conditional(s32[]{:T(128)} %convert_element_type.557, () %tuple.264, (bf16[128,768]{1,0:T(8,128)(2,1)S(1)}, f32[2,768]{1,0:T(2,128)}, bf16[2,768,2304]{2,1,0:T(8,128)(2,1)}, s32[4]{0:T(128)}, s32[]{:T(128)}, /*index=5*/s32[128,1]{0,1:T(1,128)S(1)}, s32[1,128]{1,0:T(1,128)S(1)}, s32[512]{0:T(512)}, ...), branch_computations={%region_1.1_spmd, %region_2.14_spmd} | conditional | flops 3835567360 | bytes 56483720 | solution.py:194
  56.1 35.3 %conditional.5 = (bf16[128,768]{1,0:T(8,128)(2,1)S(1)}) conditional(s32[]{:T(128)} %convert_element_type.557, () %tuple.264, (bf16[128,768]{1,0:T(8,128)(2,1)S(1)}, f32[2,768]{1,0:T(2,128)}, bf16[2,768,2304]{2,1,0:T(8,128)(2,1)}, s32[4]{0:T(128)}, s32[]{:T(128)}, /*index=5*/s32[128,1]{0,1:T(1,128)S(1)}, s32[1,128]{1,0:T(1,128)S(1)}, s32[512]{0:T(512)}, ...), branch_computations={%region_1.1_spmd, %region_2.14_spmd} | conditional | flops 3835567360 | bytes 56483720 | solution.py:194
  102.6 35.3 %conditional.5 = (bf16[128,768]{1,0:T(8,128)(2,1)S(1)}) conditional(s32[]{:T(128)} %convert_element_type.557, () %tuple.264, (bf16[128,768]{1,0:T(8,128)(2,1)S(1)}, f32[2,768]{1,0:T(2,128)}, bf16[2,768,2304]{2,1,0:T(8,128)(2,1)}, s32[4]{0:T(128)}, s32[]{:T(128)}, /*index=5*/s32[128,1]{0,1:T(1,128)S(1)}, s32[1,128]{1,0:T(1,128)S(1)}, s32[512]{0:T(512)}, ...), branch_computations={%region_1.1_spmd, %region_2.14_spmd} | conditional | flops 3835567360 | bytes 56483720 | solution.py:194
  148.2 35.3 %conditional.5 = (bf16[128,768]{1,0:T(8,128)(2,1)S(1)}) conditional(s32[]{:T(128)} %convert_element_type.557, () %tuple.264, (bf16[128,768]{1,0:T(8,128)(2,1)S(1)}, f32[2,768]{1,0:T(2,128)}, bf16[2,768,2304]{2,1,0:T(8,128)(2,1)}, s32[4]{0:T(128)}, s32[]{:T(128)}, /*index=5*/s32[128,1]{0,1:T(1,128)S(1)}, s32[1,128]{1,0:T(1,128)S(1)}, s32[512]{0:T(512)}, ...), branch_computations={%region_1.1_spmd, %region_2.14_spmd} | conditional | flops 3835567360 | bytes 56483720 | solution.py:194
  193.7 39.6 %collective-permute-start = (bf16[128,768]{1,0:T(8,128)(2,1)S(1)}, bf16[128,768]{1,0:T(8,128)(2,1)S(1)}, u32[]{:S(2)}, u32[]{:S(2)}) collective-permute-start(bf16[128,768]{1,0:T(8,128)(2,1)S(1)} %get-tuple-element.2342), channel_id=1, source_target_pairs={{0,8},{8,16},{16,24},{1,9},{9,17},{17,25},{2,10},{10,18},{18,26},{... | collective-permute-start | bytes 589832 | tf_op jit(solution)/shard_map/while/body/eval_jaxpr/ppermute | solution.py:20
  249.5 37.7 %collective-permute-start = (bf16[128,768]{1,0:T(8,128)(2,1)S(1)}, bf16[128,768]{1,0:T(8,128)(2,1)S(1)}, u32[]{:S(2)}, u32[]{:S(2)}) collective-permute-start(bf16[128,768]{1,0:T(8,128)(2,1)S(1)} %get-tuple-element.2342), channel_id=1, source_target_pairs={{0,8},{8,16},{16,24},{1,9},{9,17},{17,25},{2,10},{10,18},{18,26},{... | collective-permute-start | bytes 589832 | tf_op jit(solution)/shard_map/while/body/eval_jaxpr/ppermute | solution.py:20
  292.0 1150.5 %while.62 = (s32[]{:T(128)}, bf16[128,768]{1,0:T(8,128)(2,1)}, f32[768]{0:T(1024)}, f32[768,2304]{1,0:T(8,128)}, f32[768,768]{1,0:T(8,128)}, /*index=5*/f32[768]...) while((s32[]{:T(128)}, bf16[128,768]{1,0:T(8,128)(2,1)}, ...), condition=%wide.region_46.47_spmd.clone, body=%wide.region_17.46_spmd.clone.sunk | while | flops 10715431936 | bytes 721556480 | solution.py:246
  292.3 33.1 %conditional.6 = (bf16[128,768]{1,0:T(8,128)(2,1)}, f32[768]{0:T(1024)S(1)}, f32[768,2304]{1,0:T(8,128)}, f32[768,768]{1,0:T(8,128)}, f32[768]{0:T(1024)S(1)}, /...) conditional(s32[]{:T(128)} %convert_element_type.558, ...), branch_computations={%region_18.18_spmd, %region_19.45_spmd} | conditional | flops 10687015936 | bytes 388611008 | solution.py:232
  377.9 33.1 %conditional.6 = (bf16[128,768]{1,0:T(8,128)(2,1)}, f32[768]{0:T(1024)S(1)}, f32[768,2304]{1,0:T(8,128)}, f32[768,768]{1,0:T(8,128)}, f32[768]{0:T(1024)S(1)}, /...) conditional(s32[]{:T(128)} %convert_element_type.558, ...), branch_computations={%region_18.18_spmd, %region_19.45_spmd} | conditional | flops 10687015936 | bytes 388611008 | solution.py:232
  454.5 17.5 select_add_fusion.22
  475.8 33.1 %conditional.6 = (bf16[128,768]{1,0:T(8,128)(2,1)}, f32[768]{0:T(1024)S(1)}, f32[768,2304]{1,0:T(8,128)}, f32[768,768]{1,0:T(8,128)}, f32[768]{0:T(1024)S(1)}, /...) conditional(s32[]{:T(128)} %convert_element_type.558, ...), branch_computations={%region_18.18_spmd, %region_19.45_spmd} | conditional | flops 10687015936 | bytes 388611008 | solution.py:232
  569.9 117.6 %collective-permute-done.1 = bf16[128,768]{1,0:T(8,128)(2,1)S(1)} collective-permute-done((bf16[128,768]{1,0:T(8,128)(2,1)}, bf16[128,768]{1,0:T(8,128)(2,1)S(1)}, u32[]{:S(2)}, u32[]{:S(2)}) %collective-permute-start.1) | collective-permute-done | bytes 196640 | tf_op jit(solution)/shard_map/while/body/eval_jaxpr/ppermute | solution.py:20
  688.2 118.5 %conditional.6 = (bf16[128,768]{1,0:T(8,128)(2,1)}, f32[768]{0:T(1024)S(1)}, f32[768,2304]{1,0:T(8,128)}, f32[768,768]{1,0:T(8,128)}, f32[768]{0:T(1024)S(1)}, /...) conditional(s32[]{:T(128)} %convert_element_type.558, ...), branch_computations={%region_18.18_spmd, %region_19.45_spmd} | conditional | flops 10687015936 | bytes 388611008 | solution.py:232
  883.2 118.2 %conditional.6 = (bf16[128,768]{1,0:T(8,128)(2,1)}, f32[768]{0:T(1024)S(1)}, f32[768,2304]{1,0:T(8,128)}, f32[768,768]{1,0:T(8,128)}, f32[768]{0:T(1024)S(1)}, /...) conditional(s32[]{:T(128)} %convert_element_type.558, ...), branch_computations={%region_18.18_spmd, %region_19.45_spmd} | conditional | flops 10687015936 | bytes 388611008 | solution.py:232
  1045.8 17.5 select_add_fusion.22
  1067.8 118.4 %conditional.6 = (bf16[128,768]{1,0:T(8,128)(2,1)}, f32[768]{0:T(1024)S(1)}, f32[768,2304]{1,0:T(8,128)}, f32[768,768]{1,0:T(8,128)}, f32[768]{0:T(1024)S(1)}, /...) conditional(s32[]{:T(128)} %convert_element_type.558, ...), branch_computations={%region_18.18_spmd, %region_19.45_spmd} | conditional | flops 10687015936 | bytes 388611008 | solution.py:232
  1252.8 118.3 %conditional.6 = (bf16[128,768]{1,0:T(8,128)(2,1)}, f32[768]{0:T(1024)S(1)}, f32[768,2304]{1,0:T(8,128)}, f32[768,768]{1,0:T(8,128)}, f32[768]{0:T(1024)S(1)}, /...) conditional(s32[]{:T(128)} %convert_element_type.558, ...), branch_computations={%region_18.18_spmd, %region_19.45_spmd} | conditional | flops 10687015936 | bytes 388611008 | solution.py:232
  1516.2 24.8 %reduce-scatter.15.cloned.1.call-done = bf16[512,192]{0,1:T(8,128)(2,1)} async-done(((bf16[512,768]{0,1:T(8,128)(2,1)}), bf16[512,192]{0,1:T(8,128)(2,1)}) %reduce-scatter.15.cloned.1.call-update) | async-done | bytes 196624 | tf_op jit(solution)/shard_map/reduce_scatter | solution.py:276
  1542.7 43.9 %reduce-scatter.19.cloned.1.call-done = bf16[2,96,768]{2,1,0:T(8,128)(2,1)} async-done(((bf16[2,768,768]{2,1,0:T(8,128)(2,1)}), bf16[2,96,768]{2,1,0:T(8,128)(2,1)}) %reduce-scatter.19.cloned.1.call-update) | async-done | bytes 294928 | tf_op jit(solution)/shard_map/reduce_scatter | solution.py:255
  1588.4 67.5 %reduce-scatter.17.cloned.1.call-done = bf16[2,96,2304]{2,1,0:T(8,128)(2,1)} async-done(((bf16[2,768,2304]{2,1,0:T(8,128)(2,1)}), bf16[2,96,2304]{2,1,0:T(8,128)(2,1)}) %reduce-scatter.17.cloned.1.call-update) | async-done | bytes 884752 | tf_op jit(solution)/shard_map/reduce_scatter | solution.py:252
  1658.4 77.3 %reduce-scatter.21.cloned.1.call-done = bf16[2,96,3072]{2,1,0:T(8,128)(2,1)} async-done(((bf16[2,768,3072]{2,1,0:T(8,128)(2,1)}), bf16[2,96,3072]{2,1,0:T(8,128)(2,1)}) %reduce-scatter.21.cloned.1.call-update) | async-done | bytes 1179664 | tf_op jit(solution)/shard_map/reduce_scatter | solution.py:261
  1738.7 77.1 %reduce-scatter.23.cloned.1.call-done = bf16[2,384,768]{2,1,0:T(8,128)(2,1)} async-done(((bf16[2,3072,768]{2,1,0:T(8,128)(2,1)}), bf16[2,384,768]{2,1,0:T(8,128)(2,1)}) %reduce-scatter.23.cloned.1.call-update) | async-done | bytes 1179664 | tf_op jit(solution)/shard_map/reduce_scatter | solution.py:264
  1818.6 23.4 %reduce-scatter.13.cloned.1.call-done = bf16[512,192]{0,1:T(8,128)(2,1)} async-done(((bf16[512,768]{0,1:T(8,128)(2,1)}), bf16[512,192]{0,1:T(8,128)(2,1)}) %reduce-scatter.13.cloned.1.call-update) | async-done | bytes 196624 | tf_op jit(solution)/shard_map/reduce_scatter | solution.py:273
  (1493 shorter events, 1220.7 us)
Async XLA Ops:
  7.2 1501.2 %reduce-scatter.25.cloned.1.call-start = ((), (), s32[]{:S(2)}) async-start(), calls=%async_computation.14 | async-start | bytes 221184
  47.2 6.3 collective-permute-start
  91.4 8.6 collective-permute-start
  137.9 7.7 collective-permute-start
  183.5 7.5 collective-permute-start
  193.7 42.8 %collective-permute-start = (bf16[128,768]{1,0:T(8,128)(2,1)S(1)}, bf16[128,768]{1,0:T(8,128)(2,1)S(1)}, u32[]{:S(2)}, u32[]{:S(2)}) collective-permute-start(bf16[128,768]{1,0:T(8,128)(2,1)S(1)} %get-tuple-element.2342), channel_id=1, source_target_pairs={{0,8},{8,16},{16,24},{1,9},{9,17},{17,25},{2,10},{10,18},{18,26},{... | collective-permute-start | bytes 589832 | tf_op jit(solution)/shard_map/while/body/eval_jaxpr/ppermute | solution.py:20
  239.2 7.6 collective-permute-start
  249.5 40.9 %collective-permute-start = (bf16[128,768]{1,0:T(8,128)(2,1)S(1)}, bf16[128,768]{1,0:T(8,128)(2,1)S(1)}, u32[]{:S(2)}, u32[]{:S(2)}) collective-permute-start(bf16[128,768]{1,0:T(8,128)(2,1)S(1)} %get-tuple-element.2342), channel_id=1, source_target_pairs={{0,8},{8,16},{16,24},{1,9},{9,17},{17,25},{2,10},{10,18},{18,26},{... | collective-permute-start | bytes 589832 | tf_op jit(solution)/shard_map/while/body/eval_jaxpr/ppermute | solution.py:20
  325.5 48.7 %collective-permute-start.1 = (bf16[128,768]{1,0:T(8,128)(2,1)}, bf16[128,768]{1,0:T(8,128)(2,1)S(1)}, u32[]{:S(2)}, u32[]{:S(2)}) collective-permute-start(bf16[128,768]{1,0:T(8,128)(2,1)} %get-tuple-element.2141), channel_id=1, source_target_pairs={{8,0},{16,8},{24,16},{9,1},{17,9},{25,17},{10,2},{18,10},{26,18},{... | collective-permute-start | bytes 589832 | tf_op jit(solution)/shard_map/while/body/eval_jaxpr/ppermute | solution.py:20
  411.1 61.0 %collective-permute-start.1 = (bf16[128,768]{1,0:T(8,128)(2,1)}, bf16[128,768]{1,0:T(8,128)(2,1)S(1)}, u32[]{:S(2)}, u32[]{:S(2)}) collective-permute-start(bf16[128,768]{1,0:T(8,128)(2,1)} %get-tuple-element.2141), channel_id=1, source_target_pairs={{8,0},{16,8},{24,16},{9,1},{17,9},{25,17},{10,2},{18,10},{26,18},{... | collective-permute-start | bytes 589832 | tf_op jit(solution)/shard_map/while/body/eval_jaxpr/ppermute | solution.py:20
  508.9 178.6 %collective-permute-start.1 = (bf16[128,768]{1,0:T(8,128)(2,1)}, bf16[128,768]{1,0:T(8,128)(2,1)S(1)}, u32[]{:S(2)}, u32[]{:S(2)}) collective-permute-start(bf16[128,768]{1,0:T(8,128)(2,1)} %get-tuple-element.2141), channel_id=1, source_target_pairs={{8,0},{16,8},{24,16},{9,1},{17,9},{25,17},{10,2},{18,10},{26,18},{... | collective-permute-start | bytes 589832 | tf_op jit(solution)/shard_map/while/body/eval_jaxpr/ppermute | solution.py:20
  569.9 117.7 %copy-start.6 = (f32[3072,768]{1,0:T(8,128)}, f32[3072,768]{1,0:T(8,128)S(1)}, u32[]{:S(2)}) copy-start(f32[3072,768]{1,0:T(8,128)S(1)} %get-tuple-element.2318) | copy-start | bytes 28311556 | tf_op jit(solution)/shard_map/while
  569.9 117.6 %copy-start.52 = (f32[768]{0:T(1024)}, f32[768]{0:T(1024)S(1)}, u32[]{:S(2)}) copy-start(f32[768]{0:T(1024)S(1)} %get-tuple-element.2319) | copy-start | bytes 9220 | tf_op jit(solution)/shard_map/while
  806.7 75.3 %collective-permute-start.1 = (bf16[128,768]{1,0:T(8,128)(2,1)}, bf16[128,768]{1,0:T(8,128)(2,1)S(1)}, u32[]{:S(2)}, u32[]{:S(2)}) collective-permute-start(bf16[128,768]{1,0:T(8,128)(2,1)} %get-tuple-element.2141), channel_id=1, source_target_pairs={{8,0},{16,8},{24,16},{9,1},{17,9},{25,17},{10,2},{18,10},{26,18},{... | collective-permute-start | bytes 589832 | tf_op jit(solution)/shard_map/while/body/eval_jaxpr/ppermute | solution.py:20
  1001.4 65.5 %collective-permute-start.1 = (bf16[128,768]{1,0:T(8,128)(2,1)}, bf16[128,768]{1,0:T(8,128)(2,1)S(1)}, u32[]{:S(2)}, u32[]{:S(2)}) collective-permute-start(bf16[128,768]{1,0:T(8,128)(2,1)} %get-tuple-element.2141), channel_id=1, source_target_pairs={{8,0},{16,8},{24,16},{9,1},{17,9},{25,17},{10,2},{18,10},{26,18},{... | collective-permute-start | bytes 589832 | tf_op jit(solution)/shard_map/while/body/eval_jaxpr/ppermute | solution.py:20
  1186.2 65.7 %collective-permute-start.1 = (bf16[128,768]{1,0:T(8,128)(2,1)}, bf16[128,768]{1,0:T(8,128)(2,1)S(1)}, u32[]{:S(2)}, u32[]{:S(2)}) collective-permute-start(bf16[128,768]{1,0:T(8,128)(2,1)} %get-tuple-element.2141), channel_id=1, source_target_pairs={{8,0},{16,8},{24,16},{9,1},{17,9},{25,17},{10,2},{18,10},{26,18},{... | collective-permute-start | bytes 589832 | tf_op jit(solution)/shard_map/while/body/eval_jaxpr/ppermute | solution.py:20
  1371.1 61.9 %collective-permute-start.1 = (bf16[128,768]{1,0:T(8,128)(2,1)}, bf16[128,768]{1,0:T(8,128)(2,1)S(1)}, u32[]{:S(2)}, u32[]{:S(2)}) collective-permute-start(bf16[128,768]{1,0:T(8,128)(2,1)} %get-tuple-element.2141), channel_id=1, source_target_pairs={{8,0},{16,8},{24,16},{9,1},{17,9},{25,17},{10,2},{18,10},{26,18},{... | collective-permute-start | bytes 589832 | tf_op jit(solution)/shard_map/while/body/eval_jaxpr/ppermute | solution.py:20
  1444.8 70.0 %reduce-scatter.27.cloned.1.call-start = ((), (), s32[]{:S(2)}) async-start(), calls=%async_computation.15 | async-start | bytes 221184
  1447.1 93.9 %reduce-scatter.15.cloned.1.call-start = ((), (), s32[]{:S(2)}) async-start(), calls=%async_computation.9 | async-start | bytes 983040 | tf_op jit(solution)/shard_map/reduce_scatter | solution.py:276
  1449.7 136.9 %reduce-scatter.19.cloned.1.call-start = ((), (), s32[]{:S(2)}) async-start(), calls=%async_computation.11 | async-start | bytes 2654208 | tf_op jit(solution)/shard_map/reduce_scatter | solution.py:255
  1454.0 201.9 %reduce-scatter.17.cloned.1.call-start = ((), (), s32[]{:S(2)}) async-start(), calls=%async_computation.10 | async-start | bytes 7962624 | tf_op jit(solution)/shard_map/reduce_scatter | solution.py:252
  1467.2 268.5 %reduce-scatter.21.cloned.1.call-start = ((), (), s32[]{:S(2)}) async-start(), calls=%async_computation.12 | async-start | bytes 10616832 | tf_op jit(solution)/shard_map/reduce_scatter | solution.py:261
  1486.6 329.1 %reduce-scatter.23.cloned.1.call-start = ((), (), s32[]{:S(2)}) async-start(), calls=%async_computation.13 | async-start | bytes 10616832 | tf_op jit(solution)/shard_map/reduce_scatter | solution.py:264
  1505.9 336.0 %reduce-scatter.13.cloned.1.call-start = ((), (), s32[]{:S(2)}) async-start(), calls=%async_computation.8 | async-start | bytes 983040 | tf_op jit(solution)/shard_map/reduce_scatter | solution.py:273
  (359 other events, 2446.3 us)
Sparse Core Ops, SparseCore 0:
  1445.0 32.3 reduce-scatter.24
  1481.2 33.5 reduce-scatter.26
  1517.7 23.2 reduce-scatter.14
  1544.8 41.7 reduce-scatter.18
  1590.4 65.4 reduce-scatter.16
  1659.2 76.4 reduce-scatter.20
  1739.2 76.4 reduce-scatter.22
  1818.6 23.3 reduce-scatter.12
where the time goes:
time: 1860 us; the launch traced here: 1850 us
  other arithmetic  523 us (28%)
  waiting for transfers between devices  471 us (25%)
  matrix products  458 us (25%)
  local copies, waits for them, and re-layouts  207 us (11%)
  starting transfers between devices  106 us (6%)
  loops' own time  70 us (4%)
    add x42, other arithmetic, backward_tick(): total + term  383 us
    ppermute x14, waiting for transfers between devices, shifted(): return lax.ppermute(array, axis, pairs)  152 us
    ppermute x14, starting transfers between devices, shifted(): return lax.ppermute(array, axis, pairs)  105 us
    another operation x46, local copies, waits for them, and re-layouts  87.5 us
    reduce_scatter x1, waiting for transfers between devices, body(): lax.psum_scatter(stacked[4].astype(jnp.bfloat16), 'dp', scatter_dimension...  77.3 us
    reduce_scatter x1, waiting for transfers between devices, body(): lax.psum_scatter(stacked[5].astype(jnp.bfloat16), 'dp', scatter_dimension...  77.1 us
    reduce_scatter x1, waiting for transfers between devices, body(): lax.psum_scatter(stacked[1].astype(jnp.bfloat16), 'dp', scatter_dimension...  67.5 us
    dot_general x12, matrix products, layer_forward(): result = h + jnp.dot(active, w2, preferred_element_type=jnp.float32)  62.6 us
  transfers between devices with their start and end apart: 22, of which 18 were waited for; matrix products, arithmetic and copies ran while one was open for 26% of the time, Pallas kernels for 0%

commit v1 on v0

v1 whole, which is shorter than its diff:
```python
import functools

import jax
import jax.numpy as jnp
from jax import lax
from jax.experimental import pallas as pl
from jax.experimental.pallas import tpu as pltpu
from jax.sharding import PartitionSpec as P

D = 768
HEADS = 16
HEAD_DIM = 48
FF = 3072
SEQ = 128
EPS = 1e-06
MESH = pl.DeviceIdType.MESH
F32 = jnp.float32
BF16 = jnp.bfloat16
LOG2E = 1.4426950408889634
SCALE = HEAD_DIM ** (-0.5)
MIB = 2**20
CHUNK = 768

PAIRS = ((0, 1, 0), (0, 2, 96), (1, 2, 64), (2, 1, 32))
GROUP = 384


def nn(a, b):
    return jnp.dot(a, b, preferred_element_type=F32)


def nt(a, b):
    return lax.dot_general(a, b, (((1,), (1,)), ((), ())), preferred_element_type=F32)


def tn(a, b):
    return lax.dot_general(a, b, (((0,), (0,)), ((), ())), preferred_element_type=F32)


def lanes_of_head(first, width):
    lane = lax.broadcasted_iota(jnp.int32, (SEQ, width), 1)
    return ((lane >= first) & (lane < first + HEAD_DIM)).astype(F32).astype(BF16)


def two_heads(window, first):
    width = window.shape[1]
    return jnp.concatenate(
        [window * lanes_of_head(first, width), window * lanes_of_head(first + HEAD_DIM, width)], axis=0
    )


def add_window(tiles, first, part):
    for i in range(part.shape[1] // 128):
        piece = part[:, i * 128 : (i + 1) * 128]
        tiles[first + i] = piece if tiles[first + i] is None else tiles[first + i] + piece


def norm_parts(x):
    centre = x - jnp.mean(x, axis=-1, keepdims=True)
    spread = jnp.mean(centre * centre, axis=-1, keepdims=True)
    inverse = lax.rsqrt(spread + EPS)
    return centre * inverse, inverse


def gelu_parts(z):
    phi = 0.5 * (1.0 + lax.erf(z * 0.7071067811865476))
    density = jnp.exp2(z * z * (-0.5 * LOG2E)) * 0.3989422804014327
    return z * phi, phi + z * density


def relay_kernel(
    sections,
    micros,
    tokens,
    cotangent,
    flags,
    groups,
    gain_one,
    gain_two,
    wqkv_hbm,
    wout_hbm,
    wup_hbm,
    wdown_hbm,
    fin_out,
    inp_out,
    gains_out,
    u_out,
    dqkv_out,
    o_out,
    da_out,
    u2_out,
    dz_out,
    act_out,
    dm_out,
    wqkv,
    wout,
    wup,
    wdown,
    fwd_in,
    fwd_out,
    bwd_in,
    bwd_out,
    fin_stage,
    inp_stage,
    u_s,
    qkv_s,
    p_s,
    u2_s,
    gp_s,
    stat_s,
    o_s,
    act_s,
    dm_s,
    da_s,
    state,
    acc,
    bias,
    w_sem,
    in_sem,
    fwd_send,
    fwd_recv,
    bwd_send,
    bwd_recv,
    fin_send,
    fin_recv,
    inp_send,
    inp_recv,
    out_sem,
):
    me = lax.axis_index("pipe")
    last = sections - 1
    width = D // sections

    barrier = pltpu.get_barrier_semaphore()
    for j in range(sections):

        @pl.when(me != j)
        def _():
            pl.semaphore_signal(barrier, inc=1, device_id={"pipe": j}, device_id_type=MESH)

    def weight_copy(l, k):
        src = (wqkv_hbm, wout_hbm, wup_hbm, wdown_hbm)[k]
        dst = (wqkv, wout, wup, wdown)[k]
        return pltpu.make_async_copy(src.at[l], dst.at[l], w_sem.at[l, k])

    def token_copy(m):
        return pltpu.make_async_copy(tokens.at[pl.ds(m * SEQ, SEQ)], fwd_in.at[m], in_sem.at[0, m])

    def cotangent_copy(m):
        return pltpu.make_async_copy(cotangent.at[pl.ds(m * SEQ, SEQ)], bwd_in.at[m], in_sem.at[1, m])

    @pl.when(me == 0)
    def _():
        for m in range(micros):
            token_copy(m).start()

    for l in range(2):
        for k in range(4):
            weight_copy(l, k).start()

    @pl.when(me == last)
    def _():
        for m in range(micros):
            cotangent_copy(m).start()

    def forward_copy(m):
        return pltpu.make_async_remote_copy(
            src_ref=fwd_out.at[m],
            dst_ref=fwd_in.at[m],
            send_sem=fwd_send.at[m],
            recv_sem=fwd_recv.at[m],
            device_id={"pipe": lax.rem(me + 1, sections)},
            device_id_type=MESH,
        )

    def backward_copy(m):
        return pltpu.make_async_remote_copy(
            src_ref=bwd_out.at[m],
            dst_ref=bwd_in.at[m],
            send_sem=bwd_send.at[m],
            recv_sem=bwd_recv.at[m],
            device_id={"pipe": lax.rem(me + sections - 1, sections)},
            device_id_type=MESH,
        )

    def piece_copy(stage, out, send, recv, m, j):
        return pltpu.make_async_remote_copy(
            src_ref=stage.at[m, j],
            dst_ref=out.at[pl.ds(m * SEQ, SEQ)],
            send_sem=send.at[m, j],
            recv_sem=recv.at[m],
            device_id={"pipe": j},
            device_id_type=MESH,
        )

    def own_piece(stage, out, send, m, j):
        return pltpu.make_async_copy(stage.at[m, j], out.at[pl.ds(m * SEQ, SEQ)], send.at[m, j])

    def spread(stage, out, send, recv, m, source):
        for j in range(sections):
            stage[m, j] = state[:, j * width : (j + 1) * width].astype(BF16)
            if j == source:
                own_piece(stage, out, send, m, j).start()
            else:
                piece_copy(stage, out, send, recv, m, j).start()

    outs = (u_out, dqkv_out, o_out, da_out, u2_out, dz_out, act_out, dm_out)

    def out_copy(kind, l, m):
        slot = lax.rem(2 * m + l, 2)
        src = (
            u_s.at[l, m],
            qkv_s.at[l, m],
            o_s.at[slot],
            da_s.at[slot],
            u2_s.at[l, m],
            gp_s.at[l, m],
            act_s.at[slot],
            dm_s.at[slot],
        )[kind]
        return pltpu.make_async_copy(src, outs[kind].at[l, pl.ds(m * SEQ, SEQ)], out_sem.at[kind, l, m])

    def free_slot(kind, l, m):
        @pl.when(m > 0)
        def _():
            out_copy(kind, l, m - 1).wait()

    row = lax.broadcasted_iota(jnp.int32, (SEQ, SEQ), 0) // (SEQ // 4)
    column = lax.broadcasted_iota(jnp.int32, (SEQ, SEQ), 1) // (SEQ // 4)
    same = (row == column).astype(F32)
    for m in range(micros):
        parted = (jnp.full((1, SEQ), groups[m], jnp.int32) == 1).astype(F32)
        valid = (flags[pl.ds(m, 1), :] == 1).astype(F32)
        keep = jnp.maximum(same, 1.0 - parted) * valid
        bias[m] = (keep - 1.0) * 1e30

    pl.semaphore_wait(barrier, sections - 1)

    def forward_layer(l, m):
        first = m == 0

        def weight_wait(k):
            @pl.when(first)
            def _():
                weight_copy(l, k).wait()

        x = state[...]
        xhat, inverse = norm_parts(x)
        stat_s[l, m, :, 0:1] = inverse
        u = (xhat * gain_one[pl.ds(l, 1), :]).astype(BF16)
        u_s[l, m] = u
        out_copy(0, l, m).start()
        weight_wait(0)
        for c in range(0, 3 * D, CHUNK):
            qkv_s[l, m, :, c : c + CHUNK] = nn(u_s[l, m], wqkv[l, :, c : c + CHUNK]).astype(BF16)
        free_slot(2, l, m)
        slot = lax.rem(2 * m + l, 2)
        added = bias[m]
        for g in range(2):
            tiles = [None] * 3
            for j, (tile, count, inside) in enumerate(PAIRS):
                lo = g * GROUP + tile * 128
                hi = lo + count * 128
                q = qkv_s[l, m, :, lo:hi]
                k = two_heads(qkv_s[l, m, :, D + lo : D + hi], inside)
                v = two_heads(qkv_s[l, m, :, 2 * D + lo : 2 * D + hi], inside)
                s = nt(q, k) * (SCALE * LOG2E)
                halves = []
                for h in range(2):
                    sh = s[:, h * SEQ : (h + 1) * SEQ] + added
                    e = jnp.exp2(sh - jnp.max(sh, axis=-1, keepdims=True))
                    halves.append(e * (1.0 / jnp.sum(e, axis=-1, keepdims=True)))
                p = jnp.concatenate(halves, axis=1).astype(BF16)
                at = (g * 4 + j) * 2 * SEQ
                p_s[l, m, :, at : at + 2 * SEQ] = p
                add_window(tiles, tile, nn(p, v))
            for i in range(3):
                at = g * GROUP + i * 128
                o_s[slot, :, at : at + 128] = tiles[i].astype(BF16)
        out_copy(2, l, m).start()
        weight_wait(1)
        h = state[...] + nn(o_s[slot], wout[l])
        state[...] = h
        hhat, inverse = norm_parts(h)
        stat_s[l, m, :, 1:2] = inverse
        u2_s[l, m] = (hhat * gain_two[pl.ds(l, 1), :]).astype(BF16)
        out_copy(4, l, m).start()
        weight_wait(2)
        free_slot(6, l, m)
        weight_wait(3)
        total = state[...]
        for c in range(0, FF, CHUNK):
            z = nn(u2_s[l, m], wup[l, :, c : c + CHUNK])
            act, slope = gelu_parts(z)
            act = act.astype(BF16)
            act_s[slot, :, c : c + CHUNK] = act
            gp_s[l, m, :, c : c + CHUNK] = slope.astype(BF16)
            total = total + nn(act, wdown[l, c : c + CHUNK, :])
        state[...] = total
        out_copy(6, l, m).start()

    def norm_back(du, hat_scaled, gain, inverse):
        t = du * gain
        hat = hat_scaled * (1.0 / gain)
        weighted = du * hat_scaled
        return inverse * (
            t - jnp.mean(t, axis=-1, keepdims=True) - hat * jnp.mean(weighted, axis=-1, keepdims=True)
        ), weighted

    def add_rows(at, weighted):
        part = weighted[0:8]
        for r in range(8, SEQ, 8):
            part = part + weighted[r : r + 8]
        acc[at] = acc[at] + part

    def backward_layer(l, m):
        slot = lax.rem(2 * m + l, 2)
        dy = state[...]
        free_slot(7, l, m)
        dm_s[slot] = dy.astype(BF16)
        out_copy(7, l, m).start()
        total = None
        for c in range(0, FF, CHUNK):
            da = nt(dm_s[slot], wdown[l, c : c + CHUNK, :])
            dz = (gp_s[l, m, :, c : c + CHUNK].astype(F32) * da).astype(BF16)
            gp_s[l, m, :, c : c + CHUNK] = dz
            part = nt(dz, wup[l, :, c : c + CHUNK])
            total = part if total is None else total + part
        out_copy(5, l, m).start()
        dh, weighted = norm_back(
            total, u2_s[l, m].astype(F32), gain_two[pl.ds(l, 1), :], stat_s[l, m, :, 1:2]
        )
        add_rows(2 + l, weighted)
        dh = state[...] + dh
        state[...] = dh
        free_slot(3, l, m)
        da_s[slot] = dh.astype(BF16)
        out_copy(3, l, m).start()
        do = nt(da_s[slot], wout[l]).astype(BF16)
        for g in range(2):
            q_tiles, k_tiles, v_tiles = [None] * 3, [None] * 3, [None] * 3
            for j, (tile, count, inside) in enumerate(PAIRS):
                lo = g * GROUP + tile * 128
                hi = lo + count * 128
                q2 = two_heads(qkv_s[l, m, :, lo:hi], inside)
                k2 = two_heads(qkv_s[l, m, :, D + lo : D + hi], inside)
                v2 = two_heads(qkv_s[l, m, :, 2 * D + lo : 2 * D + hi], inside)
                d2 = two_heads(do[:, lo:hi], inside)
                at = (g * 4 + j) * 2 * SEQ
                p = p_s[l, m, :, at : at + 2 * SEQ]
                dp = nt(do[:, lo:hi], v2)
                halves = []
                for h in range(2):
                    ph = p[:, h * SEQ : (h + 1) * SEQ].astype(F32)
                    dph = dp[:, h * SEQ : (h + 1) * SEQ]
                    inner = jnp.sum(ph * dph, axis=-1, keepdims=True)
                    halves.append((ph * (dph - inner)).astype(BF16))
                add_window(q_tiles, tile, nn(jnp.concatenate(halves, axis=1), k2))
                add_window(k_tiles, tile, tn(jnp.concatenate(halves, axis=0), q2))
                stacked = jnp.concatenate([p[:, :SEQ], p[:, SEQ:]], axis=0)
                add_window(v_tiles, tile, tn(stacked, d2))
            for i in range(3):
                at = g * GROUP + i * 128
                qkv_s[l, m, :, at : at + 128] = (q_tiles[i] * SCALE).astype(BF16)
                qkv_s[l, m, :, D + at : D + at + 128] = (k_tiles[i] * SCALE).astype(BF16)
                qkv_s[l, m, :, 2 * D + at : 2 * D + at + 128] = v_tiles[i].astype(BF16)
        out_copy(1, l, m).start()
        du = nt(qkv_s[l, m], wqkv[l])
        dx, weighted = norm_back(
            du, u_s[l, m].astype(F32), gain_one[pl.ds(l, 1), :], stat_s[l, m, :, 0:1]
        )
        add_rows(l, weighted)
        state[...] = state[...] + dx

    def forward_micro(m, carry):
        @pl.when(me == 0)
        def _():
            token_copy(m).wait()

        @pl.when(me > 0)
        def _():
            forward_copy(m).wait_recv()

        state[...] = fwd_in[m].astype(F32)

        def one(l, c):
            forward_layer(l, m)
            return c

        lax.fori_loop(0, 2, one, 0)

        @pl.when(me < last)
        def _():
            fwd_out[m] = state[...].astype(BF16)
            forward_copy(m).start()

        @pl.when(me == last)
        def _():
            spread(fin_stage, fin_out, fin_send, fin_recv, m, last)

        return carry

    lax.fori_loop(0, micros, forward_micro, 0)

    acc[...] = jnp.zeros_like(acc)

    def backward_micro(m, carry):
        @pl.when(me == last)
        def _():
            cotangent_copy(m).wait()

        @pl.when(me < last)
        def _():
            backward_copy(m).wait_recv()

        state[...] = bwd_in[m].astype(F32)

        def one(i, c):
            backward_layer(1 - i, m)
            return c

        lax.fori_loop(0, 2, one, 0)

        @pl.when(me > 0)
        def _():
            bwd_out[m] = state[...].astype(BF16)
            backward_copy(m).start()

        @pl.when(me == 0)
        def _():
            spread(inp_stage, inp_out, inp_send, inp_recv, m, 0)

        return carry

    lax.fori_loop(0, micros, backward_micro, 0)
    for l in range(2):
        gains_out[l : l + 1, :] = jnp.sum(acc[l], axis=0, keepdims=True) / gain_one[l : l + 1, :]
        gains_out[2 + l : 3 + l, :] = jnp.sum(acc[2 + l], axis=0, keepdims=True) / gain_two[l : l + 1, :]

    for l in range(2):
        for kind in (2, 3, 6, 7):
            out_copy(kind, l, micros - 1).wait()
        for m in range(micros):
            for kind in (0, 1, 4, 5):
                out_copy(kind, l, m).wait()
    for m in range(micros):

        @pl.when(me < last)
        def _():
            forward_copy(m).wait_send()

        @pl.when(me > 0)
        def _():
            backward_copy(m).wait_send()

        for source, stage, out, send, recv in (
            (last, fin_stage, fin_out, fin_send, fin_recv),
            (0, inp_stage, inp_out, inp_send, inp_recv),
        ):

            @pl.when(me == source)
            def _():
                for j in range(sections):
                    if j == source:
                        own_piece(stage, out, send, m, j).wait()
                    else:
                        piece_copy(stage, out, send, recv, m, j).wait_send()

            @pl.when(me != source)
            def _():
                piece_copy(stage, out, send, recv, m, source).wait_recv()


def relay(tokens, cotangent, flags, groups, gain_one, gain_two, wqkv, wout, wup, wdown):
    sections = lax.axis_size("pipe")
    rows = tokens.shape[0]
    micros = rows // SEQ
    width = D // sections
    anywhere = pl.BlockSpec(memory_space=pl.ANY)
    vmem = pl.BlockSpec(memory_space=pltpu.VMEM)
    smem = pl.BlockSpec(memory_space=pltpu.SMEM)
    dma = pltpu.SemaphoreType.DMA

    def factor(columns):
        return jax.ShapeDtypeStruct((2, rows, columns), BF16)

    def saved(columns):
        return pltpu.VMEM((2, micros, SEQ, columns), BF16)

    def two(columns):
        return pltpu.VMEM((2, SEQ, columns), BF16)

    def per_micro(columns):
        return pltpu.VMEM((micros, SEQ, columns), BF16)

    return pl.pallas_call(
        functools.partial(relay_kernel, sections, micros),
        out_shape=(
            jax.ShapeDtypeStruct((rows, width), BF16),
            jax.ShapeDtypeStruct((rows, width), BF16),
            jax.ShapeDtypeStruct((4, D), F32),
            factor(D),
            factor(3 * D),
            factor(D),
            factor(D),
            factor(D),
            factor(FF),
            factor(FF),
            factor(D),
        ),
        in_specs=[anywhere, anywhere, vmem, smem, vmem, vmem] + [anywhere] * 4,
        out_specs=(anywhere, anywhere, vmem) + (anywhere,) * 8,
        scratch_shapes=[
            pltpu.VMEM((2, D, 3 * D), BF16),
            pltpu.VMEM((2, D, D), BF16),
            pltpu.VMEM((2, D, FF), BF16),
            pltpu.VMEM((2, FF, D), BF16),
            per_micro(D),
            per_micro(D),
            per_micro(D),
            per_micro(D),
            pltpu.VMEM((micros, sections, SEQ, width), BF16),
            pltpu.VMEM((micros, sections, SEQ, width), BF16),
            saved(D),
            saved(3 * D),
            saved(HEADS * SEQ),
            saved(D),
            saved(FF),
            pltpu.VMEM((2, micros, SEQ, 128), F32),
            two(D),
            two(FF),
            two(D),
            two(D),
            pltpu.VMEM((SEQ, D), F32),
            pltpu.VMEM((4, 8, D), F32),
            pltpu.VMEM((micros, SEQ, SEQ), F32),
            dma((2, 4)),
            dma((2, micros)),
            dma((micros,)),
            dma((micros,)),
            dma((micros,)),
            dma((micros,)),
            dma((micros, sections)),
            dma((micros,)),
            dma((micros, sections)),
            dma((micros,)),
            dma((8, 2, micros)),
        ],
        compiler_params=pltpu.CompilerParams(
            collective_id=0, has_side_effects=True, vmem_limit_bytes=60 * MIB
        ),
        name="relay",
    )(tokens, cotangent, flags, groups, gain_one, gain_two, wqkv, wout, wup, wdown)


def body(
    tokens,
    gain_one,
    qkv_weight,
    out_weight,
    gain_two,
    up_weight,
    down_weight,
    cotangent,
    flags,
    groups,
):
    micros = tokens.shape[0] // SEQ
    fin, inp, gains, u, dqkv, o, da, u2, dz, act, dm = relay(
        tokens,
        cotangent,
        flags.reshape(micros, SEQ),
        groups,
        gain_one,
        gain_two,
        qkv_weight,
        out_weight,
        up_weight,
        down_weight,
    )

    def grad(a, g):
        return jnp.einsum("lsa,lsb->lab", a, g, preferred_element_type=F32).astype(BF16)

    def scattered(total):
        return lax.psum_scatter(total, "dp", scatter_dimension=1, tiled=True).astype(F32)

    return (
        fin,
        inp.astype(F32),
        scattered(gains[0:2].astype(BF16)),
        scattered(grad(u, dqkv)),
        scattered(grad(o, da)),
        scattered(gains[2:4].astype(BF16)),
        scattered(grad(u2, dz)),
        scattered(grad(act, dm)),
    )


def solution(mesh):
    return jax.shard_map(
        body,
        mesh=mesh,
        in_specs=(
            P("dp", None),
            P("pipe", None),
            P("pipe", None, None),
            P("pipe", None, None),
            P("pipe", None),
            P("pipe", None, None),
            P("pipe", None, None),
            P("dp", None),
            P("dp"),
            P("dp"),
        ),
        out_specs=(
            P("dp", "pipe"),
            P("dp", "pipe"),
            P("pipe", "dp"),
            P("pipe", "dp", None),
            P("pipe", "dp", None),
            P("pipe", "dp"),
            P("pipe", "dp", None),
            P("pipe", "dp", None),
        ),
        check_vma=False,
    )
```

time: 1860 us -> 591 us (0.32)
  other arithmetic: 523 us -> 12 us
  matrix products: 458 us -> 35.8 us
  Pallas kernels: 0 us -> 223 us
  local copies, waits for them, and re-layouts: 207 us -> 9.73 us
  waiting for transfers between devices: 471 us -> 295 us
  starting transfers between devices: 106 us -> 0.43 us
  loops' own time: 70 us -> 0 us
    dot_general x180 -> x4, matrix products: 454 us -> 35.8 us  [grad(): jnp.einsum('lsa,lsb->lab', a, g, preferred_element_type=F32).astype(BF16)]
    add x66 -> x0, other arithmetic: 392 us -> none  [the longest x42 383 us: backward_tick(): total + term]
    pallas_call x0 -> x1, Pallas kernels: none -> 223 us  [relay(): pl.pallas_call(functools.partial(relay_kernel, sections, micros), out_sha...]
    ppermute x14 -> x0, waiting for transfers between devices: 152 us -> none  [shifted(): return lax.ppermute(array, axis, pairs)]
    ppermute x14 -> x0, starting transfers between devices: 105 us -> none  [shifted(): return lax.ppermute(array, axis, pairs)]
    another operation x50 -> x0, local copies, waits for them, and re-layouts: 87.5 us -> none
    another operation x16 -> x0, loops' own time: 70 us -> none  [the longest x7 58.6 us: backward_tick(): lax.cond(active, work, grad_zeros, grad_out)]
    another operation x14 -> x1, other arithmetic: 58 us -> 0.71 us  [the longest x10 55.3 us: body(): jnp.stack([first, second])]
  transfers between devices with their start and end apart: 22 -> 6, of which waited for: 18 -> 5; matrix products, arithmetic and copies ran while one was open for 26% -> 8% of each run, Pallas kernels for 0% -> 0%
where the time goes in v1:
time: 591 us
  waiting for transfers between devices  295 us (50%)
  Pallas kernels  223 us (38%)
  matrix products  35.8 us (6%)
  between operations  14.1 us (2%)
  other arithmetic  12 us (2%)
  local copies, waits for them, and re-layouts  9.73 us (2%)
    reduce_scatter x4, waiting for transfers between devices, scattered(): lax.psum_scatter(total, 'dp', scatter_dimension=1, tiled=True).astype(F32)  267 us
    pallas_call x1, Pallas kernels, relay(): pl.pallas_call(functools.partial(relay_kernel, sections, micros), out_sha...  223 us
    dot_general x4, matrix products, grad(): jnp.einsum('lsa,lsb->lab', a, g, preferred_element_type=F32).astype(BF16)  35.8 us
    unnamed x8, waiting for transfers between devices  28.3 us
  transfers between devices with their start and end apart: 6, of which 5 were waited for; matrix products, arithmetic and copies ran while one was open for 8% of the time, Pallas kernels for 0%

profile of v1, /device:TPU:0, one launch (start us, length us, event | category | flops | bytes accessed | tf_op | source)
XLA Modules:
  0.0 590.7 jit_solution(2050248735194646833)
XLA Ops:
  7.2 223.5 %relay.1 = (bf16[512,192]{1,0:T(8,128)(2,1)}, bf16[512,192]{1,0:T(8,128)(2,1)}, f32[4,768]{1,0:T(4,128)}, bf16[2,512,768]{2,1,0:T(8,128)(2,1)}, bf16[2,512,2304]...) custom-call(bf16[512,768]{1,0:T(8,128)(2,1)} %tokens.1, ...), custom_call_target="tpu_custom_call" | custom-call | tf_op jit(solution)/shard_map/relay/pallas_call | solution.py:496
  231.4 0.8 copy.36
  232.3 0.8 copy.34
  233.3 4.7 convolution_convert_fusion.3
  238.2 1.2 copy-done.4
  239.4 8.3 %convolution_convert_fusion.2 = bf16[2,768,2304]{2,1,0:T(8,128)(2,1)} fusion(bf16[2,512,768]{2,1,0:T(8,128)(2,1)S(1)} %copy-done.4, bf16[2,512,2304]{2,1,0:T(8,128)(2,1)} %get-tuple-element.23), kind=kOutput, calls=%fused_computation.2 | convolution fusion | flops 3627417600 | bytes 13369344 | tf_op jit(solution)/shard_map/lsa,lsb->lab/dot_general | solution.py:583
  247.8 1.3 copy-done.3
  249.1 10.3 %convolution_convert_fusion.1 = bf16[2,768,3072]{2,1,0:T(8,128)(2,1)} fusion(bf16[2,512,768]{2,1,0:T(8,128)(2,1)S(1)} %copy-done.3, bf16[2,512,3072]{2,1,0:T(8,128)(2,1)} %get-tuple-element.27), kind=kOutput, calls=%fused_computation.1 | convolution fusion | flops 4836556800 | bytes 17301504 | tf_op jit(solution)/shard_map/lsa,lsb->lab/dot_general | solution.py:583
  259.5 1.3 copy-done.2
  260.9 12.4 %convolution_convert_fusion = bf16[2,3072,768]{2,1,0:T(8,128)(2,1)} fusion(bf16[2,512,3072]{2,1,0:T(8,128)(2,1)} %get-tuple-element.28, bf16[2,512,768]{2,1,0:T(8,128)(2,1)S(1)} %copy-done.2), kind=kOutput, calls=%fused_computation | convolution fusion | flops 4836556800 | bytes 17301504 | tf_op jit(solution)/shard_map/lsa,lsb->lab/dot_general | solution.py:583
  273.3 0.9 copy-done
  274.2 0.8 copy.28
  275.0 0.9 copy.29
  275.9 0.8 copy.37
  277.3 28.2 %reduce-scatter.19.cloned.1.call-done = bf16[96,2]{1,0:T(8,128)(2,1)} async-done(((bf16[768,2]{1,0:T(8,128)(2,1)}), bf16[96,2]{1,0:T(8,128)(2,1)}) %reduce-scatter.19.cloned.1.call-update) | async-done | bytes 400
  305.5 0.8 copy.35
  306.8 45.1 %reduce-scatter.13.cloned.1.call-done = bf16[2,96,768]{2,1,0:T(8,128)(2,1)} async-done(((bf16[2,768,768]{2,1,0:T(8,128)(2,1)}), bf16[2,96,768]{2,1,0:T(8,128)(2,1)}) %reduce-scatter.13.cloned.1.call-update) | async-done | bytes 294928 | tf_op jit(solution)/shard_map/reduce_scatter | solution.py:586
  351.9 1.8 convert_element_type.40
  353.7 67.5 %reduce-scatter.11.cloned.1.call-done = bf16[2,96,2304]{2,1,0:T(8,128)(2,1)} async-done(((bf16[2,768,2304]{2,1,0:T(8,128)(2,1)}), bf16[2,96,2304]{2,1,0:T(8,128)(2,1)}) %reduce-scatter.11.cloned.1.call-update) | async-done | bytes 884752 | tf_op jit(solution)/shard_map/reduce_scatter | solution.py:586
  421.2 2.5 convert_element_type.38
  423.7 77.4 %reduce-scatter.15.cloned.1.call-done = bf16[2,96,3072]{2,1,0:T(8,128)(2,1)} async-done(((bf16[2,768,3072]{2,1,0:T(8,128)(2,1)}), bf16[2,96,3072]{2,1,0:T(8,128)(2,1)}) %reduce-scatter.15.cloned.1.call-update) | async-done | bytes 1179664 | tf_op jit(solution)/shard_map/reduce_scatter | solution.py:586
  501.1 2.9 convert_element_type.43
  504.1 77.0 %reduce-scatter.17.cloned.1.call-done = bf16[2,384,768]{2,1,0:T(8,128)(2,1)} async-done(((bf16[2,3072,768]{2,1,0:T(8,128)(2,1)}), bf16[2,384,768]{2,1,0:T(8,128)(2,1)}) %reduce-scatter.17.cloned.1.call-update) | async-done | bytes 1179664 | tf_op jit(solution)/shard_map/reduce_scatter | solution.py:586
  581.0 2.8 convert_element_type.45
  (23 shorter events, 2.4 us)
Async XLA Ops:
  7.2 268.7 %reduce-scatter.21.cloned.1.call-start = ((), (), s32[]{:S(2)}) async-start(), calls=%async_computation.11 | async-start | bytes 221184
  232.3 73.2 %reduce-scatter.19.cloned.1.call-start = ((), (), s32[]{:S(2)}) async-start(), calls=%async_computation.10 | async-start | bytes 221184
  233.2 118.7 %reduce-scatter.13.cloned.1.call-start = ((), (), s32[]{:S(2)}) async-start(), calls=%async_computation.7 | async-start | bytes 2654208 | tf_op jit(solution)/shard_map/reduce_scatter | solution.py:586
  238.0 1.4 copy-start.4
  238.0 183.2 %reduce-scatter.11.cloned.1.call-start = ((), (), s32[]{:S(2)}) async-start(), calls=%async_computation.6 | async-start | bytes 7962624 | tf_op jit(solution)/shard_map/reduce_scatter | solution.py:586
  247.7 1.4 copy-start.3
  247.7 253.4 %reduce-scatter.15.cloned.1.call-start = ((), (), s32[]{:S(2)}) async-start(), calls=%async_computation.8 | async-start | bytes 10616832 | tf_op jit(solution)/shard_map/reduce_scatter | solution.py:586
  259.5 1.4 copy-start.2
  259.5 321.5 %reduce-scatter.17.cloned.1.call-start = ((), (), s32[]{:S(2)}) async-start(), calls=%async_computation.9 | async-start | bytes 10616832 | tf_op jit(solution)/shard_map/reduce_scatter | solution.py:586
  273.3 0.9 copy-start
  273.3 1.8 copy-start.1
Sparse Core Ops, SparseCore 0:
  232.4 35.5 reduce-scatter.20
  271.9 33.4 reduce-scatter.18
  309.4 42.4 reduce-scatter.12
  355.7 65.5 reduce-scatter.10
  424.6 76.4 reduce-scatter.14
  504.5 76.4 reduce-scatter.16

commit v2 on v1

--- a/solution.py
+++ b/solution.py
@@ -70,6 +70,7 @@
 
 def relay_kernel(
     sections,
+    replicas,
     micros,
     tokens,
     cotangent,
@@ -433,9 +434,12 @@
         return carry
 
     lax.fori_loop(0, micros, backward_micro, 0)
-    for l in range(2):
-        gains_out[l : l + 1, :] = jnp.sum(acc[l], axis=0, keepdims=True) / gain_one[l : l + 1, :]
-        gains_out[2 + l : 3 + l, :] = jnp.sum(acc[2 + l], axis=0, keepdims=True) / gain_two[l : l + 1, :]
+    share = D // replicas
+    for k in range(4):
+        gain = (gain_one, gain_two)[k // 2][k % 2 : k % 2 + 1, :]
+        total = jnp.sum(acc[k], axis=0, keepdims=True) / gain
+        for r in range(replicas):
+            gains_out[r, k : k + 1, 0:share] = total[:, r * share : (r + 1) * share]
 
     for l in range(2):
         for kind in (2, 3, 6, 7):
@@ -473,6 +477,7 @@
 
 def relay(tokens, cotangent, flags, groups, gain_one, gain_two, wqkv, wout, wup, wdown):
     sections = lax.axis_size("pipe")
+    replicas = lax.axis_size("dp")
     rows = tokens.shape[0]
     micros = rows // SEQ
     width = D // sections
@@ -494,11 +499,11 @@
         return pltpu.VMEM((micros, SEQ, columns), BF16)
 
     return pl.pallas_call(
-        functools.partial(relay_kernel, sections, micros),
+        functools.partial(relay_kernel, sections, replicas, micros),
         out_shape=(
             jax.ShapeDtypeStruct((rows, width), BF16),
             jax.ShapeDtypeStruct((rows, width), BF16),
-            jax.ShapeDtypeStruct((4, D), F32),
+            jax.ShapeDtypeStruct((replicas, 8, 128), F32),
             factor(D),
             factor(3 * D),
             factor(D),
@@ -553,6 +558,270 @@
     )(tokens, cotangent, flags, groups, gain_one, gain_two, wqkv, wout, wup, wdown)
 
 
+SHARDS = 8
+ROWS = 96
+CHUNKS = 12
+
+
+def sum_kernel(
+    gains_in,
+    u_in,
+    dqkv_in,
+    o_in,
+    da_in,
+    u2_in,
+    dz_in,
+    act_in,
+    dm_in,
+    gains_out,
+    qkv_out,
+    out_out,
+    up_out,
+    down_out,
+    u_v,
+    dqkv_v,
+    o_v,
+    da_v,
+    u2_v,
+    dz_v,
+    act_v,
+    dm_v,
+    own,
+    first,
+    second,
+    third,
+    gains_v,
+    load_sem,
+    gain_send,
+    gain_recv,
+    send,
+    recv,
+    out_sem,
+):
+    me = lax.axis_index("dp")
+    core = lax.rem(me, 2)
+    x = lax.rem(me // 2, 2)
+    y = me // 4
+    other_core = me + 1 - 2 * core
+    other_x = me + 2 - 4 * x
+    other_y = me + 4 - 8 * y
+
+    barrier = pltpu.get_barrier_semaphore()
+    for j in range(SHARDS):
+
+        @pl.when(me != j)
+        def _():
+            pl.semaphore_signal(barrier, inc=1, device_id={"dp": j}, device_id_type=MESH)
+
+    sources = (u_in, dqkv_in, o_in, da_in, u2_in, dz_in, act_in, dm_in)
+    held = (u_v, dqkv_v, o_v, da_v, u2_v, dz_v, act_v, dm_v)
+
+    def load(k, l):
+        return pltpu.make_async_copy(sources[k].at[l], held[k], load_sem.at[k])
+
+    for k in range(8):
+        load(k, 1).start()
+
+    pl.semaphore_wait(barrier, SHARDS - 1)
+
+    def gain_copy(j, source):
+        return pltpu.make_async_remote_copy(
+            src_ref=gains_in.at[j],
+            dst_ref=gains_v.at[source],
+            send_sem=gain_send.at[j],
+            recv_sem=gain_recv.at[source],
+            device_id={"dp": j},
+            device_id_type=MESH,
+        )
+
+    for j in range(SHARDS):
+
+        @pl.when(me != j)
+        def _():
+            gain_copy(j, me).start()
+
+    def remote(src, dst, step, n, to):
+        return pltpu.make_async_remote_copy(
+            src_ref=src,
+            dst_ref=dst,
+            send_sem=send.at[step, n],
+            recv_sem=recv.at[step, n],
+            device_id={"dp": to},
+            device_id_type=MESH,
+        )
+
+    def give_copy(n, i):
+        return remote(own.at[i, 1 - core], first.at[n], 0, n, other_core)
+
+    def first_copy(n, i):
+        if i % 2 == 0:
+            return remote(first.at[n, :, 1 - x], second.at[n], 1, n, other_x)
+        return remote(first.at[n, 1 - y], second.at[n], 1, n, other_y)
+
+    def second_copy(n, i):
+        if i % 2 == 0:
+            return remote(second.at[n, 1 - y], third.at[n], 2, n, other_y)
+        return remote(second.at[n, 1 - x], third.at[n], 2, n, other_x)
+
+    def result_copy(n, l, i):
+        if i < 3:
+            dst = qkv_out.at[l, :, pl.ds(i * CHUNK, CHUNK)]
+        elif i < 4:
+            dst = out_out.at[l]
+        elif i < 8:
+            dst = up_out.at[l, :, pl.ds((i - 4) * CHUNK, CHUNK)]
+        else:
+            dst = down_out.at[l, pl.ds((i - 8) * ROWS, ROWS)]
+        return pltpu.make_async_copy(third.at[n], dst, out_sem.at[n])
+
+    def add_core(n, i):
+        give_copy(n, i).wait_recv()
+        first[n] = first[n] + own[i, core]
+        first_copy(n, i).start()
+
+    def layer_products(step, carry):
+        l = 1 - step
+        base = step * CHUNKS
+
+        def free(i):
+            @pl.when(step > 0)
+            def _():
+                give_copy(i, i).wait_send()
+
+        def products(k, a, g, slots):
+            load(k, l).wait()
+            load(k + 1, l).wait()
+            for i, columns in slots:
+                free(i)
+                part = tn(a[...], g[:, columns * CHUNK : (columns + 1) * CHUNK]).astype(BF16)
+                for r in range(SHARDS):
+                    own[i, r % 2, r // 4, (r // 2) % 2] = part[r * ROWS : (r + 1) * ROWS]
+                give_copy(base + i, i).start()
+                if i > 0:
+                    add_core(base + i - 1, i - 1)
+
+        def reload(k):
+            @pl.when(step == 0)
+            def _():
+                load(k, 0).start()
+                load(k + 1, 0).start()
+
+        products(0, u_v, dqkv_v, ((0, 0), (1, 1), (2, 2)))
+        reload(0)
+        products(2, o_v, da_v, ((3, 0),))
+        reload(2)
+        products(4, u2_v, dz_v, ((4, 0), (5, 1), (6, 2), (7, 3)))
+        reload(4)
+        load(6, l).wait()
+        load(7, l).wait()
+        for i in range(8, CHUNKS):
+            free(i)
+        for b in range(4):
+            part = tn(act_v[:, b * CHUNK : (b + 1) * CHUNK], dm_v[...]).astype(BF16)
+            for r in range(8):
+                own[8 + r % 4, r // 4, b // 2, b % 2] = part[r * ROWS : (r + 1) * ROWS]
+        reload(6)
+        for i in range(8, CHUNKS):
+            give_copy(base + i, i).start()
+        for i in range(7, CHUNKS):
+            add_core(base + i, i)
+        return carry
+
+    lax.fori_loop(0, 2, layer_products, 0)
+
+    def second_sums(step, carry):
+        for i in range(CHUNKS):
+            n = step * CHUNKS + i
+            first_copy(n, i).wait_recv()
+            kept = first[n, :, x] if i % 2 == 0 else first[n, y]
+            second[n] = second[n] + kept
+            second_copy(n, i).start()
+        return carry
+
+    lax.fori_loop(0, 2, second_sums, 0)
+
+    gains_v[me] = gains_in[me]
+    for j in range(SHARDS):
+
+        @pl.when(me != j)
+        def _():
+            gain_copy(j, j).wait_recv()
+
+    total = gains_v[0]
+    for j in range(1, SHARDS):
+        total = total + gains_v[j]
+    gains_out[...] = total
+
+    def last_sums(step, carry):
+        for i in range(CHUNKS):
+            n = step * CHUNKS + i
+            second_copy(n, i).wait_recv()
+            third[n] = third[n] + second[n, y if i % 2 == 0 else x]
+            result_copy(n, 1 - step, i).start()
+        return carry
+
+    lax.fori_loop(0, 2, last_sums, 0)
+
+    def finish(step, carry):
+        for i in range(CHUNKS):
+            n = step * CHUNKS + i
+            first_copy(n, i).wait_send()
+            second_copy(n, i).wait_send()
+            result_copy(n, 1 - step, i).wait()
+        return carry
+
+    lax.fori_loop(0, 2, finish, 0)
+    for i in range(CHUNKS):
+        give_copy(CHUNKS + i, i).wait_send()
+    for j in range(SHARDS):
+
+        @pl.when(me != j)
+        def _():
+            gain_copy(j, me).wait_send()
+
+
+def summed(gains, *factors):
+    rows = factors[0].shape[1]
+    anywhere = pl.BlockSpec(memory_space=pl.ANY)
+    vmem = pl.BlockSpec(memory_space=pltpu.VMEM)
+    dma = pltpu.SemaphoreType.DMA
+    total = 2 * CHUNKS
+
+    def shard(height, columns):
+        return jax.ShapeDtypeStruct((2, height, columns), BF16)
+
+    return pl.pallas_call(
+        sum_kernel,
+        out_shape=(
+            jax.ShapeDtypeStruct((8, 128), F32),
+            shard(ROWS, 3 * D),
+            shard(ROWS, D),
+            shard(ROWS, FF),
+            shard(4 * ROWS, D),
+        ),
+        in_specs=[vmem] + [anywhere] * 8,
+        out_specs=(vmem,) + (anywhere,) * 4,
+        scratch_shapes=[pltpu.VMEM((rows, f.shape[2]), BF16) for f in factors]
+        + [
+            pltpu.VMEM((CHUNKS, 2, 2, 2, ROWS, CHUNK), BF16),
+            pltpu.VMEM((total, 2, 2, ROWS, CHUNK), BF16),
+            pltpu.VMEM((total, 2, ROWS, CHUNK), BF16),
+            pltpu.VMEM((total, ROWS, CHUNK), BF16),
+            pltpu.VMEM((SHARDS, 8, 128), F32),
+            dma((8,)),
+            dma((SHARDS,)),
+            dma((SHARDS,)),
+            dma((3, total)),
+            dma((3, total)),
+            dma((total,)),
+        ],
+        compiler_params=pltpu.CompilerParams(
+            collective_id=1, has_side_effects=True, vmem_limit_bytes=60 * MIB
+        ),
+        name="sum",
+    )(gains, *factors)
+
+
 def body(
     tokens,
     gain_one,
@@ -579,21 +848,28 @@
         down_weight,
     )
 
-    def grad(a, g):
-        return jnp.einsum("lsa,lsb->lab", a, g, preferred_element_type=F32).astype(BF16)
-
-    def scattered(total):
-        return lax.psum_scatter(total, "dp", scatter_dimension=1, tiled=True).astype(F32)
-
+    replicas = lax.axis_size("dp")
+    share = D // replicas
+    if replicas == SHARDS and share == ROWS:
+        gains, g_qkv, g_out, g_up, g_down = summed(gains, u, dqkv, o, da, u2, dz, act, dm)
+        gains = gains[0:4, 0:share]
+    else:
+
+        def grad(a, g):
+            total = jnp.einsum("lsa,lsb->lab", a, g, preferred_element_type=F32).astype(BF16)
+            return lax.psum_scatter(total, "dp", scatter_dimension=1, tiled=True)
+
+        gains = lax.psum_scatter(gains[:, 0:4, 0:share], "dp", scatter_dimension=0)
+        g_qkv, g_out, g_up, g_down = grad(u, dqkv), grad(o, da), grad(u2, dz), grad(act, dm)
     return (
         fin,
         inp.astype(F32),
-        scattered(gains[0:2].astype(BF16)),
-        scattered(grad(u, dqkv)),
-        scattered(grad(o, da)),
-        scattered(gains[2:4].astype(BF16)),
-        scattered(grad(u2, dz)),
-        scattered(grad(act, dm)),
+        gains[0:2],
+        g_qkv.astype(F32),
+        g_out.astype(F32),
+        gains[2:4],
+        g_up.astype(F32),
+        g_down.astype(F32),
     )
 
 

time: 591 us -> 359 us (0.61)
  waiting for transfers between devices: 295 us -> 0 us
  Pallas kernels: 223 us -> 349 us
  matrix products: 35.8 us -> 0 us
  between operations: 14.1 us -> 0.67 us
  local copies, waits for them, and re-layouts: 9.73 us -> 2.26 us
    reduce_scatter x4 -> x0, waiting for transfers between devices: 267 us -> none  [scattered(): lax.psum_scatter(total, 'dp', scatter_dimension=1, tiled=True).astype(F32)]
    pallas_call x1 -> x2, Pallas kernels: 223 us -> 349 us  [the longest x1 223 us: relay(): pl.pallas_call(functools.partial(relay_kernel, sections, replicas, micros...]
    dot_general x4 -> x0, matrix products: 35.8 us -> none  [grad(): jnp.einsum('lsa,lsb->lab', a, g, preferred_element_type=F32).astype(BF16)]
    unnamed x8 -> x0, waiting for transfers between devices: 28.3 us -> none
    unnamed x16 -> x14, local copies, waits for them, and re-layouts: 9.72 us -> 1.69 us
  transfers between devices with their start and end apart: 6 -> 0, of which waited for: 5 -> 0; matrix products, arithmetic and copies ran while one was open for 8% -> 0% of each run, Pallas kernels for 0% -> 0%
where the time goes in v2:
time: 359 us
  Pallas kernels  349 us (97%)
  other arithmetic  6.78 us (2%)
    pallas_call x1, Pallas kernels, relay(): pl.pallas_call(functools.partial(relay_kernel, sections, replicas, micros...  223 us
    pallas_call x1, Pallas kernels, summed(): pl.pallas_call(sum_kernel, out_shape=(jax.ShapeDtypeStruct((8, 128), F32)...  126 us

profile of v2, /device:TPU:0, one launch (start us, length us, event | category | flops | bytes accessed | tf_op | source)
XLA Modules:
  0.0 359.0 jit_solution(8121518900468401520)
XLA Ops:
  0.6 223.5 %relay.1 = (bf16[512,192]{1,0:T(8,128)(2,1)}, bf16[512,192]{1,0:T(8,128)(2,1)}, f32[8,8,128]{2,1,0:T(8,128)}, bf16[2,512,768]{2,1,0:T(8,128)(2,1)}, bf16[2,512,2...) custom-call(bf16[512,768]{1,0:T(8,128)(2,1)} %tokens.1, ...), custom_call_target="tpu_custom_call" | custom-call | tf_op jit(solution)/shard_map/relay/pallas_call | solution.py:501
  224.1 125.8 %sum.1 = (f32[8,128]{1,0:T(8,128)}, bf16[2,96,2304]{2,1,0:T(8,128)(2,1)}, bf16[2,96,768]{2,1,0:T(8,128)(2,1)}, bf16[2,96,3072]{2,1,0:T(8,128)(2,1)}, bf16[2,384,768]{2,1,0:T(8,128)(2,1)}) custom-call(f32[8,8,128]{2,1,0:T(8,128)} %get-tuple-element.26.gains_in, bf16[2,512,768]{2,1,0:T(8,128)(2,1)} %get-tuple-element.27.u_in, ...), custom_call_target="tpu_custom_call" | custom-call | tf_op jit(solution)/shard_map/sum/pallas_call | solution.py:793
  349.9 0.0 copy-start
  349.9 3.0 convert_element_type.18
  353.0 0.0 copy-start.1
  353.0 0.0 copy-done
  353.0 0.0 copy-start.2
  353.0 1.6 convert_element_type.19
  354.6 0.0 copy-start.5
  354.6 0.0 copy-start.4
  354.6 0.0 copy-start.3
  354.6 0.0 copy-done.1
  354.6 1.3 convert_element_type.16
  355.9 0.0 copy-done.2
  355.9 0.9 convert_element_type.17
  356.8 0.0 copy-done.5
  356.8 0.6 fusion
  357.3 0.0 copy-done.4
  357.3 0.9 copy.19
  358.2 0.0 copy-done.3
  358.2 0.8 copy.18
Async XLA Ops:
  349.9 3.0 copy-start
  353.0 1.6 copy-start.1
  353.0 2.9 copy-start.2
  354.6 2.2 copy-start.5
  354.6 2.8 copy-start.4
  354.6 3.6 %copy-start.3 = (bf16[512,192]{1,0:T(8,128)(2,1)S(1)}, bf16[512,192]{1,0:T(8,128)(2,1)}, u32[]{:S(2)}) copy-start(bf16[512,192]{1,0:T(8,128)(2,1)} %get-tuple-element.40) | copy-start | bytes 589828

commit v3 on v2

--- a/solution.py
+++ b/solution.py
@@ -21,8 +21,9 @@
 MIB = 2**20
 CHUNK = 768
 
-PAIRS = ((0, 1, 0), (0, 2, 96), (1, 2, 64), (2, 1, 32))
-GROUP = 384
+WINDOWS = tuple(
+    (96 * j // 128, -(-(96 * j % 128 + 96) // 128), 96 * j % 128) for j in range(HEADS // 2)
+)
 
 
 def nn(a, b):
@@ -208,7 +209,7 @@
     outs = (u_out, dqkv_out, o_out, da_out, u2_out, dz_out, act_out, dm_out)
 
     def out_copy(kind, l, m):
-        slot = lax.rem(2 * m + l, 2)
+        slot = l
         src = (
             u_s.at[l, m],
             qkv_s.at[l, m],
@@ -231,7 +232,7 @@
     same = (row == column).astype(F32)
     for m in range(micros):
         parted = (jnp.full((1, SEQ), groups[m], jnp.int32) == 1).astype(F32)
-        valid = (flags[pl.ds(m, 1), :] == 1).astype(F32)
+        valid = (flags[:, m : m + 1] == 1).astype(F32)
         keep = jnp.maximum(same, 1.0 - parted) * valid
         bias[m] = (keep - 1.0) * 1e30
 
@@ -255,29 +256,26 @@
         for c in range(0, 3 * D, CHUNK):
             qkv_s[l, m, :, c : c + CHUNK] = nn(u_s[l, m], wqkv[l, :, c : c + CHUNK]).astype(BF16)
         free_slot(2, l, m)
-        slot = lax.rem(2 * m + l, 2)
+        slot = l
         added = bias[m]
-        for g in range(2):
-            tiles = [None] * 3
-            for j, (tile, count, inside) in enumerate(PAIRS):
-                lo = g * GROUP + tile * 128
-                hi = lo + count * 128
-                q = qkv_s[l, m, :, lo:hi]
-                k = two_heads(qkv_s[l, m, :, D + lo : D + hi], inside)
-                v = two_heads(qkv_s[l, m, :, 2 * D + lo : 2 * D + hi], inside)
-                s = nt(q, k) * (SCALE * LOG2E)
-                halves = []
-                for h in range(2):
-                    sh = s[:, h * SEQ : (h + 1) * SEQ] + added
-                    e = jnp.exp2(sh - jnp.max(sh, axis=-1, keepdims=True))
-                    halves.append(e * (1.0 / jnp.sum(e, axis=-1, keepdims=True)))
-                p = jnp.concatenate(halves, axis=1).astype(BF16)
-                at = (g * 4 + j) * 2 * SEQ
-                p_s[l, m, :, at : at + 2 * SEQ] = p
-                add_window(tiles, tile, nn(p, v))
-            for i in range(3):
-                at = g * GROUP + i * 128
-                o_s[slot, :, at : at + 128] = tiles[i].astype(BF16)
+        scores, tiles = [], [None] * 6
+        for tile, count, inside in WINDOWS:
+            lo, hi = tile * 128, (tile + count) * 128
+            keys = two_heads(qkv_s[l, m, :, D + lo : D + hi], inside)
+            scores.append(nt(keys, qkv_s[l, m, :, lo:hi]) * (SCALE * LOG2E))
+        for j in range(len(WINDOWS)):
+            for h in range(2):
+                s = scores[j][h * SEQ : (h + 1) * SEQ] + added
+                e = jnp.exp2(s - jnp.max(s, axis=0, keepdims=True))
+                p = e * (1.0 / jnp.sum(e, axis=0, keepdims=True))
+                p_s[l, m, 2 * j + h] = p.astype(BF16)
+        for j, (tile, count, inside) in enumerate(WINDOWS):
+            lo, hi = tile * 128, (tile + count) * 128
+            values = two_heads(qkv_s[l, m, :, 2 * D + lo : 2 * D + hi], inside)
+            p = jnp.concatenate([p_s[l, m, 2 * j], p_s[l, m, 2 * j + 1]], axis=0)
+            add_window(tiles, tile, tn(p, values))
+        for i in range(6):
+            o_s[slot, :, i * 128 : (i + 1) * 128] = tiles[i].astype(BF16)
         out_copy(2, l, m).start()
         weight_wait(1)
         h = state[...] + nn(o_s[slot], wout[l])
@@ -289,15 +287,11 @@
         weight_wait(2)
         free_slot(6, l, m)
         weight_wait(3)
-        total = state[...]
         for c in range(0, FF, CHUNK):
-            z = nn(u2_s[l, m], wup[l, :, c : c + CHUNK])
-            act, slope = gelu_parts(z)
-            act = act.astype(BF16)
-            act_s[slot, :, c : c + CHUNK] = act
+            act, slope = gelu_parts(nn(u2_s[l, m], wup[l, :, c : c + CHUNK]))
+            act_s[slot, :, c : c + CHUNK] = act.astype(BF16)
             gp_s[l, m, :, c : c + CHUNK] = slope.astype(BF16)
-            total = total + nn(act, wdown[l, c : c + CHUNK, :])
-        state[...] = total
+        state[...] = state[...] + nn(act_s[slot], wdown[l])
         out_copy(6, l, m).start()
 
     def norm_back(du, hat_scaled, gain, inverse):
@@ -315,21 +309,18 @@
         acc[at] = acc[at] + part
 
     def backward_layer(l, m):
-        slot = lax.rem(2 * m + l, 2)
+        slot = l
         dy = state[...]
         free_slot(7, l, m)
         dm_s[slot] = dy.astype(BF16)
         out_copy(7, l, m).start()
-        total = None
         for c in range(0, FF, CHUNK):
             da = nt(dm_s[slot], wdown[l, c : c + CHUNK, :])
-            dz = (gp_s[l, m, :, c : c + CHUNK].astype(F32) * da).astype(BF16)
-            gp_s[l, m, :, c : c + CHUNK] = dz
-            part = nt(dz, wup[l, :, c : c + CHUNK])
-            total = part if total is None else total + part
+            dz = gp_s[l, m, :, c : c + CHUNK].astype(F32) * da
+            gp_s[l, m, :, c : c + CHUNK] = dz.astype(BF16)
         out_copy(5, l, m).start()
         dh, weighted = norm_back(
-            total, u2_s[l, m].astype(F32), gain_two[pl.ds(l, 1), :], stat_s[l, m, :, 1:2]
+            nt(gp_s[l, m], wup[l]), u2_s[l, m].astype(F32), gain_two[pl.ds(l, 1), :], stat_s[l, m, :, 1:2]
         )
         add_rows(2 + l, weighted)
         dh = state[...] + dh
@@ -338,33 +329,33 @@
         da_s[slot] = dh.astype(BF16)
         out_copy(3, l, m).start()
         do = nt(da_s[slot], wout[l]).astype(BF16)
-        for g in range(2):
-            q_tiles, k_tiles, v_tiles = [None] * 3, [None] * 3, [None] * 3
-            for j, (tile, count, inside) in enumerate(PAIRS):
-                lo = g * GROUP + tile * 128
-                hi = lo + count * 128
-                q2 = two_heads(qkv_s[l, m, :, lo:hi], inside)
-                k2 = two_heads(qkv_s[l, m, :, D + lo : D + hi], inside)
-                v2 = two_heads(qkv_s[l, m, :, 2 * D + lo : 2 * D + hi], inside)
-                d2 = two_heads(do[:, lo:hi], inside)
-                at = (g * 4 + j) * 2 * SEQ
-                p = p_s[l, m, :, at : at + 2 * SEQ]
-                dp = nt(do[:, lo:hi], v2)
-                halves = []
-                for h in range(2):
-                    ph = p[:, h * SEQ : (h + 1) * SEQ].astype(F32)
-                    dph = dp[:, h * SEQ : (h + 1) * SEQ]
-                    inner = jnp.sum(ph * dph, axis=-1, keepdims=True)
-                    halves.append((ph * (dph - inner)).astype(BF16))
-                add_window(q_tiles, tile, nn(jnp.concatenate(halves, axis=1), k2))
-                add_window(k_tiles, tile, tn(jnp.concatenate(halves, axis=0), q2))
-                stacked = jnp.concatenate([p[:, :SEQ], p[:, SEQ:]], axis=0)
-                add_window(v_tiles, tile, tn(stacked, d2))
-            for i in range(3):
-                at = g * GROUP + i * 128
-                qkv_s[l, m, :, at : at + 128] = (q_tiles[i] * SCALE).astype(BF16)
-                qkv_s[l, m, :, D + at : D + at + 128] = (k_tiles[i] * SCALE).astype(BF16)
-                qkv_s[l, m, :, 2 * D + at : 2 * D + at + 128] = v_tiles[i].astype(BF16)
+        slopes, products = [], []
+        q_tiles, k_tiles, v_tiles = [None] * 6, [None] * 6, [None] * 6
+        for tile, count, inside in WINDOWS:
+            lo, hi = tile * 128, (tile + count) * 128
+            values = two_heads(qkv_s[l, m, :, 2 * D + lo : 2 * D + hi], inside)
+            products.append(nt(values, do[:, lo:hi]))
+        for j in range(len(WINDOWS)):
+            for h in range(2):
+                p = p_s[l, m, 2 * j + h].astype(F32)
+                dp = products[j][h * SEQ : (h + 1) * SEQ]
+                slopes.append((p * (dp - jnp.sum(p * dp, axis=0, keepdims=True))).astype(BF16))
+        for j, (tile, count, inside) in enumerate(WINDOWS):
+            lo, hi = tile * 128, (tile + count) * 128
+            pair = slopes[2 * j : 2 * j + 2]
+            keys = two_heads(qkv_s[l, m, :, D + lo : D + hi], inside)
+            query = two_heads(qkv_s[l, m, :, lo:hi], inside)
+            add_window(q_tiles, tile, tn(jnp.concatenate(pair, axis=0), keys))
+            add_window(k_tiles, tile, nn(jnp.concatenate(pair, axis=1), query))
+        for j, (tile, count, inside) in enumerate(WINDOWS):
+            given = two_heads(do[:, tile * 128 : (tile + count) * 128], inside)
+            p = jnp.concatenate([p_s[l, m, 2 * j], p_s[l, m, 2 * j + 1]], axis=1)
+            add_window(v_tiles, tile, nn(p, given))
+        for i in range(6):
+            at = i * 128
+            qkv_s[l, m, :, at : at + 128] = (q_tiles[i] * SCALE).astype(BF16)
+            qkv_s[l, m, :, D + at : D + at + 128] = (k_tiles[i] * SCALE).astype(BF16)
+            qkv_s[l, m, :, 2 * D + at : 2 * D + at + 128] = v_tiles[i].astype(BF16)
         out_copy(1, l, m).start()
         du = nt(qkv_s[l, m], wqkv[l])
         dx, weighted = norm_back(
@@ -528,7 +519,7 @@
             pltpu.VMEM((micros, sections, SEQ, width), BF16),
             saved(D),
             saved(3 * D),
-            saved(HEADS * SEQ),
+            pltpu.VMEM((2, micros, HEADS, SEQ, SEQ), BF16),
             saved(D),
             saved(FF),
             pltpu.VMEM((2, micros, SEQ, 128), F32),
@@ -838,7 +829,7 @@
     fin, inp, gains, u, dqkv, o, da, u2, dz, act, dm = relay(
         tokens,
         cotangent,
-        flags.reshape(micros, SEQ),
+        flags.reshape(micros, SEQ).T,
         groups,
         gain_one,
         gain_two,

time: 359 us -> 327 us (0.911)
  Pallas kernels: 349 us -> 316 us
    pallas_call x1, Pallas kernels: 223 us -> 190 us  [relay(): pl.pallas_call(functools.partial(relay_kernel, sections, replicas, micros...]
where the time goes in v3:
time: 327 us
  Pallas kernels  316 us (97%)
  other arithmetic  6.78 us (2%)
  local copies, waits for them, and re-layouts  3.68 us (1%)
    pallas_call x1, Pallas kernels, relay(): pl.pallas_call(functools.partial(relay_kernel, sections, replicas, micros...  190 us
    pallas_call x1, Pallas kernels, summed(): pl.pallas_call(sum_kernel, out_shape=(jax.ShapeDtypeStruct((8, 128), F32)...  126 us

profile of v3, /device:TPU:0, one launch (start us, length us, event | category | flops | bytes accessed | tf_op | source)
XLA Modules:
  0.0 327.1 jit_solution(13936359083173625695)
XLA Ops:
  0.6 1.4 copy.20
  2.0 189.6 %relay.1 = (bf16[512,192]{1,0:T(8,128)(2,1)}, bf16[512,192]{1,0:T(8,128)(2,1)}, f32[8,8,128]{2,1,0:T(8,128)}, bf16[2,512,768]{2,1,0:T(8,128)(2,1)}, bf16[2,512,2...) custom-call(bf16[512,768]{1,0:T(8,128)(2,1)} %tokens.1, ...), custom_call_target="tpu_custom_call" | custom-call | tf_op jit(solution)/shard_map/relay/pallas_call | solution.py:492
  191.6 126.4 %sum.1 = (f32[8,128]{1,0:T(8,128)}, bf16[2,96,2304]{2,1,0:T(8,128)(2,1)}, bf16[2,96,768]{2,1,0:T(8,128)(2,1)}, bf16[2,96,3072]{2,1,0:T(8,128)(2,1)}, bf16[2,384,768]{2,1,0:T(8,128)(2,1)}) custom-call(f32[8,8,128]{2,1,0:T(8,128)} %get-tuple-element.26.gains_in, bf16[2,512,768]{2,1,0:T(8,128)(2,1)} %get-tuple-element.27.u_in, ...), custom_call_target="tpu_custom_call" | custom-call | tf_op jit(solution)/shard_map/sum/pallas_call | solution.py:784
  318.0 0.0 copy-start
  318.0 3.0 convert_element_type.18
  321.1 0.0 copy-start.1
  321.1 0.0 copy-done
  321.1 0.0 copy-start.2
  321.1 1.6 convert_element_type.19
  322.6 0.0 copy-start.5
  322.6 0.0 copy-start.4
  322.7 0.0 copy-start.3
  322.7 0.0 copy-done.1
  322.7 1.3 convert_element_type.16
  324.0 0.0 copy-done.2
  324.0 0.9 convert_element_type.17
  324.8 0.0 copy-done.5
  324.8 0.6 fusion
  325.4 0.0 copy-done.4
  325.4 0.9 copy.22
  326.3 0.0 copy-done.3
  326.3 0.8 copy.21
Async XLA Ops:
  318.0 3.0 copy-start
  321.1 1.6 copy-start.1
  321.1 2.9 copy-start.2
  322.6 2.2 copy-start.5
  322.6 2.8 copy-start.4
  322.7 3.6 %copy-start.3 = (bf16[512,192]{1,0:T(8,128)(2,1)S(1)}, bf16[512,192]{1,0:T(8,128)(2,1)}, u32[]{:S(2)}) copy-start(bf16[512,192]{1,0:T(8,128)(2,1)} %get-tuple-element.48) | copy-start | bytes 589828

commit v4 on v3

--- a/solution.py
+++ b/solution.py
@@ -20,6 +20,10 @@
 SCALE = HEAD_DIM ** (-0.5)
 MIB = 2**20
 CHUNK = 768
+TILE = 256
+
+KINDS = ((0, 3), (3, 1), (4, 4), (8, 4))
+BLOCKS = 12
 
 WINDOWS = tuple(
     (96 * j // 128, -(-(96 * j % 128 + 96) // 128), 96 * j % 128) for j in range(HEADS // 2)
@@ -94,10 +98,8 @@
     dz_out,
     act_out,
     dm_out,
-    wqkv,
-    wout,
-    wup,
-    wdown,
+    turned_hbm,
+    weights,
     fwd_in,
     fwd_out,
     bwd_in,
@@ -118,6 +120,8 @@
     acc,
     bias,
     w_sem,
+    turn_sem,
+    swap_sem,
     in_sem,
     fwd_send,
     fwd_recv,
@@ -140,10 +144,49 @@
         def _():
             pl.semaphore_signal(barrier, inc=1, device_id={"pipe": j}, device_id_type=MESH)
 
-    def weight_copy(l, k):
-        src = (wqkv_hbm, wout_hbm, wup_hbm, wdown_hbm)[k]
-        dst = (wqkv, wout, wup, wdown)[k]
-        return pltpu.make_async_copy(src.at[l], dst.at[l], w_sem.at[l, k])
+    def block_rows(b, count=1):
+        start = b * D
+        return pl.ds(start if isinstance(b, int) else pl.multiple_of(start, D), count * D)
+
+    def weight_copy(l, k, j):
+        first, _ = KINDS[k]
+        if k == 1:
+            src = wout_hbm.at[l]
+        elif k == 3:
+            src = wdown_hbm.at[l, block_rows(j)]
+        else:
+            src = (wqkv_hbm, None, wup_hbm)[k].at[l, :, block_rows(j)]
+        return pltpu.make_async_copy(src, weights.at[l, block_rows(first + j)], w_sem.at[l, first + j])
+
+    def turned_copy(l, b):
+        return pltpu.make_async_copy(
+            weights.at[l, block_rows(b)], turned_hbm.at[l, block_rows(b)], turn_sem.at[l, b]
+        )
+
+    def swap_copy(l, k):
+        rows = block_rows(*KINDS[k])
+        return pltpu.make_async_copy(turned_hbm.at[l, rows], weights.at[1 - l, rows], swap_sem.at[l, k])
+
+    def turn(l, b):
+        def tile(r, c):
+            return l, pl.ds(pl.multiple_of(b * D + r * TILE, TILE), TILE), pl.ds(c * TILE, TILE)
+
+        for r in range(D // TILE):
+            weights[tile(r, r)] = weights[tile(r, r)].T
+            for c in range(r):
+                lower = weights[tile(r, c)].T
+                upper = weights[tile(c, r)].T
+                weights[tile(c, r)] = lower
+                weights[tile(r, c)] = upper
+
+    def each_block(l, action):
+        for k, (_, count) in enumerate(KINDS):
+
+            def one(j, c):
+                action(l, k, j)
+                return c
+
+            lax.fori_loop(0, count, one, 0)
 
     def token_copy(m):
         return pltpu.make_async_copy(tokens.at[pl.ds(m * SEQ, SEQ)], fwd_in.at[m], in_sem.at[0, m])
@@ -157,8 +200,9 @@
             token_copy(m).start()
 
     for l in range(2):
-        for k in range(4):
-            weight_copy(l, k).start()
+        for k, (_, count) in enumerate(KINDS):
+            for j in range(count):
+                weight_copy(l, k, j).start()
 
     @pl.when(me == last)
     def _():
@@ -232,19 +276,18 @@
     same = (row == column).astype(F32)
     for m in range(micros):
         parted = (jnp.full((1, SEQ), groups[m], jnp.int32) == 1).astype(F32)
-        valid = (flags[:, m : m + 1] == 1).astype(F32)
+        valid = jnp.broadcast_to((flags[m : m + 1, :] == 1).astype(F32), (SEQ, SEQ)).T
         keep = jnp.maximum(same, 1.0 - parted) * valid
         bias[m] = (keep - 1.0) * 1e30
 
     pl.semaphore_wait(barrier, sections - 1)
 
     def forward_layer(l, m):
-        first = m == 0
-
         def weight_wait(k):
-            @pl.when(first)
+            @pl.when((m == 0) & (me < last))
             def _():
-                weight_copy(l, k).wait()
+                for j in range(KINDS[k][1]):
+                    weight_copy(l, k, j).wait()
 
         x = state[...]
         xhat, inverse = norm_parts(x)
@@ -253,8 +296,8 @@
         u_s[l, m] = u
         out_copy(0, l, m).start()
         weight_wait(0)
-        for c in range(0, 3 * D, CHUNK):
-            qkv_s[l, m, :, c : c + CHUNK] = nn(u_s[l, m], wqkv[l, :, c : c + CHUNK]).astype(BF16)
+        for j in range(3):
+            qkv_s[l, m, :, j * D : (j + 1) * D] = nn(u_s[l, m], weights[l, block_rows(j)]).astype(BF16)
         free_slot(2, l, m)
         slot = l
         added = bias[m]
@@ -278,7 +321,7 @@
             o_s[slot, :, i * 128 : (i + 1) * 128] = tiles[i].astype(BF16)
         out_copy(2, l, m).start()
         weight_wait(1)
-        h = state[...] + nn(o_s[slot], wout[l])
+        h = state[...] + nn(o_s[slot], weights[l, block_rows(3)])
         state[...] = h
         hhat, inverse = norm_parts(h)
         stat_s[l, m, :, 1:2] = inverse
@@ -287,11 +330,11 @@
         weight_wait(2)
         free_slot(6, l, m)
         weight_wait(3)
-        for c in range(0, FF, CHUNK):
-            act, slope = gelu_parts(nn(u2_s[l, m], wup[l, :, c : c + CHUNK]))
-            act_s[slot, :, c : c + CHUNK] = act.astype(BF16)
-            gp_s[l, m, :, c : c + CHUNK] = slope.astype(BF16)
-        state[...] = state[...] + nn(act_s[slot], wdown[l])
+        for j in range(4):
+            act, slope = gelu_parts(nn(u2_s[l, m], weights[l, block_rows(4 + j)]))
+            act_s[slot, :, j * D : (j + 1) * D] = act.astype(BF16)
+            gp_s[l, m, :, j * D : (j + 1) * D] = slope.astype(BF16)
+        state[...] = state[...] + nn(act_s[slot], weights[l, block_rows(8, 4)])
         out_copy(6, l, m).start()
 
     def norm_back(du, hat_scaled, gain, inverse):
@@ -310,17 +353,26 @@
 
     def backward_layer(l, m):
         slot = l
+        held = lax.select(me == last, 1 - l, l)
+
+        def turned_wait(k):
+            @pl.when((m == 0) & (me == last))
+            def _():
+                swap_copy(l, k).wait()
+
         dy = state[...]
         free_slot(7, l, m)
+        turned_wait(3)
+        turned_wait(2)
         dm_s[slot] = dy.astype(BF16)
         out_copy(7, l, m).start()
-        for c in range(0, FF, CHUNK):
-            da = nt(dm_s[slot], wdown[l, c : c + CHUNK, :])
-            dz = gp_s[l, m, :, c : c + CHUNK].astype(F32) * da
-            gp_s[l, m, :, c : c + CHUNK] = dz.astype(BF16)
+        for j in range(4):
+            da = nn(dm_s[slot], weights[held, block_rows(8 + j)])
+            dz = gp_s[l, m, :, j * D : (j + 1) * D].astype(F32) * da
+            gp_s[l, m, :, j * D : (j + 1) * D] = dz.astype(BF16)
         out_copy(5, l, m).start()
         dh, weighted = norm_back(
-            nt(gp_s[l, m], wup[l]), u2_s[l, m].astype(F32), gain_two[pl.ds(l, 1), :], stat_s[l, m, :, 1:2]
+            nn(gp_s[l, m], weights[held, block_rows(4, 4)]), u2_s[l, m].astype(F32), gain_two[pl.ds(l, 1), :], stat_s[l, m, :, 1:2]
         )
         add_rows(2 + l, weighted)
         dh = state[...] + dh
@@ -328,7 +380,9 @@
         free_slot(3, l, m)
         da_s[slot] = dh.astype(BF16)
         out_copy(3, l, m).start()
-        do = nt(da_s[slot], wout[l]).astype(BF16)
+        turned_wait(1)
+        turned_wait(0)
+        do = nn(da_s[slot], weights[held, block_rows(3)]).astype(BF16)
         slopes, products = [], []
         q_tiles, k_tiles, v_tiles = [None] * 6, [None] * 6, [None] * 6
         for tile, count, inside in WINDOWS:
@@ -357,13 +411,36 @@
             qkv_s[l, m, :, D + at : D + at + 128] = (k_tiles[i] * SCALE).astype(BF16)
             qkv_s[l, m, :, 2 * D + at : 2 * D + at + 128] = v_tiles[i].astype(BF16)
         out_copy(1, l, m).start()
-        du = nt(qkv_s[l, m], wqkv[l])
+        du = nn(qkv_s[l, m], weights[held, block_rows(0, 3)])
         dx, weighted = norm_back(
             du, u_s[l, m].astype(F32), gain_one[pl.ds(l, 1), :], stat_s[l, m, :, 0:1]
         )
         add_rows(l, weighted)
         state[...] = state[...] + dx
 
+    @pl.when(me == last)
+    def _():
+        def make(l, k, j):
+            b = KINDS[k][0] + j
+            weight_copy(l, k, j).wait()
+            turn(l, b)
+            turned_copy(l, b).start()
+
+        def again(l, k, j):
+            turned_copy(l, KINDS[k][0] + j).wait()
+            weight_copy(l, k, j).start()
+
+        def ready(l, k, j):
+            weight_copy(l, k, j).wait()
+
+        for action in (make, again, ready):
+
+            def one(l, c):
+                each_block(l, action)
+                return c
+
+            lax.fori_loop(0, 2, one, 0)
+
     def forward_micro(m, carry):
         @pl.when(me == 0)
         def _():
@@ -377,6 +454,12 @@
 
         def one(l, c):
             forward_layer(l, m)
+
+            @pl.when((m == micros - 1) & (me == last))
+            def _():
+                for k in (3, 2, 1, 0):
+                    swap_copy(1 - l, k).start()
+
             return c
 
         lax.fori_loop(0, 2, one, 0)
@@ -393,6 +476,14 @@
         return carry
 
     lax.fori_loop(0, micros, forward_micro, 0)
+
+    @pl.when(me < last)
+    def _():
+        def one(i, c):
+            turn(1 - i // BLOCKS, lax.rem(i, BLOCKS))
+            return c
+
+        lax.fori_loop(0, 2 * BLOCKS, one, 0)
 
     acc[...] = jnp.zeros_like(acc)
 
@@ -503,14 +594,12 @@
             factor(FF),
             factor(FF),
             factor(D),
+            jax.ShapeDtypeStruct((2, BLOCKS * D, D), BF16),
         ),
         in_specs=[anywhere, anywhere, vmem, smem, vmem, vmem] + [anywhere] * 4,
-        out_specs=(anywhere, anywhere, vmem) + (anywhere,) * 8,
+        out_specs=(anywhere, anywhere, vmem) + (anywhere,) * 9,
         scratch_shapes=[
-            pltpu.VMEM((2, D, 3 * D), BF16),
-            pltpu.VMEM((2, D, D), BF16),
-            pltpu.VMEM((2, D, FF), BF16),
-            pltpu.VMEM((2, FF, D), BF16),
+            pltpu.VMEM((2, BLOCKS * D, D), BF16),
             per_micro(D),
             per_micro(D),
             per_micro(D),
@@ -530,7 +619,9 @@
             pltpu.VMEM((SEQ, D), F32),
             pltpu.VMEM((4, 8, D), F32),
             pltpu.VMEM((micros, SEQ, SEQ), F32),
-            dma((2, 4)),
+            dma((2, BLOCKS)),
+            dma((2, BLOCKS)),
+            dma((2, len(KINDS))),
             dma((2, micros)),
             dma((micros,)),
             dma((micros,)),
@@ -826,10 +917,10 @@
     groups,
 ):
     micros = tokens.shape[0] // SEQ
-    fin, inp, gains, u, dqkv, o, da, u2, dz, act, dm = relay(
+    fin, inp, gains, u, dqkv, o, da, u2, dz, act, dm, _ = relay(
         tokens,
         cotangent,
-        flags.reshape(micros, SEQ).T,
+        flags.reshape(micros, SEQ),
         groups,
         gain_one,
         gain_two,

time: 327 us -> 293 us (0.90)
  Pallas kernels: 316 us -> 280 us
    pallas_call x1, Pallas kernels: 190 us -> 154 us  [relay(): pl.pallas_call(functools.partial(relay_kernel, sections, replicas, micros...]
where the time goes in v4:
time: 293 us
  Pallas kernels  280 us (96%)
  other arithmetic  7.54 us (3%)
  local copies, waits for them, and re-layouts  4.92 us (2%)
    pallas_call x1, Pallas kernels, relay(): pl.pallas_call(functools.partial(relay_kernel, sections, replicas, micros...  154 us
    pallas_call x1, Pallas kernels, summed(): pl.pallas_call(sum_kernel, out_shape=(jax.ShapeDtypeStruct((8, 128), F32)...  125 us

profile of v4, /device:TPU:0, one launch (start us, length us, event | category | flops | bytes accessed | tf_op | source)
XLA Modules:
  0.0 292.9 jit_solution(11792024008724950634)
XLA Ops:
  0.6 154.4 %relay.1 = (bf16[512,192]{1,0:T(8,128)(2,1)}, bf16[512,192]{1,0:T(8,128)(2,1)}, f32[8,8,128]{2,1,0:T(8,128)}, bf16[2,512,768]{2,1,0:T(8,128)(2,1)}, bf16[2,512,2...) custom-call(bf16[512,768]{1,0:T(8,128)(2,1)} %tokens.1, ...), custom_call_target="tpu_custom_call" | custom-call | tf_op jit(solution)/shard_map/relay/pallas_call | solution.py:583
  155.0 1.8 copy.18
  156.8 1.8 copy.19
  158.6 125.4 %sum.1 = (f32[8,128]{1,0:T(8,128)}, bf16[2,96,2304]{2,1,0:T(8,128)(2,1)}, bf16[2,96,768]{2,1,0:T(8,128)(2,1)}, bf16[2,96,3072]{2,1,0:T(8,128)(2,1)}, bf16[2,384,768]{2,1,0:T(8,128)(2,1)}) custom-call(f32[8,8,128]{2,1,0:T(8,128)} %get-tuple-element.26.gains_in, bf16[2,512,768]{2,1,0:T(8,128)(2,1)} %get-tuple-element.27.u_in, ...), custom_call_target="tpu_custom_call" | custom-call | tf_op jit(solution)/shard_map/sum/pallas_call | solution.py:875
  284.0 0.0 copy-start.1
  284.0 1.3 fusion
  285.3 1.8 convert_element_type.17
  287.1 2.5 convert_element_type.16
  289.6 0.0 copy-done.1
  289.6 0.0 copy-start
  289.6 1.7 convert_element_type.18
  291.3 0.0 copy-done
  291.3 1.6 convert_element_type.19
Async XLA Ops:
  284.0 5.7 %copy-start.1 = (bf16[2,96,3072]{2,1,0:T(8,128)(2,1)S(1)}, bf16[2,96,3072]{2,1,0:T(8,128)(2,1)}, u32[]{:S(2)}) copy-start(bf16[2,96,3072]{2,1,0:T(8,128)(2,1)} %get-tuple-element.38) | copy-start | bytes 3538948
  289.6 1.7 copy-start

commit v5 on v4

--- a/solution.py
+++ b/solution.py
@@ -130,7 +130,6 @@
     fin_send,
     fin_recv,
     inp_send,
-    inp_recv,
     out_sem,
 ):
     me = lax.axis_index("pipe")
@@ -229,26 +228,27 @@
             device_id_type=MESH,
         )
 
-    def piece_copy(stage, out, send, recv, m, j):
+    def slots_of(m):
+        return pl.ds(pl.multiple_of(m * SEQ, SEQ), SEQ)
+
+    def fin_copy(m, j):
         return pltpu.make_async_remote_copy(
-            src_ref=stage.at[m, j],
-            dst_ref=out.at[pl.ds(m * SEQ, SEQ)],
-            send_sem=send.at[m, j],
-            recv_sem=recv.at[m],
+            src_ref=fin_stage.at[m, j],
+            dst_ref=fin_out.at[:, slots_of(m)],
+            send_sem=fin_send.at[m, j],
+            recv_sem=fin_recv.at[m],
             device_id={"pipe": j},
             device_id_type=MESH,
         )
 
-    def own_piece(stage, out, send, m, j):
-        return pltpu.make_async_copy(stage.at[m, j], out.at[pl.ds(m * SEQ, SEQ)], send.at[m, j])
-
-    def spread(stage, out, send, recv, m, source):
-        for j in range(sections):
-            stage[m, j] = state[:, j * width : (j + 1) * width].astype(BF16)
-            if j == source:
-                own_piece(stage, out, send, m, j).start()
-            else:
-                piece_copy(stage, out, send, recv, m, j).start()
+    def own_fin_copy(m):
+        return pltpu.make_async_copy(fin_stage.at[m, last], fin_out.at[:, slots_of(m)], fin_send.at[m, last])
+
+    def inp_copy(m, j):
+        return pltpu.make_async_copy(inp_stage.at[m, j], inp_out.at[j, :, slots_of(m)], inp_send.at[m, j])
+
+    def piece(j):
+        return state[:, j * width : (j + 1) * width].T.astype(BF16)
 
     outs = (u_out, dqkv_out, o_out, da_out, u2_out, dz_out, act_out, dm_out)
 
@@ -471,7 +471,12 @@
 
         @pl.when(me == last)
         def _():
-            spread(fin_stage, fin_out, fin_send, fin_recv, m, last)
+            for j in range(sections):
+                fin_stage[m, j] = piece(j)
+                if j == last:
+                    own_fin_copy(m).start()
+                else:
+                    fin_copy(m, j).start()
 
         return carry
 
@@ -511,7 +516,9 @@
 
         @pl.when(me == 0)
         def _():
-            spread(inp_stage, inp_out, inp_send, inp_recv, m, 0)
+            for j in range(sections):
+                inp_stage[m, j] = piece(j)
+                inp_copy(m, j).start()
 
         return carry
 
@@ -539,22 +546,20 @@
         def _():
             backward_copy(m).wait_send()
 
-        for source, stage, out, send, recv in (
-            (last, fin_stage, fin_out, fin_send, fin_recv),
-            (0, inp_stage, inp_out, inp_send, inp_recv),
-        ):
-
-            @pl.when(me == source)
-            def _():
-                for j in range(sections):
-                    if j == source:
-                        own_piece(stage, out, send, m, j).wait()
-                    else:
-                        piece_copy(stage, out, send, recv, m, j).wait_send()
-
-            @pl.when(me != source)
-            def _():
-                piece_copy(stage, out, send, recv, m, source).wait_recv()
+        @pl.when(me == last)
+        def _():
+            for j in range(last):
+                fin_copy(m, j).wait_send()
+            own_fin_copy(m).wait()
+
+        @pl.when(me < last)
+        def _():
+            fin_copy(m, last).wait_recv()
+
+        @pl.when(me == 0)
+        def _():
+            for j in range(sections):
+                inp_copy(m, j).wait()
 
 
 def relay(tokens, cotangent, flags, groups, gain_one, gain_two, wqkv, wout, wup, wdown):
@@ -583,8 +588,8 @@
     return pl.pallas_call(
         functools.partial(relay_kernel, sections, replicas, micros),
         out_shape=(
-            jax.ShapeDtypeStruct((rows, width), BF16),
-            jax.ShapeDtypeStruct((rows, width), BF16),
+            jax.ShapeDtypeStruct((width, rows), BF16),
+            jax.ShapeDtypeStruct((sections, width, rows), BF16),
             jax.ShapeDtypeStruct((replicas, 8, 128), F32),
             factor(D),
             factor(3 * D),
@@ -604,8 +609,8 @@
             per_micro(D),
             per_micro(D),
             per_micro(D),
-            pltpu.VMEM((micros, sections, SEQ, width), BF16),
-            pltpu.VMEM((micros, sections, SEQ, width), BF16),
+            pltpu.VMEM((micros, sections, width, SEQ), BF16),
+            pltpu.VMEM((micros, sections, width, SEQ), BF16),
             saved(D),
             saved(3 * D),
             pltpu.VMEM((2, micros, HEADS, SEQ, SEQ), BF16),
@@ -630,7 +635,6 @@
             dma((micros, sections)),
             dma((micros,)),
             dma((micros, sections)),
-            dma((micros,)),
             dma((8, 2, micros)),
         ],
         compiler_params=pltpu.CompilerParams(
@@ -646,7 +650,9 @@
 
 
 def sum_kernel(
+    sections,
     gains_in,
+    inp_in,
     u_in,
     dqkv_in,
     o_in,
@@ -656,6 +662,7 @@
     act_in,
     dm_in,
     gains_out,
+    inp_out,
     qkv_out,
     out_out,
     up_out,
@@ -676,11 +683,14 @@
     load_sem,
     gain_send,
     gain_recv,
+    inp_send,
+    inp_recv,
     send,
     recv,
     out_sem,
 ):
     me = lax.axis_index("dp")
+    section = lax.axis_index("pipe")
     core = lax.rem(me, 2)
     x = lax.rem(me // 2, 2)
     y = me // 4
@@ -695,6 +705,10 @@
         def _():
             pl.semaphore_signal(barrier, inc=1, device_id={"dp": j}, device_id_type=MESH)
 
+    @pl.when(section > 0)
+    def _():
+        pl.semaphore_signal(barrier, inc=1, device_id={"pipe": 0}, device_id_type=MESH)
+
     sources = (u_in, dqkv_in, o_in, da_in, u2_in, dz_in, act_in, dm_in)
     held = (u_v, dqkv_v, o_v, da_v, u2_v, dz_v, act_v, dm_v)
 
@@ -703,8 +717,6 @@
 
     for k in range(8):
         load(k, 1).start()
-
-    pl.semaphore_wait(barrier, SHARDS - 1)
 
     def gain_copy(j, source):
         return pltpu.make_async_remote_copy(
@@ -716,11 +728,32 @@
             device_id_type=MESH,
         )
 
-    for j in range(SHARDS):
-
-        @pl.when(me != j)
-        def _():
-            gain_copy(j, me).start()
+    def inp_copy(j):
+        return pltpu.make_async_remote_copy(
+            src_ref=inp_in.at[j],
+            dst_ref=inp_out,
+            send_sem=inp_send.at[j],
+            recv_sem=inp_recv,
+            device_id={"pipe": j},
+            device_id_type=MESH,
+        )
+
+    def own_inp_copy():
+        return pltpu.make_async_copy(inp_in.at[0], inp_out, inp_send.at[0])
+
+    def meet():
+        pl.semaphore_wait(barrier, SHARDS - 1 + lax.select(section == 0, sections - 1, 0))
+        for j in range(SHARDS):
+
+            @pl.when(me != j)
+            def _():
+                gain_copy(j, me).start()
+
+        @pl.when(section == 0)
+        def _():
+            own_inp_copy().start()
+            for j in range(1, sections):
+                inp_copy(j).start()
 
     def remote(src, dst, step, n, to):
         return pltpu.make_async_remote_copy(
@@ -778,6 +811,8 @@
                 part = tn(a[...], g[:, columns * CHUNK : (columns + 1) * CHUNK]).astype(BF16)
                 for r in range(SHARDS):
                     own[i, r % 2, r // 4, (r // 2) % 2] = part[r * ROWS : (r + 1) * ROWS]
+                if i == 0:
+                    pl.when(step == 0)(meet)
                 give_copy(base + i, i).start()
                 if i > 0:
                     add_core(base + i - 1, i - 1)
@@ -861,9 +896,19 @@
         def _():
             gain_copy(j, me).wait_send()
 
-
-def summed(gains, *factors):
-    rows = factors[0].shape[1]
+    @pl.when(section == 0)
+    def _():
+        own_inp_copy().wait()
+        for j in range(1, sections):
+            inp_copy(j).wait_send()
+
+    @pl.when(section > 0)
+    def _():
+        inp_copy(0).wait_recv()
+
+
+def summed(gains, inp, *factors):
+    sections, width, rows = inp.shape
     anywhere = pl.BlockSpec(memory_space=pl.ANY)
     vmem = pl.BlockSpec(memory_space=pltpu.VMEM)
     dma = pltpu.SemaphoreType.DMA
@@ -873,16 +918,17 @@
         return jax.ShapeDtypeStruct((2, height, columns), BF16)
 
     return pl.pallas_call(
-        sum_kernel,
+        functools.partial(sum_kernel, sections),
         out_shape=(
             jax.ShapeDtypeStruct((8, 128), F32),
+            jax.ShapeDtypeStruct((width, rows), BF16),
             shard(ROWS, 3 * D),
             shard(ROWS, D),
             shard(ROWS, FF),
             shard(4 * ROWS, D),
         ),
-        in_specs=[vmem] + [anywhere] * 8,
-        out_specs=(vmem,) + (anywhere,) * 4,
+        in_specs=[vmem] + [anywhere] * 9,
+        out_specs=(vmem,) + (anywhere,) * 5,
         scratch_shapes=[pltpu.VMEM((rows, f.shape[2]), BF16) for f in factors]
         + [
             pltpu.VMEM((CHUNKS, 2, 2, 2, ROWS, CHUNK), BF16),
@@ -893,6 +939,8 @@
             dma((8,)),
             dma((SHARDS,)),
             dma((SHARDS,)),
+            dma((sections,)),
+            dma(()),
             dma((3, total)),
             dma((3, total)),
             dma((total,)),
@@ -901,7 +949,48 @@
             collective_id=1, has_side_effects=True, vmem_limit_bytes=60 * MIB
         ),
         name="sum",
-    )(gains, *factors)
+    )(gains, inp, *factors)
+
+
+def write_kernel(count, share, gains, *refs):
+    gain_one, gain_two = refs[count], refs[count + 1]
+    gain_one[...] = gains[0:2, 0:share]
+    gain_two[...] = gains[2:4, 0:share]
+    sources, results, held, wide = (
+        refs[:count],
+        refs[count + 2 : 2 * count + 2],
+        refs[2 * count + 2 : 3 * count + 2],
+        refs[3 * count + 2 : 4 * count + 2],
+    )
+    load_sem, store_sem = refs[4 * count + 2 :]
+    loads = [pltpu.make_async_copy(sources[k], held[k], load_sem.at[k]) for k in range(count)]
+    stores = [pltpu.make_async_copy(wide[k], results[k], store_sem.at[k]) for k in range(count)]
+    for load in loads:
+        load.start()
+    for k in range(count):
+        loads[k].wait()
+        wide[k][...] = held[k][...].astype(wide[k].dtype)
+        stores[k].start()
+    for store in stores:
+        store.wait()
+
+
+def written(gains, share, arrays, types):
+    count = len(arrays)
+    anywhere = pl.BlockSpec(memory_space=pl.ANY)
+    vmem = pl.BlockSpec(memory_space=pltpu.VMEM)
+    return pl.pallas_call(
+        functools.partial(write_kernel, count, share),
+        out_shape=(jax.ShapeDtypeStruct((2, share), F32),) * 2
+        + tuple(jax.ShapeDtypeStruct(a.shape, t) for a, t in zip(arrays, types)),
+        in_specs=[vmem] + [anywhere] * count,
+        out_specs=(vmem, vmem) + (anywhere,) * count,
+        scratch_shapes=[pltpu.VMEM(a.shape, a.dtype) for a in arrays]
+        + [pltpu.VMEM(a.shape, t) for a, t in zip(arrays, types)]
+        + [pltpu.SemaphoreType.DMA((count,)), pltpu.SemaphoreType.DMA((count,))],
+        compiler_params=pltpu.CompilerParams(vmem_limit_bytes=60 * MIB),
+        name="write",
+    )(gains, *arrays)
 
 
 def body(
@@ -933,26 +1022,21 @@
     replicas = lax.axis_size("dp")
     share = D // replicas
     if replicas == SHARDS and share == ROWS:
-        gains, g_qkv, g_out, g_up, g_down = summed(gains, u, dqkv, o, da, u2, dz, act, dm)
-        gains = gains[0:4, 0:share]
+        gains, inp, g_qkv, g_out, g_up, g_down = summed(gains, inp, u, dqkv, o, da, u2, dz, act, dm)
     else:
 
         def grad(a, g):
             total = jnp.einsum("lsa,lsb->lab", a, g, preferred_element_type=F32).astype(BF16)
             return lax.psum_scatter(total, "dp", scatter_dimension=1, tiled=True)
 
-        gains = lax.psum_scatter(gains[:, 0:4, 0:share], "dp", scatter_dimension=0)
+        gains = lax.psum_scatter(gains, "dp", scatter_dimension=0)
+        inp = jnp.where(lax.axis_index("pipe") == 0, inp, jnp.zeros_like(inp))
+        inp = lax.psum_scatter(inp, "pipe", scatter_dimension=0)
         g_qkv, g_out, g_up, g_down = grad(u, dqkv), grad(o, da), grad(u2, dz), grad(act, dm)
-    return (
-        fin,
-        inp.astype(F32),
-        gains[0:2],
-        g_qkv.astype(F32),
-        g_out.astype(F32),
-        gains[2:4],
-        g_up.astype(F32),
-        g_down.astype(F32),
+    gain_one_grad, gain_two_grad, fin, inp, g_qkv, g_out, g_up, g_down = written(
+        gains, share, (fin, inp, g_qkv, g_out, g_up, g_down), (BF16,) + (F32,) * 5
     )
+    return (fin.T, inp.T, gain_one_grad, g_qkv, g_out, gain_two_grad, g_up, g_down)
 
 
 def solution(mesh):

time: 293 us -> 285 us (0.973)
  other arithmetic: 7.54 us -> 0 us
  local copies, waits for them, and re-layouts: 4.92 us -> 0 us
  Pallas kernels: 280 us -> 284 us
    convert_element_type x4 -> x0, other arithmetic: 7.54 us -> none  [the longest x1 2.49 us: body(): g_qkv.astype(F32)]
    pallas_call x1 -> x2, Pallas kernels: 125 us -> 131 us  [the longest x1 125 us: summed(): pl.pallas_call(functools.partial(sum_kernel, sections), out_shape=(jax.Sh...]
    unnamed x6 -> x0, local copies, waits for them, and re-layouts: 3.58 us -> none
where the time goes in v5:
time: 285 us; the launch traced here: 284 us
  Pallas kernels  284 us (100%)
    pallas_call x1, Pallas kernels, relay(): pl.pallas_call(functools.partial(relay_kernel, sections, replicas, micros...  153 us
    pallas_call x1, Pallas kernels, summed(): pl.pallas_call(functools.partial(sum_kernel, sections), out_shape=(jax.Sh...  125 us
    pallas_call x1, Pallas kernels, written(): pl.pallas_call(functools.partial(write_kernel, count, share), out_shape=(...  5.8 us

profile of v5, /device:TPU:0, one launch (start us, length us, event | category | flops | bytes accessed | tf_op | source)
XLA Modules:
  0.0 284.5 jit_solution(5384425038698527077)
XLA Ops:
  0.6 152.8 %relay.1 = (bf16[192,512]{1,0:T(8,128)(2,1)}, bf16[4,192,512]{2,1,0:T(8,128)(2,1)}, f32[8,8,128]{2,1,0:T(8,128)}, bf16[2,512,768]{2,1,0:T(8,128)(2,1)}, bf16[2,5...) custom-call(bf16[512,768]{1,0:T(8,128)(2,1)} %tokens.1, ...), custom_call_target="tpu_custom_call" | custom-call | tf_op jit(solution)/shard_map/relay/pallas_call | solution.py:588
  153.5 125.0 %sum.1 = (f32[8,128]{1,0:T(8,128)}, bf16[192,512]{1,0:T(8,128)(2,1)}, bf16[2,96,2304]{2,1,0:T(8,128)(2,1)}, bf16[2,96,768]{2,1,0:T(8,128)(2,1)}, bf16[2,96,3072]...) custom-call(f32[8,8,128]{2,1,0:T(8,128)} %get-tuple-element.33.gains_in, bf16[4,192,512]{2,1,0:T(8,128)(2,1)} %get-tuple-element.34.inp_in, ...), custom_call_target="tpu_custom_call" | custom-call | tf_op jit(solution)/shard_map/sum/pallas_call | solution.py:920
  278.5 5.8 %write.1 = (f32[2,96]{1,0:T(2,128)}, f32[2,96]{1,0:T(2,128)}, bf16[192,512]{1,0:T(8,128)(2,1)}, f32[192,512]{1,0:T(8,128)}, f32[2,96,2304]{2,1,0:T(8,128)}, /*in...) custom-call(f32[8,128]{1,0:T(8,128)} %get-tuple-element.43.gains, ...), custom_call_target="tpu_custom_call" | custom-call | tf_op jit(solution)/shard_map/write/pallas_call | solution.py:982

commit v6 on v5

--- a/solution.py
+++ b/solution.py
@@ -24,6 +24,7 @@
 
 KINDS = ((0, 3), (3, 1), (4, 4), (8, 4))
 BLOCKS = 12
+SHARDS = 8
 
 WINDOWS = tuple(
     (96 * j // 128, -(-(96 * j % 128 + 96) // 128), 96 * j % 128) for j in range(HEADS // 2)
@@ -77,6 +78,7 @@
     sections,
     replicas,
     micros,
+    paired,
     tokens,
     cotangent,
     flags,
@@ -98,6 +100,8 @@
     dz_out,
     act_out,
     dm_out,
+    act_other,
+    dm_other,
     turned_hbm,
     weights,
     fwd_in,
@@ -131,6 +135,10 @@
     fin_recv,
     inp_send,
     out_sem,
+    act_send,
+    act_recv,
+    dm_send,
+    dm_recv,
 ):
     me = lax.axis_index("pipe")
     last = sections - 1
@@ -142,6 +150,12 @@
         @pl.when(me != j)
         def _():
             pl.semaphore_signal(barrier, inc=1, device_id={"pipe": j}, device_id_type=MESH)
+
+    replica = lax.axis_index("dp")
+    x, y = lax.rem(replica // 2, 2), replica // 4
+    if paired:
+        for j in (replica + 2 - 4 * x, replica + 4 - 8 * y):
+            pl.semaphore_signal(barrier, inc=1, device_id={"dp": j}, device_id_type=MESH)
 
     def block_rows(b, count=1):
         start = b * D
@@ -262,14 +276,45 @@
             u2_s.at[l, m],
             gp_s.at[l, m],
             act_s.at[slot],
-            dm_s.at[slot],
+            dm_s.at[l, m],
         )[kind]
         return pltpu.make_async_copy(src, outs[kind].at[l, pl.ds(m * SEQ, SEQ)], out_sem.at[kind, l, m])
 
+    def partner(l):
+        return {"dp": lax.select(l == 1, replica + 2 - 4 * x, replica + 4 - 8 * y)}
+
+    def act_copy(l, m, b):
+        block = l * (2 * b + 1 - x) + (1 - l) * (2 * (1 - y) + b)
+        return pltpu.make_async_remote_copy(
+            src_ref=act_out.at[l, slots_of(m), block_rows(block)],
+            dst_ref=act_other.at[l, slots_of(m), pl.ds(b * D, D)],
+            send_sem=act_send.at[l, m, b],
+            recv_sem=act_recv.at[l, m, b],
+            device_id=partner(l),
+            device_id_type=MESH,
+        )
+
+    def act_start(l, m):
+        if paired:
+            for b in range(2):
+                act_copy(l, m, b).start()
+
+    def dm_copy(l, m):
+        return pltpu.make_async_remote_copy(
+            src_ref=dm_s.at[l, m],
+            dst_ref=dm_other.at[l, slots_of(m)],
+            send_sem=dm_send.at[l, m],
+            recv_sem=dm_recv.at[l, m],
+            device_id=partner(l),
+            device_id_type=MESH,
+        )
+
     def free_slot(kind, l, m):
         @pl.when(m > 0)
         def _():
             out_copy(kind, l, m - 1).wait()
+            if kind == 6:
+                act_start(l, m - 1)
 
     row = lax.broadcasted_iota(jnp.int32, (SEQ, SEQ), 0) // (SEQ // 4)
     column = lax.broadcasted_iota(jnp.int32, (SEQ, SEQ), 1) // (SEQ // 4)
@@ -280,7 +325,7 @@
         keep = jnp.maximum(same, 1.0 - parted) * valid
         bias[m] = (keep - 1.0) * 1e30
 
-    pl.semaphore_wait(barrier, sections - 1)
+    pl.semaphore_wait(barrier, sections - 1 + 2 * paired)
 
     def forward_layer(l, m):
         def weight_wait(k):
@@ -361,13 +406,14 @@
                 swap_copy(l, k).wait()
 
         dy = state[...]
-        free_slot(7, l, m)
         turned_wait(3)
         turned_wait(2)
-        dm_s[slot] = dy.astype(BF16)
+        dm_s[l, m] = dy.astype(BF16)
         out_copy(7, l, m).start()
+        if paired:
+            dm_copy(l, m).start()
         for j in range(4):
-            da = nn(dm_s[slot], weights[held, block_rows(8 + j)])
+            da = nn(dm_s[l, m], weights[held, block_rows(8 + j)])
             dz = gp_s[l, m, :, j * D : (j + 1) * D].astype(F32) * da
             gp_s[l, m, :, j * D : (j + 1) * D] = dz.astype(BF16)
         out_copy(5, l, m).start()
@@ -481,6 +527,9 @@
         return carry
 
     lax.fori_loop(0, micros, forward_micro, 0)
+    for l in range(2):
+        out_copy(6, l, micros - 1).wait()
+        act_start(l, micros - 1)
 
     @pl.when(me < last)
     def _():
@@ -531,11 +580,15 @@
             gains_out[r, k : k + 1, 0:share] = total[:, r * share : (r + 1) * share]
 
     for l in range(2):
-        for kind in (2, 3, 6, 7):
+        for kind in (2, 3):
             out_copy(kind, l, micros - 1).wait()
         for m in range(micros):
-            for kind in (0, 1, 4, 5):
+            for kind in (0, 1, 4, 5, 7):
                 out_copy(kind, l, m).wait()
+            if paired:
+                for b in range(2):
+                    act_copy(l, m, b).wait()
+                dm_copy(l, m).wait()
     for m in range(micros):
 
         @pl.when(me < last)
@@ -568,6 +621,7 @@
     rows = tokens.shape[0]
     micros = rows // SEQ
     width = D // sections
+    paired = replicas == SHARDS
     anywhere = pl.BlockSpec(memory_space=pl.ANY)
     vmem = pl.BlockSpec(memory_space=pltpu.VMEM)
     smem = pl.BlockSpec(memory_space=pltpu.SMEM)
@@ -586,7 +640,7 @@
         return pltpu.VMEM((micros, SEQ, columns), BF16)
 
     return pl.pallas_call(
-        functools.partial(relay_kernel, sections, replicas, micros),
+        functools.partial(relay_kernel, sections, replicas, micros, paired),
         out_shape=(
             jax.ShapeDtypeStruct((width, rows), BF16),
             jax.ShapeDtypeStruct((sections, width, rows), BF16),
@@ -599,10 +653,12 @@
             factor(FF),
             factor(FF),
             factor(D),
+            factor(2 * D),
+            factor(D),
             jax.ShapeDtypeStruct((2, BLOCKS * D, D), BF16),
         ),
         in_specs=[anywhere, anywhere, vmem, smem, vmem, vmem] + [anywhere] * 4,
-        out_specs=(anywhere, anywhere, vmem) + (anywhere,) * 9,
+        out_specs=(anywhere, anywhere, vmem) + (anywhere,) * 11,
         scratch_shapes=[
             pltpu.VMEM((2, BLOCKS * D, D), BF16),
             per_micro(D),
@@ -619,7 +675,7 @@
             pltpu.VMEM((2, micros, SEQ, 128), F32),
             two(D),
             two(FF),
-            two(D),
+            saved(D),
             two(D),
             pltpu.VMEM((SEQ, D), F32),
             pltpu.VMEM((4, 8, D), F32),
@@ -636,6 +692,10 @@
             dma((micros,)),
             dma((micros, sections)),
             dma((8, 2, micros)),
+            dma((2, micros, 2)),
+            dma((2, micros, 2)),
+            dma((2, micros)),
+            dma((2, micros)),
         ],
         compiler_params=pltpu.CompilerParams(
             collective_id=0, has_side_effects=True, vmem_limit_bytes=60 * MIB
@@ -644,7 +704,6 @@
     )(tokens, cotangent, flags, groups, gain_one, gain_two, wqkv, wout, wup, wdown)
 
 
-SHARDS = 8
 ROWS = 96
 CHUNKS = 12
 
@@ -661,6 +720,8 @@
     dz_in,
     act_in,
     dm_in,
+    act_other,
+    dm_other,
     gains_out,
     inp_out,
     qkv_out,
@@ -709,14 +770,26 @@
     def _():
         pl.semaphore_signal(barrier, inc=1, device_id={"pipe": 0}, device_id_type=MESH)
 
-    sources = (u_in, dqkv_in, o_in, da_in, u2_in, dz_in, act_in, dm_in)
-    held = (u_v, dqkv_v, o_v, da_v, u2_v, dz_v, act_v, dm_v)
+    sources = (u_in, dqkv_in, o_in, da_in, u2_in, dz_in)
+    held = (u_v, dqkv_v, o_v, da_v, u2_v, dz_v)
+    rows = dm_in.shape[1]
 
     def load(k, l):
         return pltpu.make_async_copy(sources[k].at[l], held[k], load_sem.at[k])
 
-    for k in range(8):
+    def down_loads(l):
+        copies = [(dm_in.at[l], dm_v.at[0:rows]), (dm_other.at[l], dm_v.at[rows : 2 * rows])]
+        for b in range(2):
+            block = l * (2 * b + x) + (1 - l) * (2 * y + b)
+            columns = pl.ds(pl.multiple_of(block * CHUNK, CHUNK), CHUNK)
+            copies.append((act_in.at[l, :, columns], act_v.at[b, 0:rows]))
+            copies.append((act_other.at[l, :, pl.ds(b * CHUNK, CHUNK)], act_v.at[b, rows : 2 * rows]))
+        return [pltpu.make_async_copy(src, dst, load_sem.at[6 + k]) for k, (src, dst) in enumerate(copies)]
+
+    for k in range(6):
         load(k, 1).start()
+    for copy in down_loads(1):
+        copy.start()
 
     def gain_copy(j, source):
         return pltpu.make_async_remote_copy(
@@ -766,7 +839,13 @@
         )
 
     def give_copy(n, i):
+        if i >= 8:
+            return remote(own.at[i, 1 - core, 0], first.at[n, 0], 0, n, other_core)
         return remote(own.at[i, 1 - core], first.at[n], 0, n, other_core)
+
+    def down_copy(n, l):
+        mine, to = lax.select(l == 1, y, x), lax.select(l == 1, other_y, other_x)
+        return remote(first.at[n, 0, 1 - mine], third.at[n], 2, n, to)
 
     def first_copy(n, i):
         if i % 2 == 0:
@@ -789,10 +868,14 @@
             dst = down_out.at[l, pl.ds((i - 8) * ROWS, ROWS)]
         return pltpu.make_async_copy(third.at[n], dst, out_sem.at[n])
 
-    def add_core(n, i):
+    def add_core(n, l, i):
         give_copy(n, i).wait_recv()
-        first[n] = first[n] + own[i, core]
-        first_copy(n, i).start()
+        if i >= 8:
+            first[n, 0] = first[n, 0] + own[i, core, 0]
+            down_copy(n, l).start()
+        else:
+            first[n] = first[n] + own[i, core]
+            first_copy(n, i).start()
 
     def layer_products(step, carry):
         l = 1 - step
@@ -815,7 +898,7 @@
                     pl.when(step == 0)(meet)
                 give_copy(base + i, i).start()
                 if i > 0:
-                    add_core(base + i - 1, i - 1)
+                    add_core(base + i - 1, l, i - 1)
 
         def reload(k):
             @pl.when(step == 0)
@@ -829,25 +912,30 @@
         reload(2)
         products(4, u2_v, dz_v, ((4, 0), (5, 1), (6, 2), (7, 3)))
         reload(4)
-        load(6, l).wait()
-        load(7, l).wait()
+        for copy in down_loads(l):
+            copy.wait()
         for i in range(8, CHUNKS):
             free(i)
-        for b in range(4):
-            part = tn(act_v[:, b * CHUNK : (b + 1) * CHUNK], dm_v[...]).astype(BF16)
+        for b in range(2):
+            part = tn(act_v[b], dm_v[...]).astype(BF16)
             for r in range(8):
-                own[8 + r % 4, r // 4, b // 2, b % 2] = part[r * ROWS : (r + 1) * ROWS]
-        reload(6)
+                own[8 + r % 4, r // 4, 0, b] = part[r * ROWS : (r + 1) * ROWS]
+
+        @pl.when(step == 0)
+        def _():
+            for copy in down_loads(0):
+                copy.start()
+
         for i in range(8, CHUNKS):
             give_copy(base + i, i).start()
         for i in range(7, CHUNKS):
-            add_core(base + i, i)
+            add_core(base + i, l, i)
         return carry
 
     lax.fori_loop(0, 2, layer_products, 0)
 
     def second_sums(step, carry):
-        for i in range(CHUNKS):
+        for i in range(8):
             n = step * CHUNKS + i
             first_copy(n, i).wait_recv()
             kept = first[n, :, x] if i % 2 == 0 else first[n, y]
@@ -872,8 +960,12 @@
     def last_sums(step, carry):
         for i in range(CHUNKS):
             n = step * CHUNKS + i
-            second_copy(n, i).wait_recv()
-            third[n] = third[n] + second[n, y if i % 2 == 0 else x]
+            if i >= 8:
+                down_copy(n, 1 - step).wait_recv()
+                third[n] = third[n] + first[n, 0, lax.select(step == 0, y, x)]
+            else:
+                second_copy(n, i).wait_recv()
+                third[n] = third[n] + second[n, y if i % 2 == 0 else x]
             result_copy(n, 1 - step, i).start()
         return carry
 
@@ -882,8 +974,11 @@
     def finish(step, carry):
         for i in range(CHUNKS):
             n = step * CHUNKS + i
-            first_copy(n, i).wait_send()
-            second_copy(n, i).wait_send()
+            if i >= 8:
+                down_copy(n, 1 - step).wait_send()
+            else:
+                first_copy(n, i).wait_send()
+                second_copy(n, i).wait_send()
             result_copy(n, 1 - step, i).wait()
         return carry
 
@@ -927,16 +1022,18 @@
             shard(ROWS, FF),
             shard(4 * ROWS, D),
         ),
-        in_specs=[vmem] + [anywhere] * 9,
+        in_specs=[vmem] + [anywhere] * 11,
         out_specs=(vmem,) + (anywhere,) * 5,
-        scratch_shapes=[pltpu.VMEM((rows, f.shape[2]), BF16) for f in factors]
+        scratch_shapes=[pltpu.VMEM((rows, f.shape[2]), BF16) for f in factors[:6]]
         + [
+            pltpu.VMEM((2, 2 * rows, CHUNK), BF16),
+            pltpu.VMEM((2 * rows, D), BF16),
             pltpu.VMEM((CHUNKS, 2, 2, 2, ROWS, CHUNK), BF16),
             pltpu.VMEM((total, 2, 2, ROWS, CHUNK), BF16),
             pltpu.VMEM((total, 2, ROWS, CHUNK), BF16),
             pltpu.VMEM((total, ROWS, CHUNK), BF16),
             pltpu.VMEM((SHARDS, 8, 128), F32),
-            dma((8,)),
+            dma((12,)),
             dma((SHARDS,)),
             dma((SHARDS,)),
             dma((sections,)),
@@ -1006,7 +1103,7 @@
     groups,
 ):
     micros = tokens.shape[0] // SEQ
-    fin, inp, gains, u, dqkv, o, da, u2, dz, act, dm, _ = relay(
+    fin, inp, gains, u, dqkv, o, da, u2, dz, act, dm, act_other, dm_other, _ = relay(
         tokens,
         cotangent,
         flags.reshape(micros, SEQ),
@@ -1022,7 +1119,9 @@
     replicas = lax.axis_size("dp")
     share = D // replicas
     if replicas == SHARDS and share == ROWS:
-        gains, inp, g_qkv, g_out, g_up, g_down = summed(gains, inp, u, dqkv, o, da, u2, dz, act, dm)
+        gains, inp, g_qkv, g_out, g_up, g_down = summed(
+            gains, inp, u, dqkv, o, da, u2, dz, act, dm, act_other, dm_other
+        )
     else:
 
         def grad(a, g):

time: 285 us -> 261 us (0.916)
  Pallas kernels: 284 us -> 260 us
    pallas_call x1, Pallas kernels: 125 us -> 100 us  [summed(): pl.pallas_call(functools.partial(sum_kernel, sections), out_shape=(jax.Sh...]
where the time goes in v6:
time: 261 us
  Pallas kernels  260 us (100%)
    pallas_call x1, Pallas kernels, relay(): pl.pallas_call(functools.partial(relay_kernel, sections, replicas, micros...  154 us
    pallas_call x1, Pallas kernels, summed(): pl.pallas_call(functools.partial(sum_kernel, sections), out_shape=(jax.Sh...  100 us
    pallas_call x1, Pallas kernels, written(): pl.pallas_call(functools.partial(write_kernel, count, share), out_shape=(...  5.8 us

profile of v6, /device:TPU:0, one launch (start us, length us, event | category | flops | bytes accessed | tf_op | source)
XLA Modules:
  0.0 261.0 jit_solution(15154720149463800172)
XLA Ops:
  0.6 154.3 %relay.1 = (bf16[192,512]{1,0:T(8,128)(2,1)}, bf16[4,192,512]{2,1,0:T(8,128)(2,1)}, f32[8,8,128]{2,1,0:T(8,128)}, bf16[2,512,768]{2,1,0:T(8,128)(2,1)}, bf16[2,5...) custom-call(bf16[512,768]{1,0:T(8,128)(2,1)} %tokens.1, ...), custom_call_target="tpu_custom_call" | custom-call | tf_op jit(solution)/shard_map/relay/pallas_call | solution.py:642
  155.0 100.1 %sum.1 = (f32[8,128]{1,0:T(8,128)}, bf16[192,512]{1,0:T(8,128)(2,1)}, bf16[2,96,2304]{2,1,0:T(8,128)(2,1)}, bf16[2,96,768]{2,1,0:T(8,128)(2,1)}, bf16[2,96,3072]...) custom-call(f32[8,8,128]{2,1,0:T(8,128)} %get-tuple-element.35.gains_in, bf16[4,192,512]{2,1,0:T(8,128)(2,1)} %get-tuple-element.36.inp_in, ...), custom_call_target="tpu_custom_call" | custom-call | tf_op jit(solution)/shard_map/sum/pallas_call | solution.py:1015
  255.0 5.8 %write.1 = (f32[2,96]{1,0:T(2,128)}, f32[2,96]{1,0:T(2,128)}, bf16[192,512]{1,0:T(8,128)(2,1)}, f32[192,512]{1,0:T(8,128)}, f32[2,96,2304]{2,1,0:T(8,128)}, /*in...) custom-call(f32[8,128]{1,0:T(8,128)} %get-tuple-element.47.gains, ...), custom_call_target="tpu_custom_call" | custom-call | tf_op jit(solution)/shard_map/write/pallas_call | solution.py:1079

commit v7 on v6

--- a/solution.py
+++ b/solution.py
@@ -24,6 +24,14 @@
 
 KINDS = ((0, 3), (3, 1), (4, 4), (8, 4))
 BLOCKS = 12
+
+FIN_WINDOW = 256
+
+
+def window_start(section, width):
+    return min(section * width // 128 * 128, D - FIN_WINDOW)
+
+
 SHARDS = 8
 
 WINDOWS = tuple(
@@ -108,8 +116,6 @@
     fwd_out,
     bwd_in,
     bwd_out,
-    fin_stage,
-    inp_stage,
     u_s,
     qkv_s,
     p_s,
@@ -212,10 +218,17 @@
         for m in range(micros):
             token_copy(m).start()
 
-    for l in range(2):
+    def weights_start(l):
         for k, (_, count) in enumerate(KINDS):
             for j in range(count):
                 weight_copy(l, k, j).start()
+
+    weights_start(0)
+
+    @pl.when(me > 0)
+    def _():
+        weights_start(1)
+
 
     @pl.when(me == last)
     def _():
@@ -245,10 +258,13 @@
     def slots_of(m):
         return pl.ds(pl.multiple_of(m * SEQ, SEQ), SEQ)
 
+    def fin_source(m, j):
+        return fwd_out.at[m, :, pl.ds(window_start(j, width), FIN_WINDOW)]
+
     def fin_copy(m, j):
         return pltpu.make_async_remote_copy(
-            src_ref=fin_stage.at[m, j],
-            dst_ref=fin_out.at[:, slots_of(m)],
+            src_ref=fin_source(m, j),
+            dst_ref=fin_out.at[slots_of(m)],
             send_sem=fin_send.at[m, j],
             recv_sem=fin_recv.at[m],
             device_id={"pipe": j},
@@ -256,13 +272,11 @@
         )
 
     def own_fin_copy(m):
-        return pltpu.make_async_copy(fin_stage.at[m, last], fin_out.at[:, slots_of(m)], fin_send.at[m, last])
-
-    def inp_copy(m, j):
-        return pltpu.make_async_copy(inp_stage.at[m, j], inp_out.at[j, :, slots_of(m)], inp_send.at[m, j])
-
-    def piece(j):
-        return state[:, j * width : (j + 1) * width].T.astype(BF16)
+        return pltpu.make_async_copy(fin_source(m, last), fin_out.at[slots_of(m)], fin_send.at[m, last])
+
+    def inp_copy(m):
+        return pltpu.make_async_copy(bwd_out.at[m], inp_out.at[slots_of(m)], inp_send.at[m])
+
 
     outs = (u_out, dqkv_out, o_out, da_out, u2_out, dz_out, act_out, dm_out)
 
@@ -324,8 +338,6 @@
         valid = jnp.broadcast_to((flags[m : m + 1, :] == 1).astype(F32), (SEQ, SEQ)).T
         keep = jnp.maximum(same, 1.0 - parted) * valid
         bias[m] = (keep - 1.0) * 1e30
-
-    pl.semaphore_wait(barrier, sections - 1 + 2 * paired)
 
     def forward_layer(l, m):
         def weight_wait(k):
@@ -366,6 +378,11 @@
             o_s[slot, :, i * 128 : (i + 1) * 128] = tiles[i].astype(BF16)
         out_copy(2, l, m).start()
         weight_wait(1)
+
+        @pl.when((m == 0) & (me == 0) & (l == 0))
+        def _():
+            weights_start(1)
+
         h = state[...] + nn(o_s[slot], weights[l, block_rows(3)])
         state[...] = h
         hhat, inverse = norm_parts(h)
@@ -373,6 +390,11 @@
         u2_s[l, m] = (hhat * gain_two[pl.ds(l, 1), :]).astype(BF16)
         out_copy(4, l, m).start()
         weight_wait(2)
+
+        @pl.when((m == 0) & (l == 0))
+        def _():
+            pl.semaphore_wait(barrier, sections - 1 + 2 * paired)
+
         free_slot(6, l, m)
         weight_wait(3)
         for j in range(4):
@@ -510,19 +532,17 @@
 
         lax.fori_loop(0, 2, one, 0)
 
+        fwd_out[m] = state[...].astype(BF16)
+
         @pl.when(me < last)
         def _():
-            fwd_out[m] = state[...].astype(BF16)
             forward_copy(m).start()
 
         @pl.when(me == last)
         def _():
-            for j in range(sections):
-                fin_stage[m, j] = piece(j)
-                if j == last:
-                    own_fin_copy(m).start()
-                else:
-                    fin_copy(m, j).start()
+            own_fin_copy(m).start()
+            for j in range(last):
+                fin_copy(m, j).start()
 
         return carry
 
@@ -558,20 +578,20 @@
 
         lax.fori_loop(0, 2, one, 0)
 
+        bwd_out[m] = state[...].astype(BF16)
+
         @pl.when(me > 0)
         def _():
-            bwd_out[m] = state[...].astype(BF16)
             backward_copy(m).start()
 
         @pl.when(me == 0)
         def _():
-            for j in range(sections):
-                inp_stage[m, j] = piece(j)
-                inp_copy(m, j).start()
+            inp_copy(m).start()
 
         return carry
 
     lax.fori_loop(0, micros, backward_micro, 0)
+
     share = D // replicas
     for k in range(4):
         gain = (gain_one, gain_two)[k // 2][k % 2 : k % 2 + 1, :]
@@ -611,8 +631,7 @@
 
         @pl.when(me == 0)
         def _():
-            for j in range(sections):
-                inp_copy(m, j).wait()
+            inp_copy(m).wait()
 
 
 def relay(tokens, cotangent, flags, groups, gain_one, gain_two, wqkv, wout, wup, wdown):
@@ -642,8 +661,8 @@
     return pl.pallas_call(
         functools.partial(relay_kernel, sections, replicas, micros, paired),
         out_shape=(
-            jax.ShapeDtypeStruct((width, rows), BF16),
-            jax.ShapeDtypeStruct((sections, width, rows), BF16),
+            jax.ShapeDtypeStruct((rows, FIN_WINDOW), BF16),
+            jax.ShapeDtypeStruct((rows, D), BF16),
             jax.ShapeDtypeStruct((replicas, 8, 128), F32),
             factor(D),
             factor(3 * D),
@@ -665,8 +684,6 @@
             per_micro(D),
             per_micro(D),
             per_micro(D),
-            pltpu.VMEM((micros, sections, width, SEQ), BF16),
-            pltpu.VMEM((micros, sections, width, SEQ), BF16),
             saved(D),
             saved(3 * D),
             pltpu.VMEM((2, micros, HEADS, SEQ, SEQ), BF16),
@@ -690,7 +707,7 @@
             dma((micros,)),
             dma((micros, sections)),
             dma((micros,)),
-            dma((micros, sections)),
+            dma((micros,)),
             dma((8, 2, micros)),
             dma((2, micros, 2)),
             dma((2, micros, 2)),
@@ -706,11 +723,15 @@
 
 ROWS = 96
 CHUNKS = 12
+ORDER = (3, 0, 1, 2) + tuple(range(4, CHUNKS))
+
+GUESTS = (1, 2)
 
 
 def sum_kernel(
     sections,
     gains_in,
+    fin_in,
     inp_in,
     u_in,
     dqkv_in,
@@ -723,6 +744,7 @@
     act_other,
     dm_other,
     gains_out,
+    fin_out,
     inp_out,
     qkv_out,
     out_out,
@@ -741,11 +763,20 @@
     second,
     third,
     gains_v,
+    fin_v,
+    fin_t,
+    inp_v,
+    inp_stage,
     load_sem,
     gain_send,
     gain_recv,
+    fin_sem,
     inp_send,
     inp_recv,
+    lend_send,
+    lend_recv,
+    back_send,
+    back_recv,
     send,
     recv,
     out_sem,
@@ -786,7 +817,7 @@
             copies.append((act_other.at[l, :, pl.ds(b * CHUNK, CHUNK)], act_v.at[b, rows : 2 * rows]))
         return [pltpu.make_async_copy(src, dst, load_sem.at[6 + k]) for k, (src, dst) in enumerate(copies)]
 
-    for k in range(6):
+    for k in (2, 3, 0, 1, 4, 5):
         load(k, 1).start()
     for copy in down_loads(1):
         copy.start()
@@ -803,7 +834,7 @@
 
     def inp_copy(j):
         return pltpu.make_async_remote_copy(
-            src_ref=inp_in.at[j],
+            src_ref=inp_stage.at[j],
             dst_ref=inp_out,
             send_sem=inp_send.at[j],
             recv_sem=inp_recv,
@@ -812,7 +843,10 @@
         )
 
     def own_inp_copy():
-        return pltpu.make_async_copy(inp_in.at[0], inp_out, inp_send.at[0])
+        return pltpu.make_async_copy(inp_stage.at[0], inp_out, inp_send.at[0])
+
+    def inp_load():
+        return pltpu.make_async_copy(inp_in, inp_v, inp_send.at[0])
 
     def meet():
         pl.semaphore_wait(barrier, SHARDS - 1 + lax.select(section == 0, sections - 1, 0))
@@ -822,11 +856,6 @@
             def _():
                 gain_copy(j, me).start()
 
-        @pl.when(section == 0)
-        def _():
-            own_inp_copy().start()
-            for j in range(1, sections):
-                inp_copy(j).start()
 
     def remote(src, dst, step, n, to):
         return pltpu.make_async_remote_copy(
@@ -856,6 +885,37 @@
         if i % 2 == 0:
             return remote(second.at[n, 1 - y], third.at[n], 2, n, other_y)
         return remote(second.at[n, 1 - x], third.at[n], 2, n, other_x)
+
+    host = sections - 1
+    guests = GUESTS if sections > 2 else ()
+
+    def lend_copy(g):
+        return pltpu.make_async_remote_copy(
+            src_ref=first.at[guests[g]],
+            dst_ref=first.at[2 * CHUNKS + g],
+            send_sem=lend_send.at[g],
+            recv_sem=lend_recv.at[g],
+            device_id={"pipe": host},
+            device_id_type=MESH,
+        )
+
+    def back_copy(g):
+        return pltpu.make_async_remote_copy(
+            src_ref=third.at[2 * CHUNKS + g],
+            dst_ref=third.at[guests[g]],
+            send_sem=back_send.at[g],
+            recv_sem=back_recv.at[g],
+            device_id={"pipe": 0},
+            device_id_type=MESH,
+        )
+
+    def lent_or(step, i, lent, kept):
+        if i not in guests:
+            kept()
+            return
+        away = (step == 0) & (section == 0)
+        pl.when(away)(functools.partial(lent, guests.index(i)))
+        pl.when(jnp.logical_not(away))(kept)
 
     def result_copy(n, l, i):
         if i < 3:
@@ -875,7 +935,7 @@
             down_copy(n, l).start()
         else:
             first[n] = first[n] + own[i, core]
-            first_copy(n, i).start()
+            lent_or(1 - l, i, lambda g: lend_copy(g).start(), lambda: first_copy(n, i).start())
 
     def layer_products(step, carry):
         l = 1 - step
@@ -894,11 +954,12 @@
                 part = tn(a[...], g[:, columns * CHUNK : (columns + 1) * CHUNK]).astype(BF16)
                 for r in range(SHARDS):
                     own[i, r % 2, r // 4, (r // 2) % 2] = part[r * ROWS : (r + 1) * ROWS]
-                if i == 0:
+                if i == ORDER[0]:
                     pl.when(step == 0)(meet)
                 give_copy(base + i, i).start()
-                if i > 0:
-                    add_core(base + i - 1, l, i - 1)
+                if i != ORDER[0]:
+                    before = ORDER[ORDER.index(i) - 1]
+                    add_core(base + before, l, before)
 
         def reload(k):
             @pl.when(step == 0)
@@ -906,10 +967,10 @@
                 load(k, 0).start()
                 load(k + 1, 0).start()
 
+        products(2, o_v, da_v, ((3, 0),))
+        reload(2)
         products(0, u_v, dqkv_v, ((0, 0), (1, 1), (2, 2)))
         reload(0)
-        products(2, o_v, da_v, ((3, 0),))
-        reload(2)
         products(4, u2_v, dz_v, ((4, 0), (5, 1), (6, 2), (7, 3)))
         reload(4)
         for copy in down_loads(l):
@@ -928,22 +989,62 @@
 
         for i in range(8, CHUNKS):
             give_copy(base + i, i).start()
-        for i in range(7, CHUNKS):
+        for i in ORDER[7:]:
             add_core(base + i, l, i)
         return carry
 
     lax.fori_loop(0, 2, layer_products, 0)
 
+    fin_load = pltpu.make_async_copy(fin_in, fin_v, fin_sem)
+    fin_load.start()
+    fin_load.wait()
+    width = D // sections
+    for j in range(sections):
+        first_lane = j * width - window_start(j, width)
+
+        @pl.when(section == j)
+        def _():
+            for r in range(0, rows, SEQ):
+                part = fin_v[r : r + SEQ, :].astype(F32)[:, first_lane : first_lane + width]
+                fin_t[:, r : r + SEQ] = part.T.astype(BF16)
+
+    fin_store = pltpu.make_async_copy(fin_t, fin_out, fin_sem)
+    fin_store.start()
+
+    @pl.when(section == 0)
+    def _():
+        inp_load().start()
+        inp_load().wait()
+        for j in range(sections):
+            for r in range(0, rows, SEQ):
+                part = inp_v[r : r + SEQ, :].astype(F32)[:, j * width : (j + 1) * width]
+                inp_stage[j, :, r : r + SEQ] = part.T.astype(BF16)
+        own_inp_copy().start()
+        for j in range(1, sections):
+            inp_copy(j).start()
+
+    for g, i in enumerate(guests):
+
+        @pl.when(section == host)
+        def _():
+            lend_copy(g).wait_recv()
+            first_copy(2 * CHUNKS + g, i).start()
+
+    def second_sum(n, i):
+        first_copy(n, i).wait_recv()
+        kept = first[n, :, x] if i % 2 == 0 else first[n, y]
+        second[n] = second[n] + kept
+        second_copy(n, i).start()
+
     def second_sums(step, carry):
-        for i in range(8):
+        for i in ORDER[:8]:
             n = step * CHUNKS + i
-            first_copy(n, i).wait_recv()
-            kept = first[n, :, x] if i % 2 == 0 else first[n, y]
-            second[n] = second[n] + kept
-            second_copy(n, i).start()
+            lent_or(step, i, lambda g: None, functools.partial(second_sum, n, i))
         return carry
 
     lax.fori_loop(0, 2, second_sums, 0)
+    for g, i in enumerate(guests):
+        pl.when(section == host)(functools.partial(second_sum, 2 * CHUNKS + g, i))
 
     gains_v[me] = gains_in[me]
     for j in range(SHARDS):
@@ -957,19 +1058,37 @@
         total = total + gains_v[j]
     gains_out[...] = total
 
+    def last_sum(n, i):
+        second_copy(n, i).wait_recv()
+        third[n] = third[n] + second[n, y if i % 2 == 0 else x]
+
     def last_sums(step, carry):
-        for i in range(CHUNKS):
+        for i in ORDER:
             n = step * CHUNKS + i
             if i >= 8:
                 down_copy(n, 1 - step).wait_recv()
                 third[n] = third[n] + first[n, 0, lax.select(step == 0, y, x)]
             else:
-                second_copy(n, i).wait_recv()
-                third[n] = third[n] + second[n, y if i % 2 == 0 else x]
-            result_copy(n, 1 - step, i).start()
+                lent_or(step, i, lambda g: None, functools.partial(last_sum, n, i))
+            if i not in guests:
+                result_copy(n, 1 - step, i).start()
         return carry
 
     lax.fori_loop(0, 2, last_sums, 0)
+
+    for g, i in enumerate(guests):
+
+        @pl.when(section == host)
+        def _():
+            last_sum(2 * CHUNKS + g, i)
+            back_copy(g).start()
+
+        @pl.when(section == 0)
+        def _():
+            back_copy(g).wait_recv()
+
+        for step in range(2):
+            result_copy(step * CHUNKS + i, 1 - step, i).start()
 
     def finish(step, carry):
         for i in range(CHUNKS):
@@ -977,12 +1096,24 @@
             if i >= 8:
                 down_copy(n, 1 - step).wait_send()
             else:
-                first_copy(n, i).wait_send()
-                second_copy(n, i).wait_send()
+
+                def sent():
+                    first_copy(n, i).wait_send()
+                    second_copy(n, i).wait_send()
+
+                lent_or(step, i, lambda g: lend_copy(g).wait_send(), sent)
             result_copy(n, 1 - step, i).wait()
         return carry
 
     lax.fori_loop(0, 2, finish, 0)
+    for g, i in enumerate(guests):
+
+        @pl.when(section == host)
+        def _():
+            first_copy(2 * CHUNKS + g, i).wait_send()
+            second_copy(2 * CHUNKS + g, i).wait_send()
+            back_copy(g).wait_send()
+
     for i in range(CHUNKS):
         give_copy(CHUNKS + i, i).wait_send()
     for j in range(SHARDS):
@@ -990,6 +1121,8 @@
         @pl.when(me != j)
         def _():
             gain_copy(j, me).wait_send()
+
+    fin_store.wait()
 
     @pl.when(section == 0)
     def _():
@@ -1002,12 +1135,14 @@
         inp_copy(0).wait_recv()
 
 
-def summed(gains, inp, *factors):
-    sections, width, rows = inp.shape
+def summed(gains, fin, inp, *factors):
+    sections = lax.axis_size("pipe")
+    rows, width = inp.shape[0], D // sections
     anywhere = pl.BlockSpec(memory_space=pl.ANY)
     vmem = pl.BlockSpec(memory_space=pltpu.VMEM)
     dma = pltpu.SemaphoreType.DMA
     total = 2 * CHUNKS
+    slots = total + len(GUESTS)
 
     def shard(height, columns):
         return jax.ShapeDtypeStruct((2, height, columns), BF16)
@@ -1016,37 +1151,47 @@
         functools.partial(sum_kernel, sections),
         out_shape=(
             jax.ShapeDtypeStruct((8, 128), F32),
+            jax.ShapeDtypeStruct((width, rows), BF16),
             jax.ShapeDtypeStruct((width, rows), BF16),
             shard(ROWS, 3 * D),
             shard(ROWS, D),
             shard(ROWS, FF),
             shard(4 * ROWS, D),
         ),
-        in_specs=[vmem] + [anywhere] * 11,
-        out_specs=(vmem,) + (anywhere,) * 5,
+        in_specs=[vmem] + [anywhere] * 12,
+        out_specs=(vmem,) + (anywhere,) * 6,
         scratch_shapes=[pltpu.VMEM((rows, f.shape[2]), BF16) for f in factors[:6]]
         + [
             pltpu.VMEM((2, 2 * rows, CHUNK), BF16),
             pltpu.VMEM((2 * rows, D), BF16),
             pltpu.VMEM((CHUNKS, 2, 2, 2, ROWS, CHUNK), BF16),
-            pltpu.VMEM((total, 2, 2, ROWS, CHUNK), BF16),
-            pltpu.VMEM((total, 2, ROWS, CHUNK), BF16),
-            pltpu.VMEM((total, ROWS, CHUNK), BF16),
+            pltpu.VMEM((slots, 2, 2, ROWS, CHUNK), BF16),
+            pltpu.VMEM((slots, 2, ROWS, CHUNK), BF16),
+            pltpu.VMEM((slots, ROWS, CHUNK), BF16),
             pltpu.VMEM((SHARDS, 8, 128), F32),
+            pltpu.VMEM((rows, FIN_WINDOW), BF16),
+            pltpu.VMEM((width, rows), BF16),
+            pltpu.VMEM((rows, D), BF16),
+            pltpu.VMEM((sections, width, rows), BF16),
             dma((12,)),
             dma((SHARDS,)),
             dma((SHARDS,)),
+            dma(()),
             dma((sections,)),
             dma(()),
-            dma((3, total)),
-            dma((3, total)),
+            dma((len(GUESTS),)),
+            dma((len(GUESTS),)),
+            dma((len(GUESTS),)),
+            dma((len(GUESTS),)),
+            dma((3, slots)),
+            dma((3, slots)),
             dma((total,)),
         ],
         compiler_params=pltpu.CompilerParams(
             collective_id=1, has_side_effects=True, vmem_limit_bytes=60 * MIB
         ),
         name="sum",
-    )(gains, inp, *factors)
+    )(gains, fin, inp, *factors)
 
 
 def write_kernel(count, share, gains, *refs):
@@ -1119,8 +1264,8 @@
     replicas = lax.axis_size("dp")
     share = D // replicas
     if replicas == SHARDS and share == ROWS:
-        gains, inp, g_qkv, g_out, g_up, g_down = summed(
-            gains, inp, u, dqkv, o, da, u2, dz, act, dm, act_other, dm_other
+        gains, fin, inp, g_qkv, g_out, g_up, g_down = summed(
+            gains, fin, inp, u, dqkv, o, da, u2, dz, act, dm, act_other, dm_other
         )
     else:
 
@@ -1129,8 +1274,12 @@
             return lax.psum_scatter(total, "dp", scatter_dimension=1, tiled=True)
 
         gains = lax.psum_scatter(gains, "dp", scatter_dimension=0)
-        inp = jnp.where(lax.axis_index("pipe") == 0, inp, jnp.zeros_like(inp))
-        inp = lax.psum_scatter(inp, "pipe", scatter_dimension=0)
+        sections = lax.axis_size("pipe")
+        width = D // sections
+        first_lanes = jnp.array([j * width - window_start(j, width) for j in range(sections)])
+        fin = lax.dynamic_slice_in_dim(fin, first_lanes[lax.axis_index("pipe")], width, 1).T
+        inp = jnp.where(lax.axis_index("pipe") == 0, inp.T, jnp.zeros_like(inp.T))
+        inp = lax.psum_scatter(inp, "pipe", scatter_dimension=0, tiled=True)
         g_qkv, g_out, g_up, g_down = grad(u, dqkv), grad(o, da), grad(u2, dz), grad(act, dm)
     gain_one_grad, gain_two_grad, fin, inp, g_qkv, g_out, g_up, g_down = written(
         gains, share, (fin, inp, g_qkv, g_out, g_up, g_down), (BF16,) + (F32,) * 5

time: 261 us -> 250 us (0.958)
  Pallas kernels: 260 us -> 249 us
    pallas_call x1, Pallas kernels: 100 us -> 90.8 us  [summed(): pl.pallas_call(functools.partial(sum_kernel, sections), out_shape=(jax.Sh...]
where the time goes in v7:
time: 250 us
  Pallas kernels  249 us (100%)
    pallas_call x1, Pallas kernels, relay(): pl.pallas_call(functools.partial(relay_kernel, sections, replicas, micros...  152 us
    pallas_call x1, Pallas kernels, summed(): pl.pallas_call(functools.partial(sum_kernel, sections), out_shape=(jax.Sh...  90.8 us
    pallas_call x1, Pallas kernels, written(): pl.pallas_call(functools.partial(write_kernel, count, share), out_shape=(...  5.79 us

profile of v7, /device:TPU:0, one launch (start us, length us, event | category | flops | bytes accessed | tf_op | source)
XLA Modules:
  0.0 249.9 jit_solution(2270867304384146726)
XLA Ops:
  0.6 152.4 %relay.1 = (bf16[512,256]{1,0:T(8,128)(2,1)}, bf16[512,768]{1,0:T(8,128)(2,1)}, f32[8,8,128]{2,1,0:T(8,128)}, bf16[2,512,768]{2,1,0:T(8,128)(2,1)}, bf16[2,512,2...) custom-call(bf16[512,768]{1,0:T(8,128)(2,1)} %tokens.1, ...), custom_call_target="tpu_custom_call" | custom-call | tf_op jit(solution)/shard_map/relay/pallas_call | solution.py:661
  153.1 90.8 %sum.1 = (f32[8,128]{1,0:T(8,128)}, bf16[192,512]{1,0:T(8,128)(2,1)}, bf16[192,512]{1,0:T(8,128)(2,1)}, bf16[2,96,2304]{2,1,0:T(8,128)(2,1)}, bf16[2,96,768]{2,1...) custom-call(f32[8,8,128]{2,1,0:T(8,128)} %get-tuple-element.36.gains_in, ...), custom_call_target="tpu_custom_call" | custom-call | tf_op jit(solution)/shard_map/sum/pallas_call | solution.py:1150
  243.9 5.8 %write.1 = (f32[2,96]{1,0:T(2,128)}, f32[2,96]{1,0:T(2,128)}, bf16[192,512]{1,0:T(8,128)(2,1)}, f32[192,512]{1,0:T(8,128)}, f32[2,96,2304]{2,1,0:T(8,128)}, /*in...) custom-call(f32[8,128]{1,0:T(8,128)} %get-tuple-element.49.gains, ...), custom_call_target="tpu_custom_call" | custom-call | tf_op jit(solution)/shard_map/write/pallas_call | solution.py:1224

commit v8 on v7

--- a/solution.py
+++ b/solution.py
@@ -108,7 +108,7 @@
     dz_out,
     act_out,
     dm_out,
-    act_other,
+    u2_other,
     dm_other,
     turned_hbm,
     weights,
@@ -141,8 +141,8 @@
     fin_recv,
     inp_send,
     out_sem,
-    act_send,
-    act_recv,
+    u2_send,
+    u2_recv,
     dm_send,
     dm_recv,
 ):
@@ -297,21 +297,15 @@
     def partner(l):
         return {"dp": lax.select(l == 1, replica + 2 - 4 * x, replica + 4 - 8 * y)}
 
-    def act_copy(l, m, b):
-        block = l * (2 * b + 1 - x) + (1 - l) * (2 * (1 - y) + b)
+    def u2_copy(l, m):
         return pltpu.make_async_remote_copy(
-            src_ref=act_out.at[l, slots_of(m), block_rows(block)],
-            dst_ref=act_other.at[l, slots_of(m), pl.ds(b * D, D)],
-            send_sem=act_send.at[l, m, b],
-            recv_sem=act_recv.at[l, m, b],
+            src_ref=u2_s.at[l, m],
+            dst_ref=u2_other.at[l, slots_of(m)],
+            send_sem=u2_send.at[l, m],
+            recv_sem=u2_recv.at[l, m],
             device_id=partner(l),
             device_id_type=MESH,
         )
-
-    def act_start(l, m):
-        if paired:
-            for b in range(2):
-                act_copy(l, m, b).start()
 
     def dm_copy(l, m):
         return pltpu.make_async_remote_copy(
@@ -327,8 +321,6 @@
         @pl.when(m > 0)
         def _():
             out_copy(kind, l, m - 1).wait()
-            if kind == 6:
-                act_start(l, m - 1)
 
     row = lax.broadcasted_iota(jnp.int32, (SEQ, SEQ), 0) // (SEQ // 4)
     column = lax.broadcasted_iota(jnp.int32, (SEQ, SEQ), 1) // (SEQ // 4)
@@ -389,12 +381,14 @@
         stat_s[l, m, :, 1:2] = inverse
         u2_s[l, m] = (hhat * gain_two[pl.ds(l, 1), :]).astype(BF16)
         out_copy(4, l, m).start()
+
+        @pl.when((m == 0) & (l == 0))
+        def _():
+            pl.semaphore_wait(barrier, sections - 1 + 2 * paired)
+
+        if paired:
+            u2_copy(l, m).start()
         weight_wait(2)
-
-        @pl.when((m == 0) & (l == 0))
-        def _():
-            pl.semaphore_wait(barrier, sections - 1 + 2 * paired)
-
         free_slot(6, l, m)
         weight_wait(3)
         for j in range(4):
@@ -547,10 +541,6 @@
         return carry
 
     lax.fori_loop(0, micros, forward_micro, 0)
-    for l in range(2):
-        out_copy(6, l, micros - 1).wait()
-        act_start(l, micros - 1)
-
     @pl.when(me < last)
     def _():
         def one(i, c):
@@ -600,14 +590,13 @@
             gains_out[r, k : k + 1, 0:share] = total[:, r * share : (r + 1) * share]
 
     for l in range(2):
-        for kind in (2, 3):
+        for kind in (2, 3, 6):
             out_copy(kind, l, micros - 1).wait()
         for m in range(micros):
             for kind in (0, 1, 4, 5, 7):
                 out_copy(kind, l, m).wait()
             if paired:
-                for b in range(2):
-                    act_copy(l, m, b).wait()
+                u2_copy(l, m).wait()
                 dm_copy(l, m).wait()
     for m in range(micros):
 
@@ -672,7 +661,7 @@
             factor(FF),
             factor(FF),
             factor(D),
-            factor(2 * D),
+            factor(D),
             factor(D),
             jax.ShapeDtypeStruct((2, BLOCKS * D, D), BF16),
         ),
@@ -709,8 +698,8 @@
             dma((micros,)),
             dma((micros,)),
             dma((8, 2, micros)),
-            dma((2, micros, 2)),
-            dma((2, micros, 2)),
+            dma((2, micros)),
+            dma((2, micros)),
             dma((2, micros)),
             dma((2, micros)),
         ],
@@ -722,10 +711,13 @@
 
 
 ROWS = 96
-CHUNKS = 12
+CHUNKS = 10
+UP, DOWN = 4, 6
+AGAIN = 256
 ORDER = (3, 0, 1, 2) + tuple(range(4, CHUNKS))
 
-GUESTS = (1, 2)
+LOANS = ((0, 1, 1, 0), (0, 1, 2, 1))
+GUESTS = 2
 
 
 def sum_kernel(
@@ -741,8 +733,10 @@
     dz_in,
     act_in,
     dm_in,
-    act_other,
+    u2_other,
     dm_other,
+    wup_hbm,
+    wdown_hbm,
     gains_out,
     fin_out,
     inp_out,
@@ -758,6 +752,8 @@
     dz_v,
     act_v,
     dm_v,
+    wup_v,
+    wdown_v,
     own,
     first,
     second,
@@ -779,6 +775,7 @@
     back_recv,
     send,
     recv,
+    up_sem,
     out_sem,
 ):
     me = lax.axis_index("dp")
@@ -797,29 +794,45 @@
         def _():
             pl.semaphore_signal(barrier, inc=1, device_id={"dp": j}, device_id_type=MESH)
 
-    @pl.when(section > 0)
-    def _():
-        pl.semaphore_signal(barrier, inc=1, device_id={"pipe": 0}, device_id_type=MESH)
-
-    sources = (u_in, dqkv_in, o_in, da_in, u2_in, dz_in)
-    held = (u_v, dqkv_v, o_v, da_v, u2_v, dz_v)
+    loans = LOANS if sections > 3 else ()
+    for j in range(1, sections):
+        for to in sorted({0} | {lender for lender, k, _, _ in loans if sections - k == j}):
+
+            @pl.when(section == j)
+            def _():
+                pl.semaphore_signal(barrier, inc=1, device_id={"pipe": to}, device_id_type=MESH)
+
+    sources = (u_in, dqkv_in, o_in, da_in)
+    held = (u_v, dqkv_v, o_v, da_v)
     rows = dm_in.shape[1]
 
     def load(k, l):
         return pltpu.make_async_copy(sources[k].at[l], held[k], load_sem.at[k])
 
-    def down_loads(l):
-        copies = [(dm_in.at[l], dm_v.at[0:rows]), (dm_other.at[l], dm_v.at[rows : 2 * rows])]
+    def hidden(l, b, other=False):
+        px, py = (1 - x, 1 - y) if other else (x, y)
+        block = l * (2 * b + px) + (1 - l) * (2 * py + b)
+        return pl.ds(pl.multiple_of(block * CHUNK, CHUNK), CHUNK)
+
+    def mlp_loads(l):
+        own_rows, other_rows = pl.ds(0, rows), pl.ds(rows, rows)
+        copies = [
+            (u2_other.at[l], u2_v.at[other_rows]),
+            (dm_other.at[l], dm_v.at[other_rows]),
+            (u2_in.at[l], u2_v.at[own_rows]),
+            (dm_in.at[l], dm_v.at[own_rows]),
+        ]
         for b in range(2):
-            block = l * (2 * b + x) + (1 - l) * (2 * y + b)
-            columns = pl.ds(pl.multiple_of(block * CHUNK, CHUNK), CHUNK)
-            copies.append((act_in.at[l, :, columns], act_v.at[b, 0:rows]))
-            copies.append((act_other.at[l, :, pl.ds(b * CHUNK, CHUNK)], act_v.at[b, rows : 2 * rows]))
-        return [pltpu.make_async_copy(src, dst, load_sem.at[6 + k]) for k, (src, dst) in enumerate(copies)]
-
-    for k in (2, 3, 0, 1, 4, 5):
+            units = hidden(l, b)
+            copies.append((wup_hbm.at[l, :, units], wup_v.at[b]))
+            copies.append((wdown_hbm.at[l, units], wdown_v.at[b]))
+            copies.append((dz_in.at[l, :, units], dz_v.at[b, own_rows]))
+            copies.append((act_in.at[l, :, units], act_v.at[b, own_rows]))
+        return [pltpu.make_async_copy(src, dst, load_sem.at[4 + k]) for k, (src, dst) in enumerate(copies)]
+
+    for k in (2, 3, 0, 1):
         load(k, 1).start()
-    for copy in down_loads(1):
+    for copy in mlp_loads(1):
         copy.start()
 
     def gain_copy(j, source):
@@ -849,7 +862,11 @@
         return pltpu.make_async_copy(inp_in, inp_v, inp_send.at[0])
 
     def meet():
-        pl.semaphore_wait(barrier, SHARDS - 1 + lax.select(section == 0, sections - 1, 0))
+        others = lax.select(section == 0, sections - 1, 0)
+        for lender in {lender for lender, _, _, _ in loans} - {0}:
+            hosts = {k for other, k, _, _ in loans if other == lender}
+            others = others + lax.select(section == lender, len(hosts), 0)
+        pl.semaphore_wait(barrier, SHARDS - 1 + others)
         for j in range(SHARDS):
 
             @pl.when(me != j)
@@ -868,7 +885,7 @@
         )
 
     def give_copy(n, i):
-        if i >= 8:
+        if i >= DOWN:
             return remote(own.at[i, 1 - core, 0], first.at[n, 0], 0, n, other_core)
         return remote(own.at[i, 1 - core], first.at[n], 0, n, other_core)
 
@@ -876,81 +893,113 @@
         mine, to = lax.select(l == 1, y, x), lax.select(l == 1, other_y, other_x)
         return remote(first.at[n, 0, 1 - mine], third.at[n], 2, n, to)
 
-    def first_copy(n, i):
+    def first_copy(n, i, l=None):
+        if i >= UP:
+            mine = lax.select(l == 1, y, x)
+            to = lax.select(l == 1, other_y, other_x)
+            return remote(first.at[n, 1 - mine], second.at[n], 1, n, to)
         if i % 2 == 0:
             return remote(first.at[n, :, 1 - x], second.at[n], 1, n, other_x)
         return remote(first.at[n, 1 - y], second.at[n], 1, n, other_y)
 
-    def second_copy(n, i):
+    def second_copy(n, i, l=None):
+        if i >= UP:
+            mine = lax.select(l == 1, x, y)
+            to = lax.select(l == 1, other_x, other_y)
+            return remote(second.at[n, 1 - mine], third.at[n], 2, n, to)
         if i % 2 == 0:
             return remote(second.at[n, 1 - y], third.at[n], 2, n, other_y)
         return remote(second.at[n, 1 - x], third.at[n], 2, n, other_x)
 
-    host = sections - 1
-    guests = GUESTS if sections > 2 else ()
-
     def lend_copy(g):
+        lender, k, i, slot = loans[g]
         return pltpu.make_async_remote_copy(
-            src_ref=first.at[guests[g]],
-            dst_ref=first.at[2 * CHUNKS + g],
+            src_ref=first.at[i],
+            dst_ref=first.at[2 * CHUNKS + slot],
             send_sem=lend_send.at[g],
             recv_sem=lend_recv.at[g],
-            device_id={"pipe": host},
+            device_id={"pipe": sections - k},
             device_id_type=MESH,
         )
 
     def back_copy(g):
+        lender, k, i, slot = loans[g]
         return pltpu.make_async_remote_copy(
-            src_ref=third.at[2 * CHUNKS + g],
-            dst_ref=third.at[guests[g]],
+            src_ref=third.at[2 * CHUNKS + slot],
+            dst_ref=third.at[i],
             send_sem=back_send.at[g],
             recv_sem=back_recv.at[g],
-            device_id={"pipe": 0},
+            device_id={"pipe": lender},
             device_id_type=MESH,
         )
 
     def lent_or(step, i, lent, kept):
-        if i not in guests:
+        away = None
+        for g, (lender, _, chunk, _) in enumerate(loans):
+            if chunk == i:
+                here = (step == 0) & (section == lender)
+                pl.when(here)(functools.partial(lent, g))
+                away = here if away is None else away | here
+        if away is None:
             kept()
-            return
-        away = (step == 0) & (section == 0)
-        pl.when(away)(functools.partial(lent, guests.index(i)))
-        pl.when(jnp.logical_not(away))(kept)
+        else:
+            pl.when(jnp.logical_not(away))(kept)
+
+    def as_host(action):
+        for g, (_, k, i, slot) in enumerate(loans):
+            pl.when(section == sections - k)(functools.partial(action, g, 2 * CHUNKS + slot, i))
+
+    lent_chunks = sorted({i for _, _, i, _ in loans})
 
     def result_copy(n, l, i):
         if i < 3:
             dst = qkv_out.at[l, :, pl.ds(i * CHUNK, CHUNK)]
         elif i < 4:
             dst = out_out.at[l]
-        elif i < 8:
-            dst = up_out.at[l, :, pl.ds((i - 4) * CHUNK, CHUNK)]
+        elif i < DOWN:
+            dst = up_out.at[l, :, hidden(l, i - UP, other=True)]
         else:
-            dst = down_out.at[l, pl.ds((i - 8) * ROWS, ROWS)]
+            dst = down_out.at[l, pl.ds((i - DOWN) * ROWS, ROWS)]
         return pltpu.make_async_copy(third.at[n], dst, out_sem.at[n])
+
+    def own_up_copy(n, l, i):
+        mine = lax.select(l == 1, x, y)
+        return pltpu.make_async_copy(second.at[n, mine], up_out.at[l, :, hidden(l, i - UP)], up_sem.at[n])
 
     def add_core(n, l, i):
         give_copy(n, i).wait_recv()
-        if i >= 8:
+        if i >= DOWN:
             first[n, 0] = first[n, 0] + own[i, core, 0]
             down_copy(n, l).start()
         else:
             first[n] = first[n] + own[i, core]
-            lent_or(1 - l, i, lambda g: lend_copy(g).start(), lambda: first_copy(n, i).start())
-
-    def layer_products(step, carry):
+            lent_or(1 - l, i, lambda g: lend_copy(g).start(), lambda: first_copy(n, i, l).start())
+
+    def free(step, i):
+        @pl.when(step > 0)
+        def _():
+            give_copy(i, i).wait_send()
+
+    def second_sum(n, i, l=None):
+        first_copy(n, i, l).wait_recv()
+        if i >= UP:
+            kept = first[n, lax.select(l == 1, y, x)]
+        else:
+            kept = first[n, :, x] if i % 2 == 0 else first[n, y]
+        second[n] = second[n] + kept
+        second_copy(n, i, l).start()
+        if i >= UP:
+            own_up_copy(n, l, i).start()
+
+    def plain_products(step, carry):
         l = 1 - step
         base = step * CHUNKS
-
-        def free(i):
-            @pl.when(step > 0)
-            def _():
-                give_copy(i, i).wait_send()
 
         def products(k, a, g, slots):
             load(k, l).wait()
             load(k + 1, l).wait()
             for i, columns in slots:
-                free(i)
+                free(step, i)
                 part = tn(a[...], g[:, columns * CHUNK : (columns + 1) * CHUNK]).astype(BF16)
                 for r in range(SHARDS):
                     own[i, r % 2, r // 4, (r // 2) % 2] = part[r * ROWS : (r + 1) * ROWS]
@@ -960,6 +1009,11 @@
                 if i != ORDER[0]:
                     before = ORDER[ORDER.index(i) - 1]
                     add_core(base + before, l, before)
+                else:
+
+                    @pl.when(step > 0)
+                    def _():
+                        add_core(base - CHUNKS + ORDER[UP - 1], l + 1, ORDER[UP - 1])
 
         def reload(k):
             @pl.when(step == 0)
@@ -971,29 +1025,80 @@
         reload(2)
         products(0, u_v, dqkv_v, ((0, 0), (1, 1), (2, 2)))
         reload(0)
-        products(4, u2_v, dz_v, ((4, 0), (5, 1), (6, 2), (7, 3)))
-        reload(4)
-        for copy in down_loads(l):
-            copy.wait()
-        for i in range(8, CHUNKS):
-            free(i)
+        return carry
+
+    lax.fori_loop(0, 2, plain_products, 0)
+    add_core(CHUNKS + ORDER[UP - 1], 0, ORDER[UP - 1])
+
+    def mlp_products(step, carry):
+        l = 1 - step
+        base = step * CHUNKS
+        copies = mlp_loads(l)
+
+        def next_loads(*which):
+            @pl.when(step == 0)
+            def _():
+                later = mlp_loads(0)
+                for k in which:
+                    later[k].start()
+
+        for k in (0, 1, 4, 5, 8, 9):
+            copies[k].wait()
+
+        def again(k, c):
+            at = pl.ds(pl.multiple_of(rows + k * AGAIN, AGAIN), AGAIN)
+            for b in range(2):
+                act, slope = gelu_parts(nn(u2_v[at], wup_v[b]))
+                act_v[b, at] = act.astype(BF16)
+                dz_v[b, at] = (slope * nt(dm_v[at], wdown_v[b])).astype(BF16)
+            return c
+
+        lax.fori_loop(0, rows // AGAIN, again, 0)
+        next_loads(4, 5, 8, 9)
+        for i in ORDER[:UP]:
+            lent_or(step, i, lambda g: None, functools.partial(second_sum, base + i, i, l))
+        for k in (2, 3, 6, 7, 10, 11):
+            copies[k].wait()
+        for b in range(2):
+            i = UP + b
+            free(step, i)
+            part = tn(u2_v[...], dz_v[b]).astype(BF16)
+            for r in range(SHARDS):
+                ry, rx = r // 4, (r // 2) % 2
+                across, along = l * ry + (1 - l) * rx, l * rx + (1 - l) * ry
+                own[i, r % 2, across, along] = part[r * ROWS : (r + 1) * ROWS]
+            give_copy(base + i, i).start()
+            if b == 1:
+                add_core(base + UP, l, UP)
+        next_loads(0, 2, 6, 10)
+        for i in range(DOWN, CHUNKS):
+            free(step, i)
         for b in range(2):
             part = tn(act_v[b], dm_v[...]).astype(BF16)
             for r in range(8):
-                own[8 + r % 4, r // 4, 0, b] = part[r * ROWS : (r + 1) * ROWS]
-
-        @pl.when(step == 0)
-        def _():
-            for copy in down_loads(0):
-                copy.start()
-
-        for i in range(8, CHUNKS):
+                own[DOWN + r % 4, r // 4, 0, b] = part[r * ROWS : (r + 1) * ROWS]
+        next_loads(1, 3, 7, 11)
+        for i in range(DOWN, CHUNKS):
             give_copy(base + i, i).start()
-        for i in ORDER[7:]:
+        for i in range(UP + 1, CHUNKS):
             add_core(base + i, l, i)
         return carry
 
-    lax.fori_loop(0, 2, layer_products, 0)
+    lax.fori_loop(0, 2, mlp_products, 0)
+
+    def up_sums(step, carry):
+        for i in range(UP, DOWN):
+            second_sum(step * CHUNKS + i, i, 1 - step)
+        return carry
+
+    lax.fori_loop(0, 2, up_sums, 0)
+
+    def take_in(g, n, i):
+        lend_copy(g).wait_recv()
+        first_copy(n, i).start()
+
+    as_host(take_in)
+    as_host(lambda g, n, i: second_sum(n, i))
 
     fin_load = pltpu.make_async_copy(fin_in, fin_v, fin_sem)
     fin_load.start()
@@ -1023,28 +1128,9 @@
         for j in range(1, sections):
             inp_copy(j).start()
 
-    for g, i in enumerate(guests):
-
-        @pl.when(section == host)
-        def _():
-            lend_copy(g).wait_recv()
-            first_copy(2 * CHUNKS + g, i).start()
-
-    def second_sum(n, i):
-        first_copy(n, i).wait_recv()
-        kept = first[n, :, x] if i % 2 == 0 else first[n, y]
-        second[n] = second[n] + kept
-        second_copy(n, i).start()
-
-    def second_sums(step, carry):
-        for i in ORDER[:8]:
-            n = step * CHUNKS + i
-            lent_or(step, i, lambda g: None, functools.partial(second_sum, n, i))
-        return carry
-
-    lax.fori_loop(0, 2, second_sums, 0)
-    for g, i in enumerate(guests):
-        pl.when(section == host)(functools.partial(second_sum, 2 * CHUNKS + g, i))
+    def take_in(g, n, i):
+        lend_copy(g).wait_recv()
+        first_copy(n, i).start()
 
     gains_v[me] = gains_in[me]
     for j in range(SHARDS):
@@ -1065,54 +1151,58 @@
     def last_sums(step, carry):
         for i in ORDER:
             n = step * CHUNKS + i
-            if i >= 8:
+            if i >= DOWN:
                 down_copy(n, 1 - step).wait_recv()
                 third[n] = third[n] + first[n, 0, lax.select(step == 0, y, x)]
+            elif i >= UP:
+                second_copy(n, i, 1 - step).wait_recv()
             else:
                 lent_or(step, i, lambda g: None, functools.partial(last_sum, n, i))
-            if i not in guests:
+            if i not in lent_chunks:
                 result_copy(n, 1 - step, i).start()
         return carry
 
     lax.fori_loop(0, 2, last_sums, 0)
 
-    for g, i in enumerate(guests):
-
-        @pl.when(section == host)
-        def _():
-            last_sum(2 * CHUNKS + g, i)
-            back_copy(g).start()
-
-        @pl.when(section == 0)
+    def give_back(g, n, i):
+        last_sum(n, i)
+        back_copy(g).start()
+
+    as_host(give_back)
+    for g, (lender, _, _, _) in enumerate(loans):
+
+        @pl.when(section == lender)
         def _():
             back_copy(g).wait_recv()
 
+    for i in lent_chunks:
         for step in range(2):
             result_copy(step * CHUNKS + i, 1 - step, i).start()
 
     def finish(step, carry):
         for i in range(CHUNKS):
             n = step * CHUNKS + i
-            if i >= 8:
+            if i >= DOWN:
                 down_copy(n, 1 - step).wait_send()
             else:
 
                 def sent():
-                    first_copy(n, i).wait_send()
-                    second_copy(n, i).wait_send()
+                    first_copy(n, i, 1 - step).wait_send()
+                    second_copy(n, i, 1 - step).wait_send()
+                    if i >= UP:
+                        own_up_copy(n, 1 - step, i).wait()
 
                 lent_or(step, i, lambda g: lend_copy(g).wait_send(), sent)
             result_copy(n, 1 - step, i).wait()
         return carry
 
     lax.fori_loop(0, 2, finish, 0)
-    for g, i in enumerate(guests):
-
-        @pl.when(section == host)
-        def _():
-            first_copy(2 * CHUNKS + g, i).wait_send()
-            second_copy(2 * CHUNKS + g, i).wait_send()
-            back_copy(g).wait_send()
+    def guest_sent(g, n, i):
+        first_copy(n, i).wait_send()
+        second_copy(n, i).wait_send()
+        back_copy(g).wait_send()
+
+    as_host(guest_sent)
 
     for i in range(CHUNKS):
         give_copy(CHUNKS + i, i).wait_send()
@@ -1142,7 +1232,7 @@
     vmem = pl.BlockSpec(memory_space=pltpu.VMEM)
     dma = pltpu.SemaphoreType.DMA
     total = 2 * CHUNKS
-    slots = total + len(GUESTS)
+    slots = total + GUESTS
 
     def shard(height, columns):
         return jax.ShapeDtypeStruct((2, height, columns), BF16)
@@ -1158,12 +1248,16 @@
             shard(ROWS, FF),
             shard(4 * ROWS, D),
         ),
-        in_specs=[vmem] + [anywhere] * 12,
+        in_specs=[vmem] + [anywhere] * 14,
         out_specs=(vmem,) + (anywhere,) * 6,
-        scratch_shapes=[pltpu.VMEM((rows, f.shape[2]), BF16) for f in factors[:6]]
+        scratch_shapes=[pltpu.VMEM((rows, f.shape[2]), BF16) for f in factors[:4]]
         + [
+            pltpu.VMEM((2 * rows, D), BF16),
+            pltpu.VMEM((2, 2 * rows, CHUNK), BF16),
             pltpu.VMEM((2, 2 * rows, CHUNK), BF16),
             pltpu.VMEM((2 * rows, D), BF16),
+            pltpu.VMEM((2, D, CHUNK), BF16),
+            pltpu.VMEM((2, CHUNK, D), BF16),
             pltpu.VMEM((CHUNKS, 2, 2, 2, ROWS, CHUNK), BF16),
             pltpu.VMEM((slots, 2, 2, ROWS, CHUNK), BF16),
             pltpu.VMEM((slots, 2, ROWS, CHUNK), BF16),
@@ -1173,18 +1267,19 @@
             pltpu.VMEM((width, rows), BF16),
             pltpu.VMEM((rows, D), BF16),
             pltpu.VMEM((sections, width, rows), BF16),
-            dma((12,)),
+            dma((16,)),
             dma((SHARDS,)),
             dma((SHARDS,)),
             dma(()),
             dma((sections,)),
             dma(()),
-            dma((len(GUESTS),)),
-            dma((len(GUESTS),)),
-            dma((len(GUESTS),)),
-            dma((len(GUESTS),)),
+            dma((len(LOANS),)),
+            dma((len(LOANS),)),
+            dma((len(LOANS),)),
+            dma((len(LOANS),)),
             dma((3, slots)),
             dma((3, slots)),
+            dma((total,)),
             dma((total,)),
         ],
         compiler_params=pltpu.CompilerParams(
@@ -1248,7 +1343,7 @@
     groups,
 ):
     micros = tokens.shape[0] // SEQ
-    fin, inp, gains, u, dqkv, o, da, u2, dz, act, dm, act_other, dm_other, _ = relay(
+    fin, inp, gains, u, dqkv, o, da, u2, dz, act, dm, u2_other, dm_other, _ = relay(
         tokens,
         cotangent,
         flags.reshape(micros, SEQ),
@@ -1265,7 +1360,7 @@
     share = D // replicas
     if replicas == SHARDS and share == ROWS:
         gains, fin, inp, g_qkv, g_out, g_up, g_down = summed(
-            gains, fin, inp, u, dqkv, o, da, u2, dz, act, dm, act_other, dm_other
+            gains, fin, inp, u, dqkv, o, da, u2, dz, act, dm, u2_other, dm_other, up_weight, down_weight
         )
     else:
 

time: 250 us -> 234 us (0.936)
  Pallas kernels: 249 us -> 233 us
    pallas_call x1, Pallas kernels: 90.8 us -> 74.9 us  [summed(): pl.pallas_call(functools.partial(sum_kernel, sections), out_shape=(jax.Sh...]
where the time goes in v8:
time: 234 us
  Pallas kernels  233 us (100%)
    pallas_call x1, Pallas kernels, relay(): pl.pallas_call(functools.partial(relay_kernel, sections, replicas, micros...  152 us
    pallas_call x1, Pallas kernels, summed(): pl.pallas_call(functools.partial(sum_kernel, sections), out_shape=(jax.Sh...  74.9 us
    pallas_call x1, Pallas kernels, written(): pl.pallas_call(functools.partial(write_kernel, count, share), out_shape=(...  5.79 us

profile of v8, /device:TPU:0, one launch (start us, length us, event | category | flops | bytes accessed | tf_op | source)
XLA Modules:
  0.0 233.6 jit_solution(6947900981943435450)
XLA Ops:
  0.6 152.1 %relay.1 = (bf16[512,256]{1,0:T(8,128)(2,1)}, bf16[512,768]{1,0:T(8,128)(2,1)}, f32[8,8,128]{2,1,0:T(8,128)}, bf16[2,512,768]{2,1,0:T(8,128)(2,1)}, bf16[2,512,2...) custom-call(bf16[512,768]{1,0:T(8,128)(2,1)} %tokens.1, ...), custom_call_target="tpu_custom_call" | custom-call | tf_op jit(solution)/shard_map/relay/pallas_call | solution.py:650
  152.7 74.9 %sum.1 = (f32[8,128]{1,0:T(8,128)}, bf16[192,512]{1,0:T(8,128)(2,1)}, bf16[192,512]{1,0:T(8,128)(2,1)}, bf16[2,96,2304]{2,1,0:T(8,128)(2,1)}, bf16[2,96,768]{2,1...) custom-call(f32[8,8,128]{2,1,0:T(8,128)} %get-tuple-element.36.gains_in, ...), custom_call_target="tpu_custom_call" | custom-call | tf_op jit(solution)/shard_map/sum/pallas_call | solution.py:1240
  227.7 5.8 %write.1 = (f32[2,96]{1,0:T(2,128)}, f32[2,96]{1,0:T(2,128)}, bf16[192,512]{1,0:T(8,128)(2,1)}, f32[192,512]{1,0:T(8,128)}, f32[2,96,2304]{2,1,0:T(8,128)}, /*in...) custom-call(f32[8,128]{1,0:T(8,128)} %get-tuple-element.49.gains, ...), custom_call_target="tpu_custom_call" | custom-call | tf_op jit(solution)/shard_map/write/pallas_call | solution.py:1319

commit v9 on v8

--- a/solution.py
+++ b/solution.py
@@ -23,6 +23,8 @@
 TILE = 256
 
 KINDS = ((0, 3), (3, 1), (4, 4), (8, 4))
+
+TURNED = (8, 11, 4, 0)
 BLOCKS = 12
 
 FIN_WINDOW = 256
@@ -183,8 +185,17 @@
         )
 
     def swap_copy(l, k):
-        rows = block_rows(*KINDS[k])
-        return pltpu.make_async_copy(turned_hbm.at[l, rows], weights.at[1 - l, rows], swap_sem.at[l, k])
+        first, count = KINDS[k]
+        to = block_rows(TURNED[k], count)
+        return pltpu.make_async_copy(
+            turned_hbm.at[l, block_rows(first, count)], weights.at[1 - l, to], swap_sem.at[l, k]
+        )
+
+    def swap_in(l, m, *kinds):
+        @pl.when((m == micros - 1) & (me == last))
+        def _():
+            for k in kinds:
+                swap_copy(1 - l, k).start()
 
     def turn(l, b):
         def tile(r, c):
@@ -377,6 +388,7 @@
 
         h = state[...] + nn(o_s[slot], weights[l, block_rows(3)])
         state[...] = h
+        swap_in(l, m, 3)
         hhat, inverse = norm_parts(h)
         stat_s[l, m, :, 1:2] = inverse
         u2_s[l, m] = (hhat * gain_two[pl.ds(l, 1), :]).astype(BF16)
@@ -395,7 +407,9 @@
             act, slope = gelu_parts(nn(u2_s[l, m], weights[l, block_rows(4 + j)]))
             act_s[slot, :, j * D : (j + 1) * D] = act.astype(BF16)
             gp_s[l, m, :, j * D : (j + 1) * D] = slope.astype(BF16)
+        swap_in(l, m, 2)
         state[...] = state[...] + nn(act_s[slot], weights[l, block_rows(8, 4)])
+        swap_in(l, m, 1, 0)
         out_copy(6, l, m).start()
 
     def norm_back(du, hat_scaled, gain, inverse):
@@ -415,6 +429,9 @@
     def backward_layer(l, m):
         slot = l
         held = lax.select(me == last, 1 - l, l)
+
+        def turned(k, j=0, count=1):
+            return held, block_rows(lax.select(me == last, TURNED[k], KINDS[k][0]) + j, count)
 
         def turned_wait(k):
             @pl.when((m == 0) & (me == last))
@@ -429,12 +446,12 @@
         if paired:
             dm_copy(l, m).start()
         for j in range(4):
-            da = nn(dm_s[l, m], weights[held, block_rows(8 + j)])
+            da = nn(dm_s[l, m], weights[turned(3, j)])
             dz = gp_s[l, m, :, j * D : (j + 1) * D].astype(F32) * da
             gp_s[l, m, :, j * D : (j + 1) * D] = dz.astype(BF16)
         out_copy(5, l, m).start()
         dh, weighted = norm_back(
-            nn(gp_s[l, m], weights[held, block_rows(4, 4)]), u2_s[l, m].astype(F32), gain_two[pl.ds(l, 1), :], stat_s[l, m, :, 1:2]
+            nn(gp_s[l, m], weights[turned(2, 0, 4)]), u2_s[l, m].astype(F32), gain_two[pl.ds(l, 1), :], stat_s[l, m, :, 1:2]
         )
         add_rows(2 + l, weighted)
         dh = state[...] + dh
@@ -444,7 +461,7 @@
         out_copy(3, l, m).start()
         turned_wait(1)
         turned_wait(0)
-        do = nn(da_s[slot], weights[held, block_rows(3)]).astype(BF16)
+        do = nn(da_s[slot], weights[turned(1)]).astype(BF16)
         slopes, products = [], []
         q_tiles, k_tiles, v_tiles = [None] * 6, [None] * 6, [None] * 6
         for tile, count, inside in WINDOWS:
@@ -473,7 +490,7 @@
             qkv_s[l, m, :, D + at : D + at + 128] = (k_tiles[i] * SCALE).astype(BF16)
             qkv_s[l, m, :, 2 * D + at : 2 * D + at + 128] = v_tiles[i].astype(BF16)
         out_copy(1, l, m).start()
-        du = nn(qkv_s[l, m], weights[held, block_rows(0, 3)])
+        du = nn(qkv_s[l, m], weights[turned(0, 0, 3)])
         dx, weighted = norm_back(
             du, u_s[l, m].astype(F32), gain_one[pl.ds(l, 1), :], stat_s[l, m, :, 0:1]
         )
@@ -516,12 +533,6 @@
 
         def one(l, c):
             forward_layer(l, m)
-
-            @pl.when((m == micros - 1) & (me == last))
-            def _():
-                for k in (3, 2, 1, 0):
-                    swap_copy(1 - l, k).start()
-
             return c
 
         lax.fori_loop(0, 2, one, 0)
@@ -1030,6 +1041,10 @@
     lax.fori_loop(0, 2, plain_products, 0)
     add_core(CHUNKS + ORDER[UP - 1], 0, ORDER[UP - 1])
 
+    def plain_sums(step):
+        for i in ORDER[:UP]:
+            lent_or(step, i, lambda g: None, functools.partial(second_sum, step * CHUNKS + i, i))
+
     def mlp_products(step, carry):
         l = 1 - step
         base = step * CHUNKS
@@ -1055,8 +1070,7 @@
 
         lax.fori_loop(0, rows // AGAIN, again, 0)
         next_loads(4, 5, 8, 9)
-        for i in ORDER[:UP]:
-            lent_or(step, i, lambda g: None, functools.partial(second_sum, base + i, i, l))
+        pl.when(step == 0)(functools.partial(plain_sums, 0))
         for k in (2, 3, 6, 7, 10, 11):
             copies[k].wait()
         for b in range(2):
@@ -1082,6 +1096,7 @@
             give_copy(base + i, i).start()
         for i in range(UP + 1, CHUNKS):
             add_core(base + i, l, i)
+        pl.when(step == 0)(functools.partial(plain_sums, 1))
         return carry
 
     lax.fori_loop(0, 2, mlp_products, 0)

time: 234 us -> 231 us (0.987)
  Pallas kernels: 233 us -> 230 us
where the time goes in v9:
time: 231 us
  Pallas kernels  230 us (100%)
    pallas_call x1, Pallas kernels, relay(): pl.pallas_call(functools.partial(relay_kernel, sections, replicas, micros...  151 us
    pallas_call x1, Pallas kernels, summed(): pl.pallas_call(functools.partial(sum_kernel, sections), out_shape=(jax.Sh...  72.8 us
    pallas_call x1, Pallas kernels, written(): pl.pallas_call(functools.partial(write_kernel, count, share), out_shape=(...  5.79 us

profile of v9, /device:TPU:0, one launch (start us, length us, event | category | flops | bytes accessed | tf_op | source)
XLA Modules:
  0.0 230.5 jit_solution(5891052391924268530)
XLA Ops:
  0.6 151.1 %relay.1 = (bf16[512,256]{1,0:T(8,128)(2,1)}, bf16[512,768]{1,0:T(8,128)(2,1)}, f32[8,8,128]{2,1,0:T(8,128)}, bf16[2,512,768]{2,1,0:T(8,128)(2,1)}, bf16[2,512,2...) custom-call(bf16[512,768]{1,0:T(8,128)(2,1)} %tokens.1, ...), custom_call_target="tpu_custom_call" | custom-call | tf_op jit(solution)/shard_map/relay/pallas_call | solution.py:661
  151.7 72.8 %sum.1 = (f32[8,128]{1,0:T(8,128)}, bf16[192,512]{1,0:T(8,128)(2,1)}, bf16[192,512]{1,0:T(8,128)(2,1)}, bf16[2,96,2304]{2,1,0:T(8,128)(2,1)}, bf16[2,96,768]{2,1...) custom-call(f32[8,8,128]{2,1,0:T(8,128)} %get-tuple-element.36.gains_in, ...), custom_call_target="tpu_custom_call" | custom-call | tf_op jit(solution)/shard_map/sum/pallas_call | solution.py:1255
  224.6 5.8 %write.1 = (f32[2,96]{1,0:T(2,128)}, f32[2,96]{1,0:T(2,128)}, bf16[192,512]{1,0:T(8,128)(2,1)}, f32[192,512]{1,0:T(8,128)}, f32[2,96,2304]{2,1,0:T(8,128)}, /*in...) custom-call(f32[8,128]{1,0:T(8,128)} %get-tuple-element.49.gains, ...), custom_call_target="tpu_custom_call" | custom-call | tf_op jit(solution)/shard_map/write/pallas_call | solution.py:1334

commit v10 on v9

--- a/solution.py
+++ b/solution.py
@@ -291,19 +291,34 @@
 
     outs = (u_out, dqkv_out, o_out, da_out, u2_out, dz_out, act_out, dm_out)
 
-    def out_copy(kind, l, m):
-        slot = l
+    def out_copies(kind, l, m):
         src = (
             u_s.at[l, m],
             qkv_s.at[l, m],
-            o_s.at[slot],
-            da_s.at[slot],
+            o_s.at[l],
+            da_s.at[l],
             u2_s.at[l, m],
             gp_s.at[l, m],
-            act_s.at[slot],
+            act_s.at[l],
             dm_s.at[l, m],
         )[kind]
-        return pltpu.make_async_copy(src, outs[kind].at[l, pl.ds(m * SEQ, SEQ)], out_sem.at[kind, l, m])
+        out = outs[kind].at[l, pl.ds(m * SEQ, SEQ)]
+        if kind not in (5, 6) or not paired:
+            return [pltpu.make_async_copy(src, out, out_sem.at[kind, l, m])]
+        copies = []
+        for b in range(2):
+            units = block_rows(l * (2 * b + x) + (1 - l) * (2 * y + b))
+            sem = out_sem.at[kind + 3 * b, l, m]
+            copies.append(pltpu.make_async_copy(src.at[:, units], out.at[:, pl.ds(b * D, D)], sem))
+        return copies
+
+    def out_start(kind, l, m):
+        for copy in out_copies(kind, l, m):
+            copy.start()
+
+    def out_wait(kind, l, m):
+        for copy in out_copies(kind, l, m):
+            copy.wait()
 
     def partner(l):
         return {"dp": lax.select(l == 1, replica + 2 - 4 * x, replica + 4 - 8 * y)}
@@ -331,7 +346,7 @@
     def free_slot(kind, l, m):
         @pl.when(m > 0)
         def _():
-            out_copy(kind, l, m - 1).wait()
+            out_wait(kind, l, m - 1)
 
     row = lax.broadcasted_iota(jnp.int32, (SEQ, SEQ), 0) // (SEQ // 4)
     column = lax.broadcasted_iota(jnp.int32, (SEQ, SEQ), 1) // (SEQ // 4)
@@ -354,7 +369,7 @@
         stat_s[l, m, :, 0:1] = inverse
         u = (xhat * gain_one[pl.ds(l, 1), :]).astype(BF16)
         u_s[l, m] = u
-        out_copy(0, l, m).start()
+        out_start(0, l, m)
         weight_wait(0)
         for j in range(3):
             qkv_s[l, m, :, j * D : (j + 1) * D] = nn(u_s[l, m], weights[l, block_rows(j)]).astype(BF16)
@@ -379,7 +394,7 @@
             add_window(tiles, tile, tn(p, values))
         for i in range(6):
             o_s[slot, :, i * 128 : (i + 1) * 128] = tiles[i].astype(BF16)
-        out_copy(2, l, m).start()
+        out_start(2, l, m)
         weight_wait(1)
 
         @pl.when((m == 0) & (me == 0) & (l == 0))
@@ -392,7 +407,7 @@
         hhat, inverse = norm_parts(h)
         stat_s[l, m, :, 1:2] = inverse
         u2_s[l, m] = (hhat * gain_two[pl.ds(l, 1), :]).astype(BF16)
-        out_copy(4, l, m).start()
+        out_start(4, l, m)
 
         @pl.when((m == 0) & (l == 0))
         def _():
@@ -410,7 +425,7 @@
         swap_in(l, m, 2)
         state[...] = state[...] + nn(act_s[slot], weights[l, block_rows(8, 4)])
         swap_in(l, m, 1, 0)
-        out_copy(6, l, m).start()
+        out_start(6, l, m)
 
     def norm_back(du, hat_scaled, gain, inverse):
         t = du * gain
@@ -442,14 +457,14 @@
         turned_wait(3)
         turned_wait(2)
         dm_s[l, m] = dy.astype(BF16)
-        out_copy(7, l, m).start()
+        out_start(7, l, m)
         if paired:
             dm_copy(l, m).start()
         for j in range(4):
             da = nn(dm_s[l, m], weights[turned(3, j)])
             dz = gp_s[l, m, :, j * D : (j + 1) * D].astype(F32) * da
             gp_s[l, m, :, j * D : (j + 1) * D] = dz.astype(BF16)
-        out_copy(5, l, m).start()
+        out_start(5, l, m)
         dh, weighted = norm_back(
             nn(gp_s[l, m], weights[turned(2, 0, 4)]), u2_s[l, m].astype(F32), gain_two[pl.ds(l, 1), :], stat_s[l, m, :, 1:2]
         )
@@ -458,7 +473,7 @@
         state[...] = dh
         free_slot(3, l, m)
         da_s[slot] = dh.astype(BF16)
-        out_copy(3, l, m).start()
+        out_start(3, l, m)
         turned_wait(1)
         turned_wait(0)
         do = nn(da_s[slot], weights[turned(1)]).astype(BF16)
@@ -489,7 +504,7 @@
             qkv_s[l, m, :, at : at + 128] = (q_tiles[i] * SCALE).astype(BF16)
             qkv_s[l, m, :, D + at : D + at + 128] = (k_tiles[i] * SCALE).astype(BF16)
             qkv_s[l, m, :, 2 * D + at : 2 * D + at + 128] = v_tiles[i].astype(BF16)
-        out_copy(1, l, m).start()
+        out_start(1, l, m)
         du = nn(qkv_s[l, m], weights[turned(0, 0, 3)])
         dx, weighted = norm_back(
             du, u_s[l, m].astype(F32), gain_one[pl.ds(l, 1), :], stat_s[l, m, :, 0:1]
@@ -602,10 +617,10 @@
 
     for l in range(2):
         for kind in (2, 3, 6):
-            out_copy(kind, l, micros - 1).wait()
+            out_wait(kind, l, micros - 1)
         for m in range(micros):
             for kind in (0, 1, 4, 5, 7):
-                out_copy(kind, l, m).wait()
+                out_wait(kind, l, m)
             if paired:
                 u2_copy(l, m).wait()
                 dm_copy(l, m).wait()
@@ -641,6 +656,7 @@
     micros = rows // SEQ
     width = D // sections
     paired = replicas == SHARDS
+    hidden = FF // 2 if paired else FF
     anywhere = pl.BlockSpec(memory_space=pl.ANY)
     vmem = pl.BlockSpec(memory_space=pltpu.VMEM)
     smem = pl.BlockSpec(memory_space=pltpu.SMEM)
@@ -669,8 +685,8 @@
             factor(D),
             factor(D),
             factor(D),
-            factor(FF),
-            factor(FF),
+            factor(hidden),
+            factor(hidden),
             factor(D),
             factor(D),
             factor(D),
@@ -708,7 +724,7 @@
             dma((micros, sections)),
             dma((micros,)),
             dma((micros,)),
-            dma((8, 2, micros)),
+            dma((10, 2, micros)),
             dma((2, micros)),
             dma((2, micros)),
             dma((2, micros)),
@@ -724,7 +740,7 @@
 ROWS = 96
 CHUNKS = 10
 UP, DOWN = 4, 6
-AGAIN = 256
+AGAIN = 512
 ORDER = (3, 0, 1, 2) + tuple(range(4, CHUNKS))
 
 LOANS = ((0, 1, 1, 0), (0, 1, 2, 1))
@@ -837,8 +853,8 @@
             units = hidden(l, b)
             copies.append((wup_hbm.at[l, :, units], wup_v.at[b]))
             copies.append((wdown_hbm.at[l, units], wdown_v.at[b]))
-            copies.append((dz_in.at[l, :, units], dz_v.at[b, own_rows]))
-            copies.append((act_in.at[l, :, units], act_v.at[b, own_rows]))
+            copies.append((dz_in.at[l, :, pl.ds(b * CHUNK, CHUNK)], dz_v.at[b, own_rows]))
+            copies.append((act_in.at[l, :, pl.ds(b * CHUNK, CHUNK)], act_v.at[b, own_rows]))
         return [pltpu.make_async_copy(src, dst, load_sem.at[4 + k]) for k, (src, dst) in enumerate(copies)]
 
     for k in (2, 3, 0, 1):
@@ -909,7 +925,7 @@
             mine = lax.select(l == 1, y, x)
             to = lax.select(l == 1, other_y, other_x)
             return remote(first.at[n, 1 - mine], second.at[n], 1, n, to)
-        if i % 2 == 0:
+        if i % 2 == 1:
             return remote(first.at[n, :, 1 - x], second.at[n], 1, n, other_x)
         return remote(first.at[n, 1 - y], second.at[n], 1, n, other_y)
 
@@ -918,7 +934,7 @@
             mine = lax.select(l == 1, x, y)
             to = lax.select(l == 1, other_x, other_y)
             return remote(second.at[n, 1 - mine], third.at[n], 2, n, to)
-        if i % 2 == 0:
+        if i % 2 == 1:
             return remote(second.at[n, 1 - y], third.at[n], 2, n, other_y)
         return remote(second.at[n, 1 - x], third.at[n], 2, n, other_x)
 
@@ -996,7 +1012,7 @@
         if i >= UP:
             kept = first[n, lax.select(l == 1, y, x)]
         else:
-            kept = first[n, :, x] if i % 2 == 0 else first[n, y]
+            kept = first[n, :, x] if i % 2 == 1 else first[n, y]
         second[n] = second[n] + kept
         second_copy(n, i, l).start()
         if i >= UP:
@@ -1161,7 +1177,7 @@
 
     def last_sum(n, i):
         second_copy(n, i).wait_recv()
-        third[n] = third[n] + second[n, y if i % 2 == 0 else x]
+        third[n] = third[n] + second[n, y if i % 2 == 1 else x]
 
     def last_sums(step, carry):
         for i in ORDER:
@@ -1315,14 +1331,20 @@
         refs[3 * count + 2 : 4 * count + 2],
     )
     load_sem, store_sem = refs[4 * count + 2 :]
-    loads = [pltpu.make_async_copy(sources[k], held[k], load_sem.at[k]) for k in range(count)]
-    stores = [pltpu.make_async_copy(wide[k], results[k], store_sem.at[k]) for k in range(count)]
+    pieces = []
+    for k in reversed(range(count)):
+        if len(sources[k].shape) == 3:
+            pieces += [tuple(r.at[l] for r in (sources[k], held[k], wide[k], results[k])) for l in range(2)]
+        else:
+            pieces.append((sources[k], held[k], wide[k], results[k]))
+    loads = [pltpu.make_async_copy(p[0], p[1], load_sem.at[i]) for i, p in enumerate(pieces)]
+    stores = [pltpu.make_async_copy(p[2], p[3], store_sem.at[i]) for i, p in enumerate(pieces)]
     for load in loads:
         load.start()
-    for k in range(count):
-        loads[k].wait()
-        wide[k][...] = held[k][...].astype(wide[k].dtype)
-        stores[k].start()
+    for load, store, piece in zip(loads, stores, pieces):
+        load.wait()
+        piece[2][...] = piece[1][...].astype(piece[2].dtype)
+        store.start()
     for store in stores:
         store.wait()
 
@@ -1339,7 +1361,7 @@
         out_specs=(vmem, vmem) + (anywhere,) * count,
         scratch_shapes=[pltpu.VMEM(a.shape, a.dtype) for a in arrays]
         + [pltpu.VMEM(a.shape, t) for a, t in zip(arrays, types)]
-        + [pltpu.SemaphoreType.DMA((count,)), pltpu.SemaphoreType.DMA((count,))],
+        + [pltpu.SemaphoreType.DMA((2 * count,)), pltpu.SemaphoreType.DMA((2 * count,))],
         compiler_params=pltpu.CompilerParams(vmem_limit_bytes=60 * MIB),
         name="write",
     )(gains, *arrays)

time: 231 us -> 230 us (level)
  no operation moved by 1% of the time
where the time goes in v10:
time: 230 us
  Pallas kernels  229 us (100%)
    pallas_call x1, Pallas kernels, relay(): pl.pallas_call(functools.partial(relay_kernel, sections, replicas, micros...  151 us
    pallas_call x1, Pallas kernels, summed(): pl.pallas_call(functools.partial(sum_kernel, sections), out_shape=(jax.Sh...  72.1 us
    pallas_call x1, Pallas kernels, written(): pl.pallas_call(functools.partial(write_kernel, count, share), out_shape=(...  5.65 us

profile of v10, /device:TPU:0, one launch (start us, length us, event | category | flops | bytes accessed | tf_op | source)
XLA Modules:
  0.0 229.6 jit_solution(6711869628760591628)
XLA Ops:
  0.6 151.0 %relay.1 = (bf16[512,256]{1,0:T(8,128)(2,1)}, bf16[512,768]{1,0:T(8,128)(2,1)}, f32[8,8,128]{2,1,0:T(8,128)}, bf16[2,512,768]{2,1,0:T(8,128)(2,1)}, bf16[2,512,2...) custom-call(bf16[512,768]{1,0:T(8,128)(2,1)} %tokens.1, ...), custom_call_target="tpu_custom_call" | custom-call | tf_op jit(solution)/shard_map/relay/pallas_call | solution.py:677
  151.7 72.1 %sum.1 = (f32[8,128]{1,0:T(8,128)}, bf16[192,512]{1,0:T(8,128)(2,1)}, bf16[192,512]{1,0:T(8,128)(2,1)}, bf16[2,96,2304]{2,1,0:T(8,128)(2,1)}, bf16[2,96,768]{2,1...) custom-call(f32[8,8,128]{2,1,0:T(8,128)} %get-tuple-element.36.gains_in, ...), custom_call_target="tpu_custom_call" | custom-call | tf_op jit(solution)/shard_map/sum/pallas_call | solution.py:1271
  223.8 5.7 %write.1 = (f32[2,96]{1,0:T(2,128)}, f32[2,96]{1,0:T(2,128)}, bf16[192,512]{1,0:T(8,128)(2,1)}, f32[192,512]{1,0:T(8,128)}, f32[2,96,2304]{2,1,0:T(8,128)}, /*in...) custom-call(f32[8,128]{1,0:T(8,128)} %get-tuple-element.49.gains, ...), custom_call_target="tpu_custom_call" | custom-call | tf_op jit(solution)/shard_map/write/pallas_call | solution.py:1356

commit v11 on v10

--- a/solution.py
+++ b/solution.py
@@ -276,14 +276,14 @@
         return pltpu.make_async_remote_copy(
             src_ref=fin_source(m, j),
             dst_ref=fin_out.at[slots_of(m)],
-            send_sem=fin_send.at[m, j],
-            recv_sem=fin_recv.at[m],
+            send_sem=fin_send.at[j],
+            recv_sem=fin_recv,
             device_id={"pipe": j},
             device_id_type=MESH,
         )
 
     def own_fin_copy(m):
-        return pltpu.make_async_copy(fin_source(m, last), fin_out.at[slots_of(m)], fin_send.at[m, last])
+        return pltpu.make_async_copy(fin_source(m, last), fin_out.at[slots_of(m)], fin_send.at[last])
 
     def inp_copy(m):
         return pltpu.make_async_copy(bwd_out.at[m], inp_out.at[slots_of(m)], inp_send.at[m])
@@ -304,11 +304,11 @@
         )[kind]
         out = outs[kind].at[l, pl.ds(m * SEQ, SEQ)]
         if kind not in (5, 6) or not paired:
-            return [pltpu.make_async_copy(src, out, out_sem.at[kind, l, m])]
+            return [pltpu.make_async_copy(src, out, out_sem.at[kind, l])]
         copies = []
         for b in range(2):
             units = block_rows(l * (2 * b + x) + (1 - l) * (2 * y + b))
-            sem = out_sem.at[kind + 3 * b, l, m]
+            sem = out_sem.at[kind + 3 * b, l]
             copies.append(pltpu.make_async_copy(src.at[:, units], out.at[:, pl.ds(b * D, D)], sem))
         return copies
 
@@ -319,6 +319,16 @@
     def out_wait(kind, l, m):
         for copy in out_copies(kind, l, m):
             copy.wait()
+
+    def whole_wait(ref, sem):
+        pltpu.make_async_copy(ref, ref, sem).wait()
+
+    def out_wait_all(kind, l):
+        if kind == 5 and paired:
+            for b in range(2):
+                whole_wait(outs[kind].at[l, :, pl.ds(b * D, D)], out_sem.at[kind + 3 * b, l])
+        else:
+            whole_wait(outs[kind].at[l], out_sem.at[kind, l])
 
     def partner(l):
         return {"dp": lax.select(l == 1, replica + 2 - 4 * x, replica + 4 - 8 * y)}
@@ -327,8 +337,8 @@
         return pltpu.make_async_remote_copy(
             src_ref=u2_s.at[l, m],
             dst_ref=u2_other.at[l, slots_of(m)],
-            send_sem=u2_send.at[l, m],
-            recv_sem=u2_recv.at[l, m],
+            send_sem=u2_send.at[l],
+            recv_sem=u2_recv.at[l],
             device_id=partner(l),
             device_id_type=MESH,
         )
@@ -337,8 +347,8 @@
         return pltpu.make_async_remote_copy(
             src_ref=dm_s.at[l, m],
             dst_ref=dm_other.at[l, slots_of(m)],
-            send_sem=dm_send.at[l, m],
-            recv_sem=dm_recv.at[l, m],
+            send_sem=dm_send.at[l],
+            recv_sem=dm_recv.at[l],
             device_id=partner(l),
             device_id_type=MESH,
         )
@@ -618,12 +628,21 @@
     for l in range(2):
         for kind in (2, 3, 6):
             out_wait(kind, l, micros - 1)
-        for m in range(micros):
-            for kind in (0, 1, 4, 5, 7):
-                out_wait(kind, l, m)
-            if paired:
-                u2_copy(l, m).wait()
-                dm_copy(l, m).wait()
+        for kind in (0, 1, 4, 5, 7):
+            out_wait_all(kind, l)
+        if paired:
+            for sem in (u2_send, u2_recv, dm_send, dm_recv):
+                whole_wait(dm_other.at[l], sem.at[l])
+
+    @pl.when(me == last)
+    def _():
+        for j in range(sections):
+            whole_wait(fin_out, fin_send.at[j])
+
+    @pl.when(me < last)
+    def _():
+        whole_wait(fin_out, fin_recv)
+
     for m in range(micros):
 
         @pl.when(me < last)
@@ -633,16 +652,6 @@
         @pl.when(me > 0)
         def _():
             backward_copy(m).wait_send()
-
-        @pl.when(me == last)
-        def _():
-            for j in range(last):
-                fin_copy(m, j).wait_send()
-            own_fin_copy(m).wait()
-
-        @pl.when(me < last)
-        def _():
-            fin_copy(m, last).wait_recv()
 
         @pl.when(me == 0)
         def _():
@@ -721,14 +730,14 @@
             dma((micros,)),
             dma((micros,)),
             dma((micros,)),
-            dma((micros, sections)),
+            dma((sections,)),
+            dma(()),
             dma((micros,)),
-            dma((micros,)),
-            dma((10, 2, micros)),
-            dma((2, micros)),
-            dma((2, micros)),
-            dma((2, micros)),
-            dma((2, micros)),
+            dma((10, 2)),
+            dma((2,)),
+            dma((2,)),
+            dma((2,)),
+            dma((2,)),
         ],
         compiler_params=pltpu.CompilerParams(
             collective_id=0, has_side_effects=True, vmem_limit_bytes=60 * MIB
@@ -800,6 +809,7 @@
     lend_recv,
     back_send,
     back_recv,
+    give_send,
     send,
     recv,
     up_sem,
@@ -866,8 +876,8 @@
         return pltpu.make_async_remote_copy(
             src_ref=gains_in.at[j],
             dst_ref=gains_v.at[source],
-            send_sem=gain_send.at[j],
-            recv_sem=gain_recv.at[source],
+            send_sem=gain_send,
+            recv_sem=gain_recv,
             device_id={"dp": j},
             device_id_type=MESH,
         )
@@ -901,11 +911,14 @@
                 gain_copy(j, me).start()
 
 
-    def remote(src, dst, step, n, to):
+    def whole_wait(ref, sem):
+        pltpu.make_async_copy(ref, ref, sem).wait()
+
+    def remote(src, dst, step, n, to, sent=None):
         return pltpu.make_async_remote_copy(
             src_ref=src,
             dst_ref=dst,
-            send_sem=send.at[step, n],
+            send_sem=send.at[step - 1, n] if sent is None else sent,
             recv_sem=recv.at[step, n],
             device_id={"dp": to},
             device_id_type=MESH,
@@ -913,8 +926,8 @@
 
     def give_copy(n, i):
         if i >= DOWN:
-            return remote(own.at[i, 1 - core, 0], first.at[n, 0], 0, n, other_core)
-        return remote(own.at[i, 1 - core], first.at[n], 0, n, other_core)
+            return remote(own.at[i, 1 - core, 0], first.at[n, 0], 0, n, other_core, give_send.at[i])
+        return remote(own.at[i, 1 - core], first.at[n], 0, n, other_core, give_send.at[i])
 
     def down_copy(n, l):
         mine, to = lax.select(l == 1, y, x), lax.select(l == 1, other_y, other_x)
@@ -987,11 +1000,11 @@
             dst = up_out.at[l, :, hidden(l, i - UP, other=True)]
         else:
             dst = down_out.at[l, pl.ds((i - DOWN) * ROWS, ROWS)]
-        return pltpu.make_async_copy(third.at[n], dst, out_sem.at[n])
+        return pltpu.make_async_copy(third.at[n], dst, out_sem.at[1 - l])
 
     def own_up_copy(n, l, i):
         mine = lax.select(l == 1, x, y)
-        return pltpu.make_async_copy(second.at[n, mine], up_out.at[l, :, hidden(l, i - UP)], up_sem.at[n])
+        return pltpu.make_async_copy(second.at[n, mine], up_out.at[l, :, hidden(l, i - UP)], up_sem.at[1 - l])
 
     def add_core(n, l, i):
         give_copy(n, i).wait_recv()
@@ -1164,12 +1177,7 @@
         first_copy(n, i).start()
 
     gains_v[me] = gains_in[me]
-    for j in range(SHARDS):
-
-        @pl.when(me != j)
-        def _():
-            gain_copy(j, j).wait_recv()
-
+    whole_wait(gains_v.at[0 : SHARDS - 1], gain_recv)
     total = gains_v[0]
     for j in range(1, SHARDS):
         total = total + gains_v[j]
@@ -1220,11 +1228,10 @@
                 def sent():
                     first_copy(n, i, 1 - step).wait_send()
                     second_copy(n, i, 1 - step).wait_send()
-                    if i >= UP:
-                        own_up_copy(n, 1 - step, i).wait()
 
                 lent_or(step, i, lambda g: lend_copy(g).wait_send(), sent)
-            result_copy(n, 1 - step, i).wait()
+        whole_wait(third.at[0:CHUNKS], out_sem.at[step])
+        whole_wait(third.at[0 : DOWN - UP], up_sem.at[step])
         return carry
 
     lax.fori_loop(0, 2, finish, 0)
@@ -1237,12 +1244,7 @@
 
     for i in range(CHUNKS):
         give_copy(CHUNKS + i, i).wait_send()
-    for j in range(SHARDS):
-
-        @pl.when(me != j)
-        def _():
-            gain_copy(j, me).wait_send()
-
+    whole_wait(gains_v.at[0 : SHARDS - 1], gain_send)
     fin_store.wait()
 
     @pl.when(section == 0)
@@ -1299,8 +1301,8 @@
             pltpu.VMEM((rows, D), BF16),
             pltpu.VMEM((sections, width, rows), BF16),
             dma((16,)),
-            dma((SHARDS,)),
-            dma((SHARDS,)),
+            dma(()),
+            dma(()),
             dma(()),
             dma((sections,)),
             dma(()),
@@ -1308,10 +1310,11 @@
             dma((len(LOANS),)),
             dma((len(LOANS),)),
             dma((len(LOANS),)),
+            dma((CHUNKS,)),
+            dma((2, slots)),
             dma((3, slots)),
-            dma((3, slots)),
-            dma((total,)),
-            dma((total,)),
+            dma((2,)),
+            dma((2,)),
         ],
         compiler_params=pltpu.CompilerParams(
             collective_id=1, has_side_effects=True, vmem_limit_bytes=60 * MIB

time: 230 us -> 228 us (level)
  no operation moved by 1% of the time
where the time goes in v11:
time: 228 us
  Pallas kernels  227 us (100%)
    pallas_call x1, Pallas kernels, relay(): pl.pallas_call(functools.partial(relay_kernel, sections, replicas, micros...  150 us
    pallas_call x1, Pallas kernels, summed(): pl.pallas_call(functools.partial(sum_kernel, sections), out_shape=(jax.Sh...  71.4 us
    pallas_call x1, Pallas kernels, written(): pl.pallas_call(functools.partial(write_kernel, count, share), out_shape=(...  5.65 us

profile of v11, /device:TPU:0, one launch (start us, length us, event | category | flops | bytes accessed | tf_op | source)
XLA Modules:
  0.0 228.0 jit_solution(7156431551969297507)
XLA Ops:
  0.6 150.2 %relay.1 = (bf16[512,256]{1,0:T(8,128)(2,1)}, bf16[512,768]{1,0:T(8,128)(2,1)}, f32[8,8,128]{2,1,0:T(8,128)}, bf16[2,512,768]{2,1,0:T(8,128)(2,1)}, bf16[2,512,2...) custom-call(bf16[512,768]{1,0:T(8,128)(2,1)} %tokens.1, ...), custom_call_target="tpu_custom_call" | custom-call | tf_op jit(solution)/shard_map/relay/pallas_call | solution.py:686
  150.8 71.4 %sum.1 = (f32[8,128]{1,0:T(8,128)}, bf16[192,512]{1,0:T(8,128)(2,1)}, bf16[192,512]{1,0:T(8,128)(2,1)}, bf16[2,96,2304]{2,1,0:T(8,128)(2,1)}, bf16[2,96,768]{2,1...) custom-call(f32[8,8,128]{2,1,0:T(8,128)} %get-tuple-element.36.gains_in, ...), custom_call_target="tpu_custom_call" | custom-call | tf_op jit(solution)/shard_map/sum/pallas_call | solution.py:1273
  222.2 5.7 %write.1 = (f32[2,96]{1,0:T(2,128)}, f32[2,96]{1,0:T(2,128)}, bf16[192,512]{1,0:T(8,128)(2,1)}, f32[192,512]{1,0:T(8,128)}, f32[2,96,2304]{2,1,0:T(8,128)}, /*in...) custom-call(f32[8,128]{1,0:T(8,128)} %get-tuple-element.49.gains, ...), custom_call_target="tpu_custom_call" | custom-call | tf_op jit(solution)/shard_map/write/pallas_call | solution.py:1359

commit v12 on v11

--- a/solution.py
+++ b/solution.py
@@ -152,18 +152,8 @@
     last = sections - 1
     width = D // sections
 
-    barrier = pltpu.get_barrier_semaphore()
-    for j in range(sections):
-
-        @pl.when(me != j)
-        def _():
-            pl.semaphore_signal(barrier, inc=1, device_id={"pipe": j}, device_id_type=MESH)
-
     replica = lax.axis_index("dp")
     x, y = lax.rem(replica // 2, 2), replica // 4
-    if paired:
-        for j in (replica + 2 - 4 * x, replica + 4 - 8 * y):
-            pl.semaphore_signal(barrier, inc=1, device_id={"dp": j}, device_id_type=MESH)
 
     def block_rows(b, count=1):
         start = b * D
@@ -177,12 +167,18 @@
             src = wdown_hbm.at[l, block_rows(j)]
         else:
             src = (wqkv_hbm, None, wup_hbm)[k].at[l, :, block_rows(j)]
-        return pltpu.make_async_copy(src, weights.at[l, block_rows(first + j)], w_sem.at[l, first + j])
-
-    def turned_copy(l, b):
+        return pltpu.make_async_copy(src, weights.at[l, block_rows(first + j)], w_sem.at[l, k])
+
+    def turned_copy(l, k, b):
         return pltpu.make_async_copy(
-            weights.at[l, block_rows(b)], turned_hbm.at[l, block_rows(b)], turn_sem.at[l, b]
+            weights.at[l, block_rows(b)], turned_hbm.at[l, block_rows(b)], turn_sem.at[l, k]
         )
+
+    def whole_wait(ref, sem):
+        pltpu.make_async_copy(ref, ref, sem).wait()
+
+    def kind_wait(l, k, sem):
+        whole_wait(weights.at[l, block_rows(*KINDS[k])], sem.at[l, k])
 
     def swap_copy(l, k):
         first, count = KINDS[k]
@@ -209,15 +205,6 @@
                 weights[tile(c, r)] = lower
                 weights[tile(r, c)] = upper
 
-    def each_block(l, action):
-        for k, (_, count) in enumerate(KINDS):
-
-            def one(j, c):
-                action(l, k, j)
-                return c
-
-            lax.fori_loop(0, count, one, 0)
-
     def token_copy(m):
         return pltpu.make_async_copy(tokens.at[pl.ds(m * SEQ, SEQ)], fwd_in.at[m], in_sem.at[0, m])
 
@@ -240,6 +227,17 @@
     def _():
         weights_start(1)
 
+
+    barrier = pltpu.get_barrier_semaphore()
+    for j in range(sections):
+
+        @pl.when(me != j)
+        def _():
+            pl.semaphore_signal(barrier, inc=1, device_id={"pipe": j}, device_id_type=MESH)
+
+    if paired:
+        for j in (replica + 2 - 4 * x, replica + 4 - 8 * y):
+            pl.semaphore_signal(barrier, inc=1, device_id={"dp": j}, device_id_type=MESH)
 
     @pl.when(me == last)
     def _():
@@ -320,9 +318,6 @@
         for copy in out_copies(kind, l, m):
             copy.wait()
 
-    def whole_wait(ref, sem):
-        pltpu.make_async_copy(ref, ref, sem).wait()
-
     def out_wait_all(kind, l):
         if kind == 5 and paired:
             for b in range(2):
@@ -371,8 +366,7 @@
         def weight_wait(k):
             @pl.when((m == 0) & (me < last))
             def _():
-                for j in range(KINDS[k][1]):
-                    weight_copy(l, k, j).wait()
+                kind_wait(l, k, w_sem)
 
         x = state[...]
         xhat, inverse = norm_parts(x)
@@ -524,26 +518,32 @@
 
     @pl.when(me == last)
     def _():
-        def make(l, k, j):
-            b = KINDS[k][0] + j
-            weight_copy(l, k, j).wait()
-            turn(l, b)
-            turned_copy(l, b).start()
-
-        def again(l, k, j):
-            turned_copy(l, KINDS[k][0] + j).wait()
-            weight_copy(l, k, j).start()
-
-        def ready(l, k, j):
-            weight_copy(l, k, j).wait()
+        def make(l, c):
+            for k, (first, count) in enumerate(KINDS):
+                kind_wait(l, k, w_sem)
+
+                def one(j, c):
+                    turn(l, first + j)
+                    turned_copy(l, k, first + j).start()
+                    return c
+
+                lax.fori_loop(0, count, one, 0)
+            return c
+
+        def again(l, c):
+            for k, (_, count) in enumerate(KINDS):
+                kind_wait(l, k, turn_sem)
+                for j in range(count):
+                    weight_copy(l, k, j).start()
+            return c
+
+        def ready(l, c):
+            for k in range(len(KINDS)):
+                kind_wait(l, k, w_sem)
+            return c
 
         for action in (make, again, ready):
-
-            def one(l, c):
-                each_block(l, action)
-                return c
-
-            lax.fori_loop(0, 2, one, 0)
+            lax.fori_loop(0, 2, action, 0)
 
     def forward_micro(m, carry):
         @pl.when(me == 0)
@@ -722,8 +722,8 @@
             pltpu.VMEM((SEQ, D), F32),
             pltpu.VMEM((4, 8, D), F32),
             pltpu.VMEM((micros, SEQ, SEQ), F32),
-            dma((2, BLOCKS)),
-            dma((2, BLOCKS)),
+            dma((2, len(KINDS))),
+            dma((2, len(KINDS))),
             dma((2, len(KINDS))),
             dma((2, micros)),
             dma((micros,)),
@@ -824,21 +824,7 @@
     other_x = me + 2 - 4 * x
     other_y = me + 4 - 8 * y
 
-    barrier = pltpu.get_barrier_semaphore()
-    for j in range(SHARDS):
-
-        @pl.when(me != j)
-        def _():
-            pl.semaphore_signal(barrier, inc=1, device_id={"dp": j}, device_id_type=MESH)
-
     loans = LOANS if sections > 3 else ()
-    for j in range(1, sections):
-        for to in sorted({0} | {lender for lender, k, _, _ in loans if sections - k == j}):
-
-            @pl.when(section == j)
-            def _():
-                pl.semaphore_signal(barrier, inc=1, device_id={"pipe": to}, device_id_type=MESH)
-
     sources = (u_in, dqkv_in, o_in, da_in)
     held = (u_v, dqkv_v, o_v, da_v)
     rows = dm_in.shape[1]
@@ -869,6 +855,21 @@
 
     for k in (2, 3, 0, 1):
         load(k, 1).start()
+
+    barrier = pltpu.get_barrier_semaphore()
+    for j in range(SHARDS):
+
+        @pl.when(me != j)
+        def _():
+            pl.semaphore_signal(barrier, inc=1, device_id={"dp": j}, device_id_type=MESH)
+
+    for j in range(1, sections):
+        for to in sorted({0} | {lender for lender, k, _, _ in loans if sections - k == j}):
+
+            @pl.when(section == j)
+            def _():
+                pl.semaphore_signal(barrier, inc=1, device_id={"pipe": to}, device_id_type=MESH)
+
     for copy in mlp_loads(1):
         copy.start()
 
@@ -914,11 +915,14 @@
     def whole_wait(ref, sem):
         pltpu.make_async_copy(ref, ref, sem).wait()
 
+    def sender(n):
+        return 2 + n - 2 * CHUNKS if isinstance(n, int) and n >= 2 * CHUNKS else n // CHUNKS
+
     def remote(src, dst, step, n, to, sent=None):
         return pltpu.make_async_remote_copy(
             src_ref=src,
             dst_ref=dst,
-            send_sem=send.at[step - 1, n] if sent is None else sent,
+            send_sem=send.at[step - 1, sender(n)] if sent is None else sent,
             recv_sem=recv.at[step, n],
             device_id={"dp": to},
             device_id_type=MESH,
@@ -1218,23 +1222,28 @@
         for step in range(2):
             result_copy(step * CHUNKS + i, 1 - step, i).start()
 
-    def finish(step, carry):
-        for i in range(CHUNKS):
-            n = step * CHUNKS + i
-            if i >= DOWN:
-                down_copy(n, 1 - step).wait_send()
-            else:
-
-                def sent():
-                    first_copy(n, i, 1 - step).wait_send()
-                    second_copy(n, i, 1 - step).wait_send()
-
-                lent_or(step, i, lambda g: lend_copy(g).wait_send(), sent)
+    def sent(step, lent):
+        whole_wait(second.at[0 : DOWN - lent], send.at[0, step])
+        whole_wait(third.at[0 : CHUNKS - lent], send.at[1, step])
+
+    for step in range(2):
         whole_wait(third.at[0:CHUNKS], out_sem.at[step])
         whole_wait(third.at[0 : DOWN - UP], up_sem.at[step])
-        return carry
-
-    lax.fori_loop(0, 2, finish, 0)
+    sent(1, 0)
+    lenders = sorted({lender for lender, _, _, _ in loans})
+    keeps = section >= 0
+    for lender in lenders:
+        keeps = keeps & (section != lender)
+
+        @pl.when(section == lender)
+        def _():
+            lent = [g for g, loan in enumerate(loans) if loan[0] == lender]
+            sent(0, len(lent))
+            for g in lent:
+                lend_copy(g).wait_send()
+
+    pl.when(keeps)(functools.partial(sent, 0, 0))
+
     def guest_sent(g, n, i):
         first_copy(n, i).wait_send()
         second_copy(n, i).wait_send()
@@ -1311,7 +1320,7 @@
             dma((len(LOANS),)),
             dma((len(LOANS),)),
             dma((CHUNKS,)),
-            dma((2, slots)),
+            dma((2, 2 + GUESTS)),
             dma((3, slots)),
             dma((2,)),
             dma((2,)),

time: 228 us -> 228 us (level)
  no operation moved by 1% of the time
where the time goes in v12:
time: 228 us; the launch traced here: 227 us
  Pallas kernels  226 us (99%)
    pallas_call x1, Pallas kernels, relay(): pl.pallas_call(functools.partial(relay_kernel, sections, replicas, micros...  150 us
    pallas_call x1, Pallas kernels, summed(): pl.pallas_call(functools.partial(sum_kernel, sections), out_shape=(jax.Sh...  71.1 us
    pallas_call x1, Pallas kernels, written(): pl.pallas_call(functools.partial(write_kernel, count, share), out_shape=(...  5.65 us

profile of v12, /device:TPU:0, one launch (start us, length us, event | category | flops | bytes accessed | tf_op | source)
XLA Modules:
  0.0 227.3 jit_solution(12886182020057889775)
XLA Ops:
  0.6 149.7 %relay.1 = (bf16[512,256]{1,0:T(8,128)(2,1)}, bf16[512,768]{1,0:T(8,128)(2,1)}, f32[8,8,128]{2,1,0:T(8,128)}, bf16[2,512,768]{2,1,0:T(8,128)(2,1)}, bf16[2,512,2...) custom-call(bf16[512,768]{1,0:T(8,128)(2,1)} %tokens.1, ...), custom_call_target="tpu_custom_call" | custom-call | tf_op jit(solution)/shard_map/relay/pallas_call | solution.py:686
  150.4 71.1 %sum.1 = (f32[8,128]{1,0:T(8,128)}, bf16[192,512]{1,0:T(8,128)(2,1)}, bf16[192,512]{1,0:T(8,128)(2,1)}, bf16[2,96,2304]{2,1,0:T(8,128)(2,1)}, bf16[2,96,768]{2,1...) custom-call(f32[8,8,128]{2,1,0:T(8,128)} %get-tuple-element.36.gains_in, ...), custom_call_target="tpu_custom_call" | custom-call | tf_op jit(solution)/shard_map/sum/pallas_call | solution.py:1282
  221.5 5.7 %write.1 = (f32[2,96]{1,0:T(2,128)}, f32[2,96]{1,0:T(2,128)}, bf16[192,512]{1,0:T(8,128)(2,1)}, f32[192,512]{1,0:T(8,128)}, f32[2,96,2304]{2,1,0:T(8,128)}, /*in...) custom-call(f32[8,128]{1,0:T(8,128)} %get-tuple-element.49.gains, ...), custom_call_target="tpu_custom_call" | custom-call | tf_op jit(solution)/shard_map/write/pallas_call | solution.py:1368

commit v13 on v12

--- a/solution.py
+++ b/solution.py
@@ -421,12 +421,12 @@
             u2_copy(l, m).start()
         weight_wait(2)
         free_slot(6, l, m)
-        weight_wait(3)
         for j in range(4):
             act, slope = gelu_parts(nn(u2_s[l, m], weights[l, block_rows(4 + j)]))
             act_s[slot, :, j * D : (j + 1) * D] = act.astype(BF16)
             gp_s[l, m, :, j * D : (j + 1) * D] = slope.astype(BF16)
         swap_in(l, m, 2)
+        weight_wait(3)
         state[...] = state[...] + nn(act_s[slot], weights[l, block_rows(8, 4)])
         swap_in(l, m, 1, 0)
         out_start(6, l, m)
@@ -459,7 +459,6 @@
 
         dy = state[...]
         turned_wait(3)
-        turned_wait(2)
         dm_s[l, m] = dy.astype(BF16)
         out_start(7, l, m)
         if paired:
@@ -469,6 +468,7 @@
             dz = gp_s[l, m, :, j * D : (j + 1) * D].astype(F32) * da
             gp_s[l, m, :, j * D : (j + 1) * D] = dz.astype(BF16)
         out_start(5, l, m)
+        turned_wait(2)
         dh, weighted = norm_back(
             nn(gp_s[l, m], weights[turned(2, 0, 4)]), u2_s[l, m].astype(F32), gain_two[pl.ds(l, 1), :], stat_s[l, m, :, 1:2]
         )
@@ -479,7 +479,6 @@
         da_s[slot] = dh.astype(BF16)
         out_start(3, l, m)
         turned_wait(1)
-        turned_wait(0)
         do = nn(da_s[slot], weights[turned(1)]).astype(BF16)
         slopes, products = [], []
         q_tiles, k_tiles, v_tiles = [None] * 6, [None] * 6, [None] * 6
@@ -509,6 +508,7 @@
             qkv_s[l, m, :, D + at : D + at + 128] = (k_tiles[i] * SCALE).astype(BF16)
             qkv_s[l, m, :, 2 * D + at : 2 * D + at + 128] = v_tiles[i].astype(BF16)
         out_start(1, l, m)
+        turned_wait(0)
         du = nn(qkv_s[l, m], weights[turned(0, 0, 3)])
         dx, weighted = norm_back(
             du, u_s[l, m].astype(F32), gain_one[pl.ds(l, 1), :], stat_s[l, m, :, 0:1]

time: 228 us -> 234 us (1.026)
  Pallas kernels: 226 us -> 233 us
    pallas_call x1, Pallas kernels: 150 us -> 157 us  [relay(): pl.pallas_call(functools.partial(relay_kernel, sections, replicas, micros...]
where the time goes in v13:
time: 234 us
  Pallas kernels  233 us (100%)
    pallas_call x1, Pallas kernels, relay(): pl.pallas_call(functools.partial(relay_kernel, sections, replicas, micros...  157 us
    pallas_call x1, Pallas kernels, summed(): pl.pallas_call(functools.partial(sum_kernel, sections), out_shape=(jax.Sh...  70.8 us
    pallas_call x1, Pallas kernels, written(): pl.pallas_call(functools.partial(write_kernel, count, share), out_shape=(...  5.65 us

profile of v13, /device:TPU:0, one launch (start us, length us, event | category | flops | bytes accessed | tf_op | source)
XLA Modules:
  0.0 234.0 jit_solution(15974974062078150145)
XLA Ops:
  0.6 156.8 %relay.1 = (bf16[512,256]{1,0:T(8,128)(2,1)}, bf16[512,768]{1,0:T(8,128)(2,1)}, f32[8,8,128]{2,1,0:T(8,128)}, bf16[2,512,768]{2,1,0:T(8,128)(2,1)}, bf16[2,512,2...) custom-call(bf16[512,768]{1,0:T(8,128)(2,1)} %tokens.1, ...), custom_call_target="tpu_custom_call" | custom-call | tf_op jit(solution)/shard_map/relay/pallas_call | solution.py:686
  157.4 70.8 %sum.1 = (f32[8,128]{1,0:T(8,128)}, bf16[192,512]{1,0:T(8,128)(2,1)}, bf16[192,512]{1,0:T(8,128)(2,1)}, bf16[2,96,2304]{2,1,0:T(8,128)(2,1)}, bf16[2,96,768]{2,1...) custom-call(f32[8,8,128]{2,1,0:T(8,128)} %get-tuple-element.36.gains_in, ...), custom_call_target="tpu_custom_call" | custom-call | tf_op jit(solution)/shard_map/sum/pallas_call | solution.py:1282
  228.2 5.7 %write.1 = (f32[2,96]{1,0:T(2,128)}, f32[2,96]{1,0:T(2,128)}, bf16[192,512]{1,0:T(8,128)(2,1)}, f32[192,512]{1,0:T(8,128)}, f32[2,96,2304]{2,1,0:T(8,128)}, /*in...) custom-call(f32[8,128]{1,0:T(8,128)} %get-tuple-element.49.gains, ...), custom_call_target="tpu_custom_call" | custom-call | tf_op jit(solution)/shard_map/write/pallas_call | solution.py:1368
